TPU v7x, 128 devices: a whole 4x4x4 slice. The times are simulated.
128 devices in a mesh: grp: 4 (over y), enc: 32 (over x, z, core).
Axes of the slice: x: 4, y: 4, z: 4, core: 2. Of those that a mesh axis runs over, the one named last changes fastest.
Arguments:
- patches: bfloat16 [32768, 1280], P(('grp', 'enc')), may hold values from -16 to 16
- ln_gain: float32 [1280], replicated, may hold values from 0.1 to 1.9
- qkv_weight: bfloat16 [1280, 3840], P('enc')
- out_weight: bfloat16 [1280, 1280], P('enc'), may hold values from -0.15625 to 0.15625
- image_counts: int32 [128, 4], P(('grp', 'enc')), may hold values from 1 to 128, as said below
- window_order: int32 [256, 128], P(('grp', 'enc')), may hold values from 0 to 255, as said below
- owner_map: int32 [32768, 1], P(('grp', 'enc')), may hold values from 0 to 127; in each aligned block of 256 rows (0 to 255, 256 to 511, ...) at most 4 rows name the same one
- owner_grads: bfloat16 [65536, 1280], P(('grp', 'enc')), may hold values from -6 to 6
Outputs:
- owner_rows: bfloat16 [65536, 1280], P(('grp', 'enc'))
- patch_grads: bfloat16 [32768, 1280], P(('grp', 'enc'))
- qkv_grad: float32 [1280, 3840], P('enc')
- out_grad: float32 [1280, 1280], P('enc')
Inputs may be any that keep to these rules, and one draw needn't show every extreme that they name: `image_counts`: each pack's 4 counts sum to 256 and its largest count is exactly 128. `window_order`: each pack's entries, read in order, are a permutation of 0 to 255 that lists all rows of its first image, then all rows of its second, and so on; within an image the order is arbitrary. `owner_map`: in each pack no owner is named by more than 4 of the pack's rows, a bound that some block reaches.
All inputs are finite; a program needn't handle non-finite values.
Results may differ from a plain program's by a relative error of at most 0.024.
Values may be sent and summed in bfloat16 or wider, within the bound.
No kernel may reach another device: no remote copies, remote signals or barrier semaphores. Data moves between devices by JAX's collectives and lax.ppermute only.
A program may use at most 128 MiB of HBM per device.

v0:
```python
import math

import jax
import jax.numpy as jnp
from jax import lax
from jax.sharding import PartitionSpec as P

HEADS = 16
HD = 80
WIN = 128


EPSILON = 1e-06


def rms_norm(device_rows):
    widened = device_rows.astype(jnp.float32)
    inverse_spread = lax.rsqrt(jnp.mean(widened * widened, axis=-1, keepdims=True) + EPSILON)
    return (widened * inverse_spread, inverse_spread)


def softmax_probs(query_rows, key_rows, allowed, score_scale):
    scores = (
        jnp.einsum("wihd,wjhd->whij", query_rows, key_rows, preferred_element_type=jnp.float32)
        * score_scale
    )
    scores = jnp.where(allowed[:, None], scores, -1e30)
    row_max = jnp.max(scores, axis=-1, keepdims=True)
    expanded = jnp.exp(scores - row_max)
    return expanded / jnp.sum(expanded, axis=-1, keepdims=True)


def body(
    patches, ln_gain, qkv_weight, out_weight, image_counts, window_order, owner_map, owner_grads
):
    pack_size = patches.shape[0]
    model_width = patches.shape[1]
    windows = pack_size // WIN
    score_scale = HD ** (-0.5)
    devices = lax.axis_size(("grp", "enc"))
    total_slots = owner_grads.shape[0]
    capacity = total_slots // devices
    row_order = window_order.reshape(pack_size)
    owners = owner_map[:, 0]
    onehot = (owners[:, None] == jnp.arange(devices, dtype=jnp.int32)[None, :]).astype(jnp.int32)
    before = jnp.cumsum(onehot, axis=0) - onehot
    slot_index = jnp.sum(before * onehot, axis=1)
    target_window = (owners * capacity + slot_index)[row_order]
    returned = lax.all_to_all(owner_grads, ("grp", "enc"), split_axis=0, concat_axis=0, tiled=True)
    grad_embeds = returned[target_window]
    image_ends = jnp.cumsum(image_counts[0])
    image_of = jnp.sum(
        jnp.arange(pack_size, dtype=jnp.int32)[:, None] >= image_ends[None, :], axis=1
    )
    image_window = image_of[row_order].reshape(windows, WIN)
    allowed = image_window[:, :, None] == image_window[:, None, :]
    ordered = patches[row_order]
    scaled, inverse_spread = rms_norm(ordered)
    normed = (scaled * ln_gain).astype(jnp.bfloat16)
    piece_qkv = lax.all_gather(qkv_weight, "enc", axis=0, tiled=True)
    piece_out = lax.all_gather(out_weight, "enc", axis=0, tiled=True)
    summed = jnp.dot(normed, piece_qkv, preferred_element_type=jnp.float32)
    qkv = summed.astype(jnp.bfloat16)
    query_rows = qkv[:, :model_width].reshape(windows, WIN, HEADS, HD)
    key_rows = qkv[:, model_width : 2 * model_width].reshape(windows, WIN, HEADS, HD)
    value_rows = qkv[:, 2 * model_width :].reshape(windows, WIN, HEADS, HD)
    attn_probs = softmax_probs(query_rows, key_rows, allowed, score_scale)
    probs_bf16 = attn_probs.astype(jnp.bfloat16)
    attended = jnp.einsum(
        "whij,wjhd->wihd", probs_bf16, value_rows, preferred_element_type=jnp.float32
    )
    attended = attended.astype(jnp.bfloat16).reshape(pack_size, model_width)
    embeds = (
        ordered.astype(jnp.float32)
        + jnp.dot(attended, piece_out, preferred_element_type=jnp.float32)
    ).astype(jnp.bfloat16)
    outgoing = jnp.zeros((total_slots, model_width), jnp.bfloat16).at[target_window].set(embeds)
    owner_rows = lax.all_to_all(outgoing, ("grp", "enc"), split_axis=0, concat_axis=0, tiled=True)
    grad_attended = jnp.einsum(
        "ro,io->ri", grad_embeds, piece_out, preferred_element_type=jnp.float32
    ).astype(jnp.bfloat16)
    grad_heads = grad_attended.reshape(windows, WIN, HEADS, HD)
    grad_value = jnp.einsum(
        "whij,wihd->wjhd", probs_bf16, grad_heads, preferred_element_type=jnp.float32
    ).astype(jnp.bfloat16)
    grad_probs = jnp.einsum(
        "wihd,wjhd->whij", grad_heads, value_rows, preferred_element_type=jnp.float32
    )
    inner = jnp.sum(attn_probs * grad_probs, axis=-1, keepdims=True)
    grad_scores = (attn_probs * (grad_probs - inner) * score_scale).astype(jnp.bfloat16)
    grad_query = jnp.einsum(
        "whij,wjhd->wihd", grad_scores, key_rows, preferred_element_type=jnp.float32
    ).astype(jnp.bfloat16)
    grad_key = jnp.einsum(
        "whij,wihd->wjhd", grad_scores, query_rows, preferred_element_type=jnp.float32
    ).astype(jnp.bfloat16)
    grad_qkv = jnp.concatenate(
        [
            grad_query.reshape(pack_size, model_width),
            grad_key.reshape(pack_size, model_width),
            grad_value.reshape(pack_size, model_width),
        ],
        axis=1,
    )
    grad_normed = jnp.einsum(
        "rk,ck->rc", grad_qkv, piece_qkv, preferred_element_type=jnp.float32
    ).astype(jnp.bfloat16)
    scaled_grad = grad_normed.astype(jnp.float32) * ln_gain
    grad_layer = (
        scaled_grad - scaled * jnp.mean(scaled_grad * scaled, axis=-1, keepdims=True)
    ) * inverse_spread
    window_grads = (grad_embeds.astype(jnp.float32) + grad_layer).astype(jnp.bfloat16)
    patch_grads = jnp.zeros((pack_size, model_width), jnp.bfloat16).at[row_order].set(window_grads)
    first_block = jnp.einsum("rc,rk->ck", normed, grad_qkv, preferred_element_type=jnp.float32)
    second_block = jnp.einsum(
        "rc,rk->ck", attended, grad_embeds, preferred_element_type=jnp.float32
    )
    group_share = lax.psum_scatter(
        jnp.concatenate([first_block, second_block], axis=1).astype(jnp.bfloat16),
        "enc",
        scatter_dimension=0,
        tiled=True,
    )
    summed_all = lax.psum(group_share, "grp").astype(jnp.float32)
    grad_factor = 1.0 / math.sqrt(pack_size * devices)
    qkv_grad = summed_all[:, : 3 * model_width] * grad_factor
    out_grad = summed_all[:, 3 * model_width :] * grad_factor
    return (owner_rows, patch_grads, qkv_grad, out_grad)


def solution(mesh):
    in_specs = (
        P(("grp", "enc"), None),
        P(),
        P("enc", None),
        P("enc", None),
        P(("grp", "enc"), None),
        P(("grp", "enc"), None),
        P(("grp", "enc"), None),
        P(("grp", "enc"), None),
    )
    out_specs = (P(("grp", "enc"), None), P(("grp", "enc"), None), P("enc", None), P("enc", None))
    return jax.shard_map(body, mesh=mesh, in_specs=in_specs, out_specs=out_specs, check_vma=False)
```

profile of v0, /device:TPU:0, one launch (start us, length us, event | category | flops | bytes accessed | tf_op | source)
XLA Modules:
  0.0 340.2 jit_solution(12587545354844730988)
XLA Ops:
  7.2 0.7 all-gather.5.cloned.1.call-update
  8.0 0.7 all-gather.3.cloned.1.call-update
  8.7 3.5 %all_to_all.19 = bf16[128,4,1280]{2,1,0:T(4,128)(2,1)} reshape(bf16[512,1280]{1,0:T(8,128)(2,1)} %param.15) | data formatting | bytes 2621440 | tf_op jit(solution)/shard_map/all_to_all | solution.py:49
  12.2 11.1 %all-to-all-start.1 = ((bf16[128,4,1280]{2,1,0:T(4,128)(2,1)}), bf16[128,4,1280]{2,1,0:T(4,128)(2,1)S(1)}, u32[]{:S(2)}, u32[]{:S(2)}) async-start(bf16[128,4,1280]{2,1,0:T(4,128)(2,1)} %all_to_all.19), calls=%async_computation.1 | async-start | bytes 2621440 | tf_op jit(solution)/shard_map/all_to_all | solution.py:49
  24.1 1.9 gather_fusion.2
  26.3 1.9 gather_fusion
  28.2 1.3 gather_fusion.1
  29.8 16.9 %all-to-all-done.1 = bf16[128,4,1280]{2,1,0:T(4,128)(2,1)S(1)} async-done(((bf16[128,4,1280]{2,1,0:T(4,128)(2,1)}), bf16[128,4,1280]{2,1,0:T(4,128)(2,1)S(1)}, u32[]{:S(2)}, u32[]{:S(2)}) %all-to-all-start.1) | async-done | bytes 1310752 | tf_op jit(solution)/shard_map/all_to_all | solution.py:49
  46.7 0.3 all_to_all.21
  47.1 1.3 gather_fusion.3
  48.3 20.8 %all-gather.5.cloned.1.call-done = bf16[1280,1280]{1,0:T(8,128)(2,1)} async-done(((bf16[40,1280]{1,0:T(8,128)(2,1)}), bf16[1280,1280]{1,0:T(8,128)(2,1)}) %all-gather.5.cloned.1.call-update) | async-done | bytes 3276816 | tf_op jit(solution)/shard_map/all_gather | solution.py:61
  69.1 3.0 convolution_convert_fusion.4
  72.1 1.6 reshape.202
  73.7 1.0 copy.60
  74.7 52.5 %all-gather.3.cloned.1.call-done = bf16[1280,3840]{1,0:T(8,128)(2,1)} async-done(((bf16[40,3840]{1,0:T(8,128)(2,1)}), bf16[1280,3840]{1,0:T(8,128)(2,1)}) %all-gather.3.cloned.1.call-update) | async-done | bytes 9830416 | tf_op jit(solution)/shard_map/all_gather | solution.py:60
  127.2 6.6 %convolution_convert_fusion.2 = bf16[256,3840]{1,0:T(8,128)(2,1)S(1)} fusion(bf16[1280,3840]{1,0:T(8,128)(2,1)} %all-gather.3.cloned.1.call-done, bf16[256,1280]{1,0:T(8,128)(2,1)S(1)} %gather_fusion.1, f32[1280]{0:T(1024)S(1)} %copy-done.10, f32[256]{0:T(256)S(1)} %add_rsqrt_fusion), kind=kOutput, calls=%fused_computation.11 | convolution fusion | flops 2518876160 | bytes 12457984 | tf_op jit(solution)/shard_map/dot_general | solution.py:62
  133.8 1.3 fusion.72
  135.1 2.5 reshape.201
  137.7 1.7 copy.55
  139.4 2.5 reshape.200
  141.9 1.7 copy.54
  143.6 2.5 reshape.199
  146.2 1.7 copy.56
  147.8 3.5 %fusion.73 = (f32[2,16,128]{2,1,0:T(8,128)S(1)}, f32[2,16,128,128]{2,3,1,0:T(8,128)}) fusion(pred[2,128,128]{1,2,0:T(8,128)(4,1)S(1)} %broadcast_compare_fusion, bf16[2,128,16,80]{1,3,2,0:T(8,128)(2,1)} %copy.54, bf16[2,128,16,80]{1,3,2,0:T(8,128)(2,1)} %copy.55), kind=kOutput, calls=%fused_computation.97 | convolution fusion | flops 85983360 | bytes 3457024 | tf_op jit(solution)/shard_map/sub | solution.py:29
  151.3 3.4 %fusion.38 = bf16[2,128,16,80]{1,3,2,0:T(8,128)(2,1)} fusion(bf16[2,128,16,80]{1,3,2,0:T(8,128)(2,1)S(1)} %copy.60, f32[2,16,128,128]{2,3,1,0:T(8,128)} %get-tuple-element.8, f32[2,16,128]{2,1,0:T(8,128)S(1)} %get-tuple-element.7), kind=kOutput, calls=%fused_computation.45 | convolution fusion | flops 85262336 | bytes 3424256 | tf_op jit(solution)/shard_map/whij,wihd->wjhd/dot_general | solution.py:83
  154.8 1.3 fusion.37
  156.1 1.8 fusion.74
  157.9 5.2 %fusion.34 = bf16[2,128,16,80]{1,3,2,0:T(8,128)(2,1)} fusion(bf16[2,128,16,80]{1,3,2,0:T(8,128)(2,1)S(1)} %copy-done.4, f32[2,16,128,128]{2,3,1,0:T(8,128)} %fusion.74, f32[2,16,128,128]{2,3,1,0:T(8,128)} %get-tuple-element.8, f32[2,16,128]{2,1,0:T(8,128)S(1)} %get-tuple-element.7), kind=kOutput, calls=%fused_computation.43 | convolution fusion | flops 87888000 | bytes 5521408 | tf_op jit(solution)/shard_map/whij,wjhd->wihd/dot_general | solution.py:91
  163.2 5.2 %fusion.31 = bf16[2,128,16,80]{1,3,2,0:T(8,128)(2,1)} fusion(bf16[2,128,16,80]{1,3,2,0:T(8,128)(2,1)S(1)} %copy-done.5, f32[2,16,128,128]{2,3,1,0:T(8,128)} %fusion.74, f32[2,16,128,128]{2,3,1,0:T(8,128)} %get-tuple-element.8, f32[2,16,128]{2,1,0:T(8,128)S(1)} %get-tuple-element.7), kind=kOutput, calls=%fused_computation.42 | convolution fusion | flops 87888000 | bytes 5521408 | tf_op jit(solution)/shard_map/whij,wihd->wjhd/dot_general | solution.py:94
  168.4 0.7 copy.70
  169.1 0.7 copy.58
  169.8 0.7 copy.67
  170.5 0.7 copy.64
  171.3 1.0 convolution_convert_fusion.1
  172.5 3.3 convolution_convert_fusion
  175.8 5.8 %pad_maximum_fusion = bf16[1280,5120]{1,0:T(8,128)(2,1)} fusion(bf16[1280,1280]{1,0:T(8,128)(2,1)S(1)} %convolution_convert_fusion.1, bf16[1280,3840]{1,0:T(8,128)(2,1)S(1)} %convolution_convert_fusion), kind=kLoop, calls=%fused_computation.9 | loop fusion | flops 26214400 | bytes 26214400 | tf_op jit(solution)/shard_map/concatenate | solution.py:119
  181.6 3.0 fusion.4
  184.6 2.1 scatter_custom_fusion
  186.8 1.2 all_to_all.16
  188.0 8.6 %all-to-all-start = ((bf16[128,4,1280]{2,1,0:T(4,128)(2,1)}), bf16[128,4,1280]{2,1,0:T(4,128)(2,1)}, u32[]{:S(2)}, u32[]{:S(2)}) async-start(bf16[128,4,1280]{2,1,0:T(4,128)(2,1)} %all_to_all.16), calls=%async_computation | async-start | bytes 2621440 | tf_op jit(solution)/shard_map/all_to_all | solution.py:78
  196.7 90.5 %reduce-scatter.2.cloned.1.call-done = bf16[40,5120]{1,0:T(8,128)(2,1)} async-done(((bf16[1280,5120]{1,0:T(8,128)(2,1)}), bf16[40,5120]{1,0:T(8,128)(2,1)}) %reduce-scatter.2.cloned.1.call-update) | async-done | bytes 409616 | tf_op jit(solution)/shard_map/reduce_scatter | solution.py:118
  287.2 8.4 %fusion.25 = (f32[256]{0:T(256)S(1)}, f32[256,1280]{1,0:T(8,128)}) fusion(bf16[256,1280]{1,0:T(8,128)(2,1)S(1)} %gather_fusion.1, f32[256]{0:T(256)S(1)} %add_rsqrt_fusion, f32[1280]{0:T(1024)S(1)} %copy-done.10, bf16[256,3840]{0,1:T(8,128)(2,1)} %copy-done.2, bf16[1280,3840]{1,0:T(8,128)(2,1)} %all-gather.3.cloned.1.call-done), kind=kOutput, calls=%fused_computation.36 | convolution fusion | flops 2518875904 | bytes 13769728 | tf_op jit(solution)/shard_map/rk,ck->rc/dot_general | solution.py:105
  295.5 3.7 %scatter_custom_fusion.1 = bf16[256,1280]{1,0:T(8,128)(2,1)} fusion(s32[256]{0:T(256)S(1)} %bitcast.88, f32[256,1280]{1,0:T(8,128)} %get-tuple-element.10, bf16[256,1280]{1,0:T(8,128)(2,1)S(1)} %gather_fusion.1, bf16[256,1280]{1,0:T(8,128)(2,1)S(1)} %gather_fusion.3, f32[256]{0:T(256)S(1)} %broadcast_multiply_fusion, f32[256]{0:T(256)S(1)} %add_rsqrt_fusion, ...), kind=kCustom, calls=%fused_computation.52 | custom fusion | flops 2621440 | bytes 3278850 | tf_op jit(solution)/shard_map/scatter | solution.py:113
  299.2 3.4 all_to_all.18
  302.6 28.4 %all-reduce.2.cloned.1.call-done = bf16[40,5120]{1,0:T(8,128)(2,1)} async-done(((bf16[40,5120]{1,0:T(8,128)(2,1)}), bf16[40,5120]{1,0:T(8,128)(2,1)}) %all-reduce.2.cloned.1.call-update) | async-done | bytes 409616 | tf_op jit(solution)/shard_map/psum | solution.py:124
  331.0 1.1 convert_element_type.94
  332.1 0.7 slice_multiply_fusion.1
  332.8 0.9 slice_multiply_fusion
  (60 shorter events, 1.7 us)
Async XLA Ops:
  7.2 21.0 %copy-start = (bf16[256,1280]{1,0:T(8,128)(2,1)S(1)}, bf16[256,1280]{1,0:T(8,128)(2,1)}, u32[]{:S(2)}) copy-start(bf16[256,1280]{1,0:T(8,128)(2,1)} %param.8) | copy-start | bytes 1966084
  7.2 61.9 %all-gather.5.cloned.1.call-start = ((), (), s32[]{:S(2)}) async-start(), calls=%async_computation.4 | async-start | bytes 3379200 | tf_op jit(solution)/shard_map/all_gather | solution.py:61
  7.9 119.3 %all-gather.3.cloned.1.call-start = ((), (), s32[]{:S(2)}) async-start(), calls=%async_computation.3 | async-start | bytes 10137600 | tf_op jit(solution)/shard_map/all_gather | solution.py:60
  8.7 14.7 %copy-start.11 = (s32[256,1]{0,1:T(1,128)S(1)}, s32[256,1]{0,1:T(1,128)}, u32[]{:S(2)}) copy-start(s32[256,1]{0,1:T(1,128)} %param.14) | copy-start | bytes 3076
  8.7 14.8 %copy-start.13 = (s32[1,4]{1,0:T(1,128)S(1)}, s32[1,4]{1,0:T(1,128)}, u32[]{:S(2)}) copy-start(s32[1,4]{1,0:T(1,128)} %param.12) | copy-start | bytes 52
  12.2 11.9 %copy-start.12 = (s32[2,128]{1,0:T(2,128)S(1)}, s32[2,128]{1,0:T(2,128)}, u32[]{:S(2)}) copy-start(s32[2,128]{1,0:T(2,128)} %param.13) | copy-start | bytes 3076
  12.2 34.6 %all-to-all-start.1 = ((bf16[128,4,1280]{2,1,0:T(4,128)(2,1)}), bf16[128,4,1280]{2,1,0:T(4,128)(2,1)S(1)}, u32[]{:S(2)}, u32[]{:S(2)}) async-start(bf16[128,4,1280]{2,1,0:T(4,128)(2,1)} %all_to_all.19), calls=%async_computation.1 | async-start | bytes 2621440 | tf_op jit(solution)/shard_map/all_to_all | solution.py:49
  23.3 263.8 %reduce-scatter.2.cloned.1.call-start = ((), (), s32[]{:S(2)}) async-start(), calls=%async_computation.5 | async-start | bytes 13516800 | tf_op jit(solution)/shard_map/reduce_scatter | solution.py:118
  72.1 55.1 %copy-start.10 = (f32[1280]{0:T(1024)S(1)}, f32[1280]{0:T(1024)}, u32[]{:S(2)}) copy-start(f32[1280]{0:T(1024)} %param.9) | copy-start | bytes 15364
  151.3 3.5 %copy-start.3 = (bf16[2,128,16,80]{1,3,2,0:T(8,128)(2,1)S(1)}, bf16[2,128,16,80]{1,3,2,0:T(8,128)(2,1)}, u32[]{:S(2)}) copy-start(bf16[2,128,16,80]{1,3,2,0:T(8,128)(2,1)} %copy.56) | copy-start | bytes 1966084
  151.3 3.5 %copy-start.14 = (f32[2,16,128,128]{2,3,1,0:T(8,128)S(1)}, f32[2,16,128,128]{2,3,1,0:T(8,128)}, u32[]{:S(2)}) copy-start(f32[2,16,128,128]{2,3,1,0:T(8,128)} %get-tuple-element.8) | copy-start | bytes 6291460
  156.1 1.8 copy-start.4
  157.9 5.2 %copy-start.5 = (bf16[2,128,16,80]{1,3,2,0:T(8,128)(2,1)S(1)}, bf16[2,128,16,80]{1,3,2,0:T(8,128)(2,1)}, u32[]{:S(2)}) copy-start(bf16[2,128,16,80]{1,3,2,0:T(8,128)(2,1)} %copy.54) | copy-start | bytes 1966084
  163.1 5.2 %copy-start.8 = (bf16[2,128,16,80]{1,3,2,0:T(8,128)(2,1)S(1)}, bf16[2,128,16,80]{1,3,2,0:T(8,128)(2,1)}, u32[]{:S(2)}) copy-start(bf16[2,128,16,80]{1,3,2,0:T(8,128)(2,1)} %fusion.38) | copy-start | bytes 1966084
  163.1 5.9 %copy-start.6 = (bf16[2,128,16,80]{1,3,2,0:T(8,128)(2,1)S(1)}, bf16[2,128,16,80]{1,3,2,0:T(8,128)(2,1)}, u32[]{:S(2)}) copy-start(bf16[2,128,16,80]{1,3,2,0:T(8,128)(2,1)} %fusion.37) | copy-start | bytes 1966084
  168.4 1.4 copy-start.9
  168.4 2.1 copy-start.7
  172.5 3.3 copy-start.2
  188.0 111.2 %all-to-all-start = ((bf16[128,4,1280]{2,1,0:T(4,128)(2,1)}), bf16[128,4,1280]{2,1,0:T(4,128)(2,1)}, u32[]{:S(2)}, u32[]{:S(2)}) async-start(bf16[128,4,1280]{2,1,0:T(4,128)(2,1)} %all_to_all.16), calls=%async_computation | async-start | bytes 2621440 | tf_op jit(solution)/shard_map/all_to_all | solution.py:78
  196.6 134.4 %all-reduce.2.cloned.1.call-start = ((), (), s32[]{:S(2)}) async-start(), calls=%async_computation.6 | async-start | bytes 819200 | tf_op jit(solution)/shard_map/psum | solution.py:124
  295.5 38.1 %copy-start.1 = (bf16[256,1280]{1,0:T(8,128)(2,1)S(1)}, bf16[256,1280]{1,0:T(8,128)(2,1)}, u32[]{:S(2)}) copy-start(bf16[256,1280]{1,0:T(8,128)(2,1)} %param.8) | copy-start | bytes 1966084
Sparse Core Ops, SparseCore 0:
  10.3 58.7 all-gather.4
  71.5 55.7 all-gather.2
  181.8 105.3 reduce-scatter.1
  289.5 41.4 all-reduce.1
where the time goes:
time: 341 us; the launch traced here: 340 us
  waiting for transfers between devices  211 us (62%)
  matrix products  45.8 us (13%)
  local copies, waits for them, and re-layouts  36.7 us (11%)
  starting transfers between devices  19.9 us (6%)
  between operations  14.1 us (4%)
  other arithmetic  13.1 us (4%)
    reduce_scatter x1, waiting for transfers between devices, body(): lax.psum_scatter(jnp.concatenate([first_block, second_block], axis=1).ast...  90.5 us
    all_gather x1, waiting for transfers between devices, body(): piece_qkv = lax.all_gather(qkv_weight, 'enc', axis=0, tiled=True)  52.5 us
    psum x1, waiting for transfers between devices, body(): summed_all = lax.psum(group_share, 'grp').astype(jnp.float32)  28.4 us
    all_gather x1, waiting for transfers between devices, body(): piece_out = lax.all_gather(out_weight, 'enc', axis=0, tiled=True)  20.8 us
    all_to_all x1, waiting for transfers between devices, body(): lax.all_to_all(owner_grads, ('grp', 'enc'), split_axis=0, concat_axis=0,...  16.9 us
    all_to_all x1, starting transfers between devices, body(): lax.all_to_all(owner_grads, ('grp', 'enc'), split_axis=0, concat_axis=0,...  11.1 us
    all_to_all x1, starting transfers between devices, body(): lax.all_to_all(outgoing, ('grp', 'enc'), split_axis=0, concat_axis=0, til...  8.6 us
    dot_general x1, matrix products, body(): jnp.einsum('rk,ck->rc', grad_qkv, piece_qkv, preferred_element_type=jnp.f...  8.36 us
  transfers between devices with their start and end apart: 6, of which 5 were waited for; matrix products, arithmetic and copies ran while one was open for 9% of the time, Pallas kernels for 0%

commit v1 on v0

v1 whole, which is shorter than its diff:
```python
import math

import jax
import jax.numpy as jnp
from jax import lax
from jax.experimental import pallas as pl
from jax.experimental.pallas import tpu as pltpu
from jax.sharding import PartitionSpec as P

HEADS = 16
HD = 80
WIN = 128
EPSILON = 1e-06
D = 1280
ROWS = 256
HALF = 640
HPC = HEADS // 2
BF = jnp.bfloat16
F32 = jnp.float32
VMEM_LIMIT = 58 * 1024 * 1024
STEPS = (0, 1, -1, 2)


def ring(axis, step):
    pairs = []
    for x in range(4):
        for z in range(4):
            for c in range(2):
                to = ((x + step) % 4, z) if axis == "x" else (x, (z + step) % 4)
                pairs.append(((x * 4 + z) * 2 + c, (to[0] * 4 + to[1]) * 2 + c))
    return pairs


def hop(value, axis, step):
    if axis == "y":
        return lax.ppermute(value, "grp", [(i, (i + step) % 4) for i in range(4)])
    return lax.ppermute(value, "enc", ring(axis, step))


def to_sibling(value):
    return lax.ppermute(value, "enc", [(i, i ^ 1) for i in range(32)])


def to_halves(value, same, back=False):
    pairs = []
    for x in range(4):
        for z in range(4):
            for c in range(2):
                half = c if same else 1 - c
                source = (x * 4 + z) * 2 + c
                target = ((x % 2 + 2 * half) * 4 + z) * 2 + x // 2
                pairs.append((target, source) if back else (source, target))
    return lax.ppermute(value, "enc", pairs)


def gather_line(shard, first):
    behind = hop(shard, first, 1)
    ahead = hop(shard, first, -1)
    across = hop(shard, first, 2)
    return jnp.stack([shard, ahead, behind, across])


def gather_rest(line, second):
    line_behind = hop(line, second, 1)
    line_ahead = hop(line, second, -1)
    far_low = hop(line_behind[:2], second, 1)
    far_high = hop(line_ahead[2:], second, -1)
    return line, line_ahead, line_behind, far_low, far_high


def add(*values):
    total = values[0].astype(F32)
    for v in values[1:]:
        total = total + v.astype(F32)
    return total


def scatter_first(up, down, axis):
    return hop(up, axis, 1), hop(down, axis, -1)


def scatter_second(own, from_up, from_down, next_up, next_down, first, second):
    last_up = hop(add(next_up, from_up[:2]).astype(BF), first, 1)
    last_down = hop(add(next_down, from_down[:2]).astype(BF), first, -1)
    total = jnp.concatenate([add(own[:2], last_up, from_down[2:]), add(own[2:], from_up[2:], last_down)])
    rounded = total.astype(BF)
    one = hop(rounded[1], second, 1)
    two = hop(rounded[2], second, -1)
    three = hop(rounded[3], second, 2)
    return add(total[0], one, two, three)


def dot(a, b):
    return jnp.dot(a, b, preferred_element_type=F32)


def dot_nt(a, b):
    return lax.dot_general(a, b, (((1,), (1,)), ((), ())), preferred_element_type=F32)


def dot_tn(a, b):
    return lax.dot_general(a, b, (((0,), (0,)), ((), ())), preferred_element_type=F32)


def call(kernel, outs, ins, in_spaces, out_spaces=None, scratch=(), us=3):
    spaces = {"v": pltpu.VMEM, "s": pltpu.SMEM, "a": pltpu.HBM}
    out_spaces = out_spaces or "v" * len(outs)
    return pl.pallas_call(
        kernel,
        out_shape=[jax.ShapeDtypeStruct(s, t) for s, t in outs],
        in_specs=[pl.BlockSpec(memory_space=spaces[c]) for c in in_spaces],
        out_specs=[pl.BlockSpec(memory_space=spaces[c]) for c in out_spaces],
        scratch_shapes=list(scratch),
        compiler_params=pltpu.CompilerParams(vmem_limit_bytes=VMEM_LIMIT),
        cost_estimate=pl.CostEstimate(flops=us * 10**9, bytes_accessed=us * 3 * 10**6, transcendentals=0),
    )(*ins)


def prepare_kernel(counts, patches, gain, order, owners, naug, gather, ordered):
    rows = lax.broadcasted_iota(jnp.int32, (ROWS, ROWS), 1)
    perm = (order[...] == rows).astype(BF)
    row = lax.broadcasted_iota(jnp.int32, (ROWS, 128), 0)
    lane = lax.broadcasted_iota(jnp.int32, (ROWS, 128), 1)
    image = jnp.zeros((ROWS, 128), jnp.int32)
    end = 0
    for k in range(4):
        end = end + counts[0, k]
        image = image + (row >= end).astype(jnp.int32)
    kinds = dot(perm, (image == lane).astype(BF)).astype(BF)
    named = (owners[...] == lane).astype(BF)
    earlier = (rows < lax.broadcasted_iota(jnp.int32, (ROWS, ROWS), 0)).astype(BF)
    before = dot(earlier, named)
    slot = jnp.sum(before * named.astype(F32), axis=1, keepdims=True).astype(jnp.int32)
    target = owners[...] * 4 + slot
    slots = lax.broadcasted_iota(jnp.int32, (ROWS, 512), 1)
    gather[...] = dot(perm, (target == slots).astype(BF)).astype(BF)
    rowsw = dot(perm, patches[...])
    ordered[...] = rowsw.astype(BF)
    spread = lax.rsqrt(jnp.mean(rowsw * rowsw, axis=1, keepdims=True) + EPSILON)
    naug[:, :D] = (rowsw * spread * gain[...]).astype(BF)
    naug[:, D:] = kinds


def pick_kernel(gather, returned, out):
    out[...] = dot(gather[...], returned[...]).astype(BF)


class Copies:
    def __init__(self, sems):
        self.sems, self.used = sems, 0

    def make(self, src, dst):
        self.used += 1
        return pltpu.make_async_copy(src, dst, self.sems.at[self.used - 1])

    def start(self, src, dst):
        copy = self.make(src, dst)
        copy.start()
        return copy


def wait_all(copies):
    for c in copies:
        c.wait()


def assemble(place, parts, first, copy_one, scatter=False):
    line, ahead, behind, low, high = parts
    x, z = place[0], place[1]
    copies = []
    for i, step in enumerate(STEPS):
        for j, inner in enumerate(STEPS):
            if step == 0:
                ref = line.at[j]
            elif step == 1:
                ref = ahead.at[j]
            elif step == -1:
                ref = behind.at[j]
            else:
                ref = low.at[j] if j < 2 else high.at[j - 2]
            if scatter:
                ref = pieces_at(*parts, step, j)
            if first == "z":
                dx, dz = step, inner
            else:
                dx, dz = inner, step
            copies += copy_one(ref, (x + dx + 4) % 4, (z + dz + 4) % 4)
    return copies


def at_rows(index, size):
    return pl.ds(pl.multiple_of(index * size, size), size)


def forward_kernel(place, own, sib, a0, a1, a2, a3, a4, b0, b1, b2, b3, b4,
                   probs_out, qkv_out, attended, mine, theirs,
                   wqkv, wout, both, scores, probs, qkv, sems):
    copies = Copies(sems)
    from_a = assemble(
        place, (a0, a1, a2, a3, a4), "z",
        lambda ref, x, z: [copies.start(ref, wqkv.at[at_rows(x * 4 + z, 80), pl.ds(0, 1280)])],
    )
    from_b = assemble(
        place, (b0, b1, b2, b3, b4), "x",
        lambda ref, x, z: [
            copies.start(ref.at[:, pl.ds(0, 640)], wqkv.at[at_rows(x * 4 + z, 80), pl.ds(1280, 640)])
        ],
    )
    from_b_out = assemble(
        place, (b0, b1, b2, b3, b4), "x",
        lambda ref, x, z: [
            copies.start(ref.at[:, pl.ds(640, 640)], wout.at[at_rows((x % 2) * 4 + z, 80), at_rows(x // 2, 640)])
        ],
    )
    both[:ROWS, :] = own[:, :D]
    both[ROWS:, :] = sib[:, :D]
    wait_all(from_a)

    def project(col):
        qkv[:, col] = dot(both[...], wqkv[:, col]).astype(BF)

    @pl.loop(0, 5)
    def _(t):
        project(at_rows(t, 256))

    wait_all(from_b)
    project(pl.ds(1280, 256))
    project(pl.ds(1536, 256))
    project(pl.ds(1792, 128))
    out_copies = [copies.start(qkv, qkv_out)]
    scale = HD ** (-0.5)

    @pl.loop(0, 4)
    def _(w):
        rows = at_rows(w, WIN)
        local = at_rows(w % 2, WIN)
        kinds = jnp.where(w < 2, own[local, D:].astype(F32), sib[local, D:].astype(F32)).astype(BF)
        allowed = dot_nt(kinds, kinds) > 0.5
        for h in range(HPC):
            q = qkv[rows, h * HD:(h + 1) * HD]
            k = qkv[rows, HALF + h * HD:HALF + (h + 1) * HD]
            scores[h] = dot_nt(k, q)
        for h in range(HPC):
            s = jnp.where(allowed, scores[h] * scale, -1e30)
            e = jnp.exp(s - jnp.max(s, axis=0, keepdims=True))
            probs[w, h] = e * (1.0 / jnp.sum(e, axis=0, keepdims=True))
        for h in range(HPC):
            v = qkv[rows, 2 * HALF + h * HD:2 * HALF + (h + 1) * HD]
            attended[rows, h * HD:(h + 1) * HD] = dot_tn(probs[w, h].astype(BF), v).astype(BF)

    out_copies.append(copies.start(probs, probs_out))
    wait_all(from_b_out)

    @pl.loop(0, 5)
    def _(t):
        col = at_rows(t, 256)
        part = dot(attended[...], wout[:, col])
        mine[:, col] = part[:ROWS]
        theirs[:, col] = part[ROWS:].astype(BF)

    wait_all(out_copies)


def embed_kernel(mine, theirs, ordered, gather, out):
    embeds = (ordered[...].astype(F32) + (mine[...] + theirs[...].astype(F32))).astype(BF)
    out[...] = dot_tn(gather[...], embeds).astype(BF)


def turn_kernel(own, sib, out):
    out[:, :ROWS] = own[:, :D].T
    out[:, ROWS:] = sib[:, :D].T


def pieces_at(own, up, down, next_up, next_down, step, inner):
    if step == 0:
        return own.at[inner]
    if step == 1:
        return next_up.at[inner] if inner < 2 else up.at[inner]
    if step == -1:
        return down.at[inner + 2] if inner < 2 else next_down.at[inner - 2]
    return up.at[inner] if inner < 2 else down.at[inner - 2]


def backward_kernel(place, gown, gsib, b0, b1, b2, b3, b4, normed_hbm, probs_hbm, qkv_hbm, attended_hbm,
                    gqkv_out, aown, aup, adown, alow, ahigh, bown, bup, bdown, blow, bhigh,
                    wout, grads, gatt, terms, oterms, scores, small, normed_t, attended, attended_t,
                    probs, qkv, gqkv, sems):
    copies = Copies(sems)
    grads_in = [
        copies.start(gown, grads.at[pl.ds(0, ROWS)]),
        copies.start(gsib, grads.at[pl.ds(ROWS, ROWS)]),
    ]
    grads_in += assemble(
        place, (b0, b1, b2, b3, b4), "x",
        lambda ref, x, z: [
            copies.start(ref.at[:, pl.ds(640, 640)], wout.at[at_rows((x % 2) * 4 + z, 80), at_rows(x // 2, 640)])
        ],
    )
    first_in = [copies.start(qkv_hbm, qkv), copies.start(probs_hbm, probs)]
    second_in = [copies.start(attended_hbm, attended), copies.start(normed_hbm, normed_t)]
    wait_all(grads_in)
    gatt[...] = dot_nt(grads[...], wout[...]).astype(BF)
    scale = HD ** (-0.5)
    wait_all(first_in)

    @pl.loop(0, 4)
    def _(w):
        rows = at_rows(w, WIN)
        for h in range(HPC):
            a, b = h * HD, (h + 1) * HD
            scores[h] = dot_nt(qkv[rows, 2 * HALF + a:2 * HALF + b], gatt[rows, a:b])
        for h in range(HPC):
            a, b = h * HD, (h + 1) * HD
            gqkv[rows, 2 * HALF + a:2 * HALF + b] = dot(probs[w, h].astype(BF), gatt[rows, a:b]).astype(BF)
        for h in range(HPC):
            p = probs[w, h]
            g = scores[h]
            inner = jnp.sum(p * g, axis=0, keepdims=True)
            small[h] = (p * (g - inner) * scale).astype(BF)
        for h in range(HPC):
            a, b = h * HD, (h + 1) * HD
            gqkv[rows, HALF + a:HALF + b] = dot(small[h], qkv[rows, a:b]).astype(BF)
            gqkv[rows, a:b] = dot_tn(small[h], qkv[rows, HALF + a:HALF + b]).astype(BF)

    out_copies = [copies.start(gqkv, gqkv_out)]
    wait_all(second_in)

    def weigh(col):
        terms[:, col] = dot(normed_t[...], gqkv[:, col]).astype(BF)

    @pl.loop(0, 5)
    def _(t):
        weigh(at_rows(t, 256))

    out_copies += assemble(
        place, (aown, aup, adown, alow, ahigh), "z",
        lambda ref, x, z: [copies.start(terms.at[at_rows(x * 4 + z, 80), pl.ds(0, 1280)], ref)],
        scatter=True,
    )
    weigh(pl.ds(1280, 256))
    weigh(pl.ds(1536, 256))
    weigh(pl.ds(1792, 128))
    out_copies += assemble(
        place, (bown, bup, bdown, blow, bhigh), "x",
        lambda ref, x, z: [
            copies.start(terms.at[at_rows(x * 4 + z, 80), pl.ds(1280, 640)], ref.at[:, pl.ds(0, 640)])
        ],
        scatter=True,
    )
    attended_t[...] = attended[...].T

    @pl.loop(0, 5)
    def _(t):
        col = at_rows(t, 256)
        oterms[:, col] = dot(attended_t[...], grads[:, col]).astype(BF)

    out_copies += assemble(
        place, (bown, bup, bdown, blow, bhigh), "x",
        lambda ref, x, z: [
            copies.start(oterms.at[at_rows((x % 2) * 4 + z, 80), at_rows(x // 2, 640)], ref.at[:, pl.ds(640, 640)])
        ],
        scatter=True,
    )
    wait_all(out_copies)


def norm_grad_kernel(place, gqkv, a0, a1, a2, a3, a4, b0, b1, b2, b3, b4, mine, theirs, wqkv, sems):
    copies = Copies(sems)
    parts = assemble(
        place, (a0, a1, a2, a3, a4), "z",
        lambda ref, x, z: [copies.start(ref, wqkv.at[at_rows(x * 4 + z, 80), pl.ds(0, 1280)])],
    )
    parts += assemble(
        place, (b0, b1, b2, b3, b4), "x",
        lambda ref, x, z: [
            copies.start(ref.at[:, pl.ds(0, 640)], wqkv.at[at_rows(x * 4 + z, 80), pl.ds(1280, 640)])
        ],
    )
    wait_all(parts)
    for t in range(5):
        col = slice(t * 256, (t + 1) * 256)
        part = dot_nt(gqkv[...], wqkv[col, :])
        mine[:, col] = part[:ROWS]
        theirs[:, col] = part[ROWS:].astype(BF)


def finish_kernel(mine, theirs, ordered, gain, grads, order_t, out):
    rows = lax.broadcasted_iota(jnp.int32, (ROWS, ROWS), 0)
    back = (order_t[...] == rows).astype(BF)
    rowsw = ordered[...].astype(F32)
    spread = lax.rsqrt(jnp.mean(rowsw * rowsw, axis=1, keepdims=True) + EPSILON)
    scaled = rowsw * spread
    normed = (mine[...] + theirs[...].astype(F32)).astype(BF).astype(F32)
    u = normed * gain[...]
    layer = (u - scaled * jnp.mean(u * scaled, axis=1, keepdims=True)) * spread
    window = (grads[...].astype(F32) + layer).astype(BF)
    out[...] = dot(back, window).astype(BF)


def body(patches, ln_gain, qkv_weight, out_weight, image_counts, window_order, owner_map, owner_grads):
    index = lax.axis_index("enc")
    x, z, core = index // 8, (index // 2) % 4, index % 2
    place = jnp.stack([x, z])
    gain = ln_gain.reshape(1, D)
    order = window_order.reshape(ROWS, 1)
    order_t = window_order.reshape(1, ROWS)

    first_core = core == 0
    with jax.named_scope("weights"):

        def columns(half):
            return jnp.concatenate([qkv_weight[:, (2 * t + half) * HALF :][:, :HALF] for t in range(3)], axis=1)

        low, high = columns(0), columns(1)
        got = to_sibling(jnp.where(first_core, high, low))
        keep = jnp.where(first_core, low, high)
        out_low, out_high = out_weight[:, :HALF], out_weight[:, HALF:]
        out_same = to_halves(jnp.where(first_core, out_low, out_high), True)
        out_other = to_halves(jnp.where(first_core, out_high, out_low), False)
    with jax.named_scope("weights"):
        shard = jnp.where(first_core, jnp.concatenate([keep, got]), jnp.concatenate([got, keep]))
        out_shard = jnp.where(
            x < 2, jnp.concatenate([out_same, out_other]), jnp.concatenate([out_other, out_same])
        )
        line_a = gather_line(shard[:, : 2 * HALF], "z")
        line_b = gather_line(jnp.concatenate([shard[:, 2 * HALF :], out_shard], axis=1), "x")
        part_a = gather_rest(line_a, "x")
        part_b = gather_rest(line_b, "z")
    with jax.named_scope("prepare"):
        naug, gather, ordered = call(
            prepare_kernel,
            [((ROWS, D + 128), BF), ((ROWS, 512), BF), ((ROWS, D), BF)],
            (image_counts, patches, gain, order, owner_map),
            "svvvv",
        )
        nsib = to_sibling(naug)
        (normed_t,) = call(turn_kernel, [((D, 512), BF)], (naug, nsib), "vv")

    with jax.named_scope("grads_in"):
        owner_grads, part_a, part_b, normed_t = lax.optimization_barrier((owner_grads, part_a, part_b, normed_t))
        returned = lax.all_to_all(owner_grads, ("grp", "enc"), split_axis=0, concat_axis=0, tiled=True)
    with jax.named_scope("forward"):
        probs, qkv, attended, mine, theirs = call(
            forward_kernel,
            [((4, HPC, WIN, WIN), F32), ((512, 3 * HALF), BF), ((512, HALF), BF), ((ROWS, D), F32), ((ROWS, D), BF)],
            (place, naug, nsib, *part_a, *part_b),
            "svv" + "a" * 10,
            "aavvv",
            scratch=[
                pltpu.VMEM((D, 3 * HALF), BF),
                pltpu.VMEM((HALF, D), BF),
                pltpu.VMEM((512, D), BF),
                pltpu.VMEM((HPC, WIN, WIN), F32),
                pltpu.VMEM((4, HPC, WIN, WIN), F32),
                pltpu.VMEM((512, 3 * HALF), BF),
                pltpu.SemaphoreType.DMA((50,)),
            ],
            us=14,
        )
        from_sib = to_sibling(theirs)
        (outgoing,) = call(embed_kernel, [((512, D), BF)], (mine, from_sib, ordered, gather), "vvvv")
    with jax.named_scope("grads_in"):
        returned, _ = lax.optimization_barrier((returned, outgoing))
        (gown,) = call(pick_kernel, [((ROWS, D), BF)], (gather, returned), "vv")
        gsib = to_sibling(gown)
    with jax.named_scope("backward"):
        gown, gsib, outgoing = lax.optimization_barrier((gown, gsib, outgoing.reshape(128, 4, D)))
        pieces = [((4, 80, D), BF)] * 3 + [((2, 80, D), BF)] * 2
        gqkv, *terms = call(
            backward_kernel,
            [((512, 3 * HALF), BF)] + pieces + pieces,
            (place, gown, gsib, *part_b, normed_t, probs, qkv, attended),
            "s" + "a" * 11,
            "a" * 11,
            scratch=[
                pltpu.VMEM((HALF, D), BF),
                pltpu.VMEM((512, D), BF),
                pltpu.VMEM((512, HALF), BF),
                pltpu.VMEM((D, 3 * HALF), BF),
                pltpu.VMEM((HALF, D), BF),
                pltpu.VMEM((HPC, WIN, WIN), F32),
                pltpu.VMEM((HPC, WIN, WIN), BF),
                pltpu.VMEM((D, 512), BF),
                pltpu.VMEM((512, HALF), BF),
                pltpu.VMEM((HALF, 512), BF),
                pltpu.VMEM((4, HPC, WIN, WIN), F32),
                pltpu.VMEM((512, 3 * HALF), BF),
                pltpu.VMEM((512, 3 * HALF), BF),
                pltpu.SemaphoreType.DMA((72,)),
            ],
            us=21,
        )
    with jax.named_scope("rows_out"):
        owner_rows = lax.all_to_all(outgoing, ("grp", "enc"), split_axis=0, concat_axis=0, tiled=True)
        owner_rows = owner_rows.reshape(512, D)
        owner_rows, terms = lax.optimization_barrier((owner_rows, terms))
    with jax.named_scope("weight_grads"):
        up_a, down_a = scatter_first(*terms[1:3], "x")
        up_b, down_b = scatter_first(*terms[6:8], "z")
    with jax.named_scope("norm_grad"):
        gqkv, up_a, down_a = lax.optimization_barrier((gqkv, up_a, down_a))
        nmine, ntheirs = call(
            norm_grad_kernel,
            [((ROWS, D), F32), ((ROWS, D), BF)],
            (place, gqkv, *part_a, *part_b),
            "sv" + "a" * 10,
            scratch=[pltpu.VMEM((D, 3 * HALF), BF), pltpu.SemaphoreType.DMA((32,))],
            us=8,
        )
    with jax.named_scope("weight_grads"):
        sum_a = scatter_second(terms[0], up_a, down_a, *terms[3:5], "x", "z")
        sum_b = scatter_second(terms[5], up_b, down_b, *terms[8:], "z", "x")
    with jax.named_scope("norm_grad"):
        nfrom = to_sibling(ntheirs)
        (patch_grads,) = call(
            finish_kernel, [((ROWS, D), BF)], (nmine, nfrom, ordered, gain, gown, order_t), "vvvvvv"
        )
    with jax.named_scope("back_to_rows"):
        mine = jnp.concatenate([sum_a, sum_b[:, :HALF]], axis=1).astype(BF)
        low, high = mine[:40], mine[40:]
        got = to_sibling(jnp.where(first_core, high, low))
        keep = jnp.where(first_core, low, high)
        out_terms = sum_b[:, HALF:].astype(BF)
        low, high = out_terms[:40], out_terms[40:]
        out_same = to_halves(jnp.where(x < 2, low, high), True, back=True)
        out_other = to_halves(jnp.where(x < 2, high, low), False, back=True)
        low, high = jnp.where(first_core, keep, got), jnp.where(first_core, got, keep)
        out_low, out_high = jnp.where(first_core, out_same, out_other), jnp.where(first_core, out_other, out_same)
        blocks = jnp.stack(
            [jnp.concatenate([low[:, t * HALF : (t + 1) * HALF], high[:, t * HALF : (t + 1) * HALF]], axis=1) for t in range(3)]
            + [jnp.concatenate([out_low, out_high], axis=1)]
        )
    with jax.named_scope("over_groups"):
        me = lax.axis_index("grp")

        def block(step):
            return lax.dynamic_index_in_dim(blocks, (me + step + 4) % 4, 0, keepdims=False)

        total = block(0).astype(F32)
        for step in STEPS[1:]:
            total = total + hop(block(step), "y", step).astype(F32)
        total = total.astype(BF)
        every = [total] + [hop(total, "y", -step) for step in STEPS[1:]]
        factor = 1.0 / math.sqrt(ROWS * 128)

        def summed(t):
            step = (t - me + 4) % 4
            value = jnp.where(
                step == 0, every[0], jnp.where(step == 1, every[1], jnp.where(step == 3, every[2], every[3]))
            )
            return value.astype(F32) * factor

        qkv_grad = jnp.concatenate([summed(t) for t in range(3)], axis=1)
        out_grad = summed(3)
    return owner_rows, patch_grads, qkv_grad, out_grad


def solution(mesh):
    rows = P(("grp", "enc"), None)
    in_specs = (rows, P(), P("enc", None), P("enc", None), rows, rows, rows, rows)
    out_specs = (rows, rows, P("enc", None), P("enc", None))
    return jax.shard_map(body, mesh=mesh, in_specs=in_specs, out_specs=out_specs, check_vma=False)
```

time: 341 us -> 224 us (0.66)
  waiting for transfers between devices: 211 us -> 64.6 us
  starting transfers between devices: 19.9 us -> 80.1 us
  Pallas kernels: 0 us -> 59.8 us
  matrix products: 45.8 us -> 0 us
  local copies, waits for them, and re-layouts: 36.7 us -> 11.9 us
  between operations: 14.1 us -> 1.2 us
  other arithmetic: 13.1 us -> 5.02 us
    reduce_scatter x1 -> x0, waiting for transfers between devices: 90.5 us -> none  [body(): lax.psum_scatter(jnp.concatenate([first_block, second_block], axis=1).ast...]
    all_gather x2 -> x0, waiting for transfers between devices: 73.3 us -> none  [the longest x1 52.5 us: body(): piece_qkv = lax.all_gather(qkv_weight, 'enc', axis=0, tiled=True)]
    ppermute x0 -> x44, waiting for transfers between devices: none -> 62.5 us  [the longest x28 51.1 us: hop(): return lax.ppermute(value, 'enc', ring(axis, step))]
    ppermute x0 -> x44, starting transfers between devices: none -> 62.3 us  [the longest x28 46.1 us: hop(): return lax.ppermute(value, 'enc', ring(axis, step))]
    pallas_call x0 -> x8, Pallas kernels: none -> 59.8 us  [call(): pl.pallas_call(kernel, out_shape=[jax.ShapeDtypeStruct(s, t) for s, t in...]
    dot_general x11 -> x0, matrix products: 42.3 us -> none  [the longest x1 8.36 us: body(): jnp.einsum('rk,ck->rc', grad_qkv, piece_qkv, preferred_element_type=jnp.f...]
    psum x1 -> x0, waiting for transfers between devices: 28.4 us -> none  [body(): summed_all = lax.psum(group_share, 'grp').astype(jnp.float32)]
    all_to_all x1, waiting for transfers between devices: 16.9 us -> 1.18 us  [body(): lax.all_to_all(owner_grads, ('grp', 'enc'), split_axis=0, concat_axis=0,...]
  transfers between devices with their start and end apart: 6 -> 46, of which waited for: 5 -> 26; matrix products, arithmetic and copies ran while one was open for 9% -> 4% of each run, Pallas kernels for 0% -> 26%
where the time goes in v1:
time: 224 us; the launch traced here: 223 us
  starting transfers between devices  80.1 us (36%)
  waiting for transfers between devices  64.6 us (29%)
  Pallas kernels  59.8 us (27%)
  local copies, waits for them, and re-layouts  11.9 us (5%)
  other arithmetic  5.02 us (2%)
    pallas_call x8, Pallas kernels, call(): pl.pallas_call(kernel, out_shape=[jax.ShapeDtypeStruct(s, t) for s, t in...  59.8 us
    ppermute x28, waiting for transfers between devices, hop(): return lax.ppermute(value, 'enc', ring(axis, step))  51.1 us
    ppermute x28, starting transfers between devices, hop(): return lax.ppermute(value, 'enc', ring(axis, step))  46.1 us
    all_to_all x1, starting transfers between devices, body(): lax.all_to_all(owner_grads, ('grp', 'enc'), split_axis=0, concat_axis=0,...  9.12 us
    all_to_all x1, starting transfers between devices, body(): lax.all_to_all(outgoing, ('grp', 'enc'), split_axis=0, concat_axis=0, til...  8.59 us
    ppermute x6, starting transfers between devices, hop(): return lax.ppermute(value, 'grp', [(i, (i + step) % 4) for i in range(4)])  8.56 us
    ppermute x6, waiting for transfers between devices, hop(): return lax.ppermute(value, 'grp', [(i, (i + step) % 4) for i in range(4)])  6.37 us
    ppermute x4, starting transfers between devices, to_halves(): return lax.ppermute(value, 'enc', pairs)  5.71 us
  transfers between devices with their start and end apart: 46, of which 26 were waited for; matrix products, arithmetic and copies ran while one was open for 4% of the time, Pallas kernels for 26%

profile of v1, /device:TPU:0, one launch (start us, length us, event | category | flops | bytes accessed | tf_op | source)
XLA Modules:
  0.0 222.5 jit_solution(3225459029990623980)
XLA Ops:
  1.5 3.2 %collective-permute-start.9 = (bf16[40,640]{1,0:T(8,128)(2,1)S(1)}, bf16[40,640]{1,0:T(8,128)(2,1)S(1)}, u32[]{:S(2)}, u32[]{:S(2)}) collective-permute-start(bf16[40,640]{1,0:T(8,128)(2,1)S(1)} %get-tuple-element.146), channel_id=1, source_target_pairs={{0,16},{1,0},{2,18},{3,2},{4,20},{5,4},{6,22},{7,6},{8,24},{9,8},{... | collective-permute-start | bytes 153608 | tf_op jit(solution)/shard_map/weights/ppermute | solution.py:53
  6.4 1.5 collective-permute-start
  10.2 4.0 %collective-permute-start.3 = (bf16[80,1280]{1,0:T(8,128)(2,1)S(1)}, bf16[80,1280]{1,0:T(8,128)(2,1)S(1)}, u32[]{:S(2)}, u32[]{:S(2)}) collective-permute-start(bf16[80,1280]{1,0:T(8,128)(2,1)S(1)} %get-tuple-element.124), channel_id=1, source_target_pairs={{0,4},{1,5},{2,6},{3,7},{4,0},{5,1},{6,2},{7,3},{8,12},{9,13},{10,... | collective-permute-start | bytes 614408 | tf_op jit(solution)/shard_map/weights/ppermute | solution.py:37
  15.2 2.2 collective-permute-start.1
  17.5 1.7 collective-permute-start.12
  20.1 2.3 %collective-permute-start.10 = (bf16[80,1280]{1,0:T(8,128)(2,1)S(1)}, bf16[80,1280]{1,0:T(8,128)(2,1)S(1)}, u32[]{:S(2)}, u32[]{:S(2)}) collective-permute-start(bf16[80,1280]{1,0:T(8,128)(2,1)S(1)} %get-tuple-element.136), channel_id=1, source_target_pairs={{0,24},{1,25},{2,26},{3,27},{4,28},{5,29},{6,30},{7,31},{8,0},{9,1... | collective-permute-start | bytes 614408 | tf_op jit(solution)/shard_map/weights/ppermute | solution.py:37
  22.4 1.5 collective-permute-done.2
  24.7 1.7 collective-permute-start.4
  27.1 2.6 %collective-permute-done.11 = bf16[80,1280]{1,0:T(8,128)(2,1)S(1)} collective-permute-done((bf16[80,1280]{1,0:T(8,128)(2,1)S(1)}, bf16[80,1280]{1,0:T(8,128)(2,1)S(1)}, u32[]{:S(2)}, u32[]{:S(2)}) %collective-permute-start.11) | collective-permute-done | bytes 204832 | tf_op jit(solution)/shard_map/weights/ppermute | solution.py:37
  30.3 2.0 collective-permute-start.14
  32.3 3.1 %prepare.2 = (bf16[256,1408]{1,0:T(8,128)(2,1)}, bf16[256,512]{1,0:T(8,128)(2,1)}, bf16[256,1280]{1,0:T(8,128)(2,1)}) custom-call(s32[1,4]{1,0:T(1,128)} %counts.1, bf16[256,1280]{1,0:T(8,128)(2,1)} %patches.1, f32[1,1280]{1,0:T(1,128)} %reshape.27.gain, s32[256,1]{1,0:T(8,128)} %copy.13.order, s32[256,1]{1,0:T(8,128)} %copy.14.owners), custom_call_target="tpu_custom_call" | custom-call | flops 3000000000 | bytes 9000000 | tf_op jit(solution)/shard_map/prepare/pallas_call | solution.py:108
  35.5 11.6 %collective-permute-done.5.a2 = bf16[4,80,1280]{2,1,0:T(8,128)(2,1)S(1)} collective-permute-done((bf16[4,80,1280]{2,1,0:T(8,128)(2,1)S(1)}, bf16[4,80,1280]{2,1,0:T(8,128)(2,1)S(1)}, u32[]{:S(2)}, u32[]{:S(2)}) %collective-permute-start.5) | collective-permute-done | bytes 819232 | tf_op jit(solution)/shard_map/weights/ppermute | solution.py:37
  48.0 3.3 %collective-permute-start.7 = (bf16[2,80,1280]{2,1,0:T(8,128)(2,1)S(1)}, bf16[2,80,1280]{2,1,0:T(8,128)(2,1)S(1)}, u32[]{:S(2)}, u32[]{:S(2)}) collective-permute-start(bf16[2,80,1280]{2,1,0:T(8,128)(2,1)S(1)} %slice.201), channel_id=1, source_target_pairs={{0,24},{1,25},{2,26},{3,27},{4,28},{5,29},{6,30},{7,31},{8,0},{9,1... | collective-permute-start | bytes 1228808 | tf_op jit(solution)/shard_map/weights/ppermute | solution.py:37
  53.2 2.4 %collective-permute-start.16 = (bf16[2,80,1280]{2,1,0:T(8,128)(2,1)S(1)}, bf16[2,80,1280]{2,1,0:T(8,128)(2,1)S(1)}, u32[]{:S(2)}, u32[]{:S(2)}) collective-permute-start(bf16[2,80,1280]{2,1,0:T(8,128)(2,1)S(1)} %slice.204), channel_id=1, source_target_pairs={{0,6},{1,7},{2,0},{3,1},{4,2},{5,3},{6,4},{7,5},{8,14},{9,15},{10,... | collective-permute-start | bytes 1228808 | tf_op jit(solution)/shard_map/weights/ppermute | solution.py:37
  56.3 2.9 %prepare.3.normed_hbm = bf16[1280,512]{1,0:T(8,128)(2,1)} custom-call(bf16[256,1408]{1,0:T(8,128)(2,1)} %get-tuple-element.56.own, bf16[256,1408]{1,0:T(8,128)(2,1)} %collective-permute-done.17.sib), custom_call_target="tpu_custom_call" | custom-call | flops 3000000000 | bytes 9000000 | tf_op jit(solution)/shard_map/prepare/pallas_call | solution.py:108
  59.4 3.1 %collective-permute-done.15.b3 = bf16[2,80,1280]{2,1,0:T(8,128)(2,1)} collective-permute-done((bf16[2,80,1280]{2,1,0:T(8,128)(2,1)S(1)}, bf16[2,80,1280]{2,1,0:T(8,128)(2,1)}, u32[]{:S(2)}, u32[]{:S(2)}) %collective-permute-start.15) | collective-permute-done | bytes 409632 | tf_op jit(solution)/shard_map/weights/ppermute | solution.py:37
  62.7 1.3 all_to_all.11
  64.0 9.1 %all-to-all-start = ((bf16[128,4,1280]{2,1,0:T(4,128)(2,1)}), bf16[128,4,1280]{2,1,0:T(4,128)(2,1)S(1)}, u32[]{:S(2)}, u32[]{:S(2)}) async-start(bf16[128,4,1280]{2,1,0:T(4,128)(2,1)} %all_to_all.11), calls=%async_computation | async-start | bytes 2621440 | tf_op jit(solution)/shard_map/grads_in/all_to_all | solution.py:441
  73.1 14.0 %forward.2 = (f32[4,8,128,128]{3,2,1,0:T(8,128)}, bf16[512,1920]{1,0:T(8,128)(2,1)}, bf16[512,640]{1,0:T(8,128)(2,1)}, f32[256,1280]{1,0:T(8,128)}, bf16[256,1280]{1,0:T(8,128)(2,1)}) custom-call(s32[2]{0:T(128)} %pad_add_fusion.place, bf16[256,1408]{1,0:T(8,128)(2,1)} %get-tuple-element.56.own, bf16[256,1408]{1,0:T(8,128)(2,1)} %collective-permute-done.17.sib, ...), custom_call_target="tpu_custom_call" | custom-call | flops 14000000000 | bytes 42000000 | tf_op jit(solution)/shard_map/forward/pallas_call | solution.py:108
  87.4 2.3 %collective-permute-done.18.theirs = bf16[256,1280]{1,0:T(8,128)(2,1)S(1)} collective-permute-done((bf16[256,1280]{1,0:T(8,128)(2,1)}, bf16[256,1280]{1,0:T(8,128)(2,1)S(1)}, u32[]{:S(2)}, u32[]{:S(2)}) %collective-permute-start.18) | collective-permute-done | bytes 655392 | tf_op jit(solution)/shard_map/forward/ppermute | solution.py:41
  90.6 3.4 %forward.3 = bf16[512,1280]{1,0:T(8,128)(2,1)} custom-call(f32[256,1280]{1,0:T(8,128)} %get-tuple-element.68.mine, bf16[256,1280]{1,0:T(8,128)(2,1)} %copy-done.19, bf16[256,1280]{1,0:T(8,128)(2,1)} %get-tuple-element.70.ordered, bf16[256,512]{1,0:T(8,128)(2,1)} %get-tuple-element.55.gather), custom_call_target="tpu_custom_call" | custom-call | flops 3000000000 | bytes 9000000 | tf_op jit(solution)/shard_map/forward/pallas_call | solution.py:108
  96.4 2.9 %grads_in.1.gown.grads = bf16[256,1280]{1,0:T(8,128)(2,1)} custom-call(bf16[256,512]{1,0:T(8,128)(2,1)} %get-tuple-element.55.gather, bf16[512,1280]{1,0:T(8,128)(2,1)} %all_to_all.13.returned), custom_call_target="tpu_custom_call" | custom-call | flops 3000000000 | bytes 9000000 | tf_op jit(solution)/shard_map/grads_in/pallas_call | solution.py:108
  99.3 1.2 reshape.29
  102.4 8.6 %all-to-all-start.1 = ((bf16[128,4,1280]{2,1,0:T(4,128)(2,1)}), bf16[128,4,1280]{2,1,0:T(4,128)(2,1)S(1)}, u32[]{:S(2)}, u32[]{:S(2)}) async-start(bf16[128,4,1280]{2,1,0:T(4,128)(2,1)} %reshape.29), calls=%async_computation.1 | async-start | bytes 2621440 | tf_op jit(solution)/shard_map/rows_out/all_to_all | solution.py:494
  111.0 21.2 %backward.1 = (bf16[512,1920]{1,0:T(8,128)(2,1)}, bf16[4,80,1280]{2,1,0:T(8,128)(2,1)}, bf16[4,80,1280]{2,1,0:T(8,128)(2,1)}, bf16[4,80,1280]{2,1,0:T(8,128)(2,1...) custom-call(s32[2]{0:T(128)} %pad_add_fusion.place, ...), custom_call_target="tpu_custom_call" | custom-call | flops 20999999488 | bytes 63000000 | tf_op jit(solution)/shard_map/backward/pallas_call | solution.py:108
  135.0 2.5 %collective-permute-start.21 = (bf16[4,80,1280]{2,1,0:T(8,128)(2,1)}, bf16[4,80,1280]{2,1,0:T(8,128)(2,1)S(1)}, u32[]{:S(2)}, u32[]{:S(2)}) collective-permute-start(bf16[4,80,1280]{2,1,0:T(8,128)(2,1)} %get-tuple-element.92), channel_id=1, source_target_pairs={{0,24},{1,25},{2,26},{3,27},{4,28},{5,29},{6,30},{7,31},{8,0},{9,1... | collective-permute-start | bytes 2457608 | tf_op jit(solution)/shard_map/weight_grads/ppermute | solution.py:37
  137.6 2.0 collective-permute-start.30
  139.6 15.6 %collective-permute-done.20 = bf16[4,80,1280]{2,1,0:T(8,128)(2,1)S(1)} collective-permute-done((bf16[4,80,1280]{2,1,0:T(8,128)(2,1)}, bf16[4,80,1280]{2,1,0:T(8,128)(2,1)S(1)}, u32[]{:S(2)}, u32[]{:S(2)}) %collective-permute-start.20) | collective-permute-done | bytes 819232 | tf_op jit(solution)/shard_map/weight_grads/ppermute | solution.py:37
  155.2 8.5 %norm_grad.2 = (f32[256,1280]{1,0:T(8,128)}, bf16[256,1280]{1,0:T(8,128)(2,1)}) custom-call(s32[2]{0:T(128)} %pad_add_fusion.place, bf16[512,1920]{1,0:T(8,128)(2,1)} %get-tuple-element.93.gqkv, bf16[4,80,1280]{2,1,0:T(8,128)(2,1)} %copy-done.4, bf16[4,80,1280]{2,1,0:T(8,128)(2,1)} %copy-done.10, bf16[4,80,1280]{2,1,0:T(8,128)(2,1)} %copy-done.11, ...), custom_call_target="tpu_custom_call" | custom-call | flops 8000000000 | bytes 24000000 | tf_op jit(solution)/shard_map/norm_grad/pallas_call | solution.py:108
  163.9 2.9 %collective-permute-start.32 = (bf16[2,80,1280]{2,1,0:T(8,128)(2,1)S(1)}, bf16[2,80,1280]{2,1,0:T(8,128)(2,1)S(1)}, u32[]{:S(2)}, u32[]{:S(2)}) collective-permute-start(bf16[2,80,1280]{2,1,0:T(8,128)(2,1)S(1)} %add_convert_fusion.1), channel_id=1, source_target_pairs={{0,6},{1,7},{2,0},{3,1},{4,2},{5,3},{6,4},{7,5},{8,14},{9,15},{10,... | collective-permute-start | bytes 1228808 | tf_op jit(solution)/shard_map/weight_grads/ppermute | solution.py:37
  167.1 3.0 %collective-permute-start.25 = (bf16[2,80,1280]{2,1,0:T(8,128)(2,1)S(1)}, bf16[2,80,1280]{2,1,0:T(8,128)(2,1)S(1)}, u32[]{:S(2)}, u32[]{:S(2)}) collective-permute-start(bf16[2,80,1280]{2,1,0:T(8,128)(2,1)S(1)} %add_convert_fusion.4), channel_id=1, source_target_pairs={{0,24},{1,25},{2,26},{3,27},{4,28},{5,29},{6,30},{7,31},{8,0},{9,1... | collective-permute-start | bytes 1228808 | tf_op jit(solution)/shard_map/weight_grads/ppermute | solution.py:37
  170.5 5.6 %collective-permute-done.32 = bf16[2,80,1280]{2,1,0:T(8,128)(2,1)S(1)} collective-permute-done((bf16[2,80,1280]{2,1,0:T(8,128)(2,1)S(1)}, bf16[2,80,1280]{2,1,0:T(8,128)(2,1)S(1)}, u32[]{:S(2)}, u32[]{:S(2)}) %collective-permute-start.32) | collective-permute-done | bytes 409632 | tf_op jit(solution)/shard_map/weight_grads/ppermute | solution.py:37
  176.2 3.6 %collective-permute-done.29 = bf16[2,80,1280]{2,1,0:T(8,128)(2,1)S(1)} collective-permute-done((bf16[2,80,1280]{2,1,0:T(8,128)(2,1)S(1)}, bf16[2,80,1280]{2,1,0:T(8,128)(2,1)S(1)}, u32[]{:S(2)}, u32[]{:S(2)}) %collective-permute-start.29) | collective-permute-done | bytes 409632 | tf_op jit(solution)/shard_map/weight_grads/ppermute | solution.py:37
  180.1 2.8 %collective-permute-start.34 = (bf16[80,1280]{1,0:T(8,128)(2,1)S(1)}, bf16[80,1280]{1,0:T(8,128)(2,1)S(1)}, u32[]{:S(2)}, u32[]{:S(2)}) collective-permute-start(bf16[80,1280]{1,0:T(8,128)(2,1)S(1)} %get-tuple-element.122), channel_id=1, source_target_pairs={{0,16},{1,17},{2,18},{3,19},{4,20},{5,21},{6,22},{7,23},{8,24},{9,... | collective-permute-start | bytes 614408 | tf_op jit(solution)/shard_map/weight_grads/ppermute | solution.py:37
  182.9 1.4 collective-permute-start.33
  185.4 5.5 %collective-permute-start.27 = (bf16[80,1280]{1,0:T(8,128)(2,1)S(1)}, bf16[80,1280]{1,0:T(8,128)(2,1)S(1)}, u32[]{:S(2)}, u32[]{:S(2)}) collective-permute-start(bf16[80,1280]{1,0:T(8,128)(2,1)S(1)} %get-tuple-element.120), channel_id=1, source_target_pairs={{0,4},{1,5},{2,6},{3,7},{4,0},{5,1},{6,2},{7,3},{8,12},{9,13},{10,... | collective-permute-start | bytes 614408 | tf_op jit(solution)/shard_map/weight_grads/ppermute | solution.py:37
  190.9 1.3 collective-permute-start.26
  194.0 2.2 %collective-permute-done.27 = bf16[80,1280]{1,0:T(8,128)(2,1)S(1)} collective-permute-done((bf16[80,1280]{1,0:T(8,128)(2,1)S(1)}, bf16[80,1280]{1,0:T(8,128)(2,1)S(1)}, u32[]{:S(2)}, u32[]{:S(2)}) %collective-permute-start.27) | collective-permute-done | bytes 204832 | tf_op jit(solution)/shard_map/weight_grads/ppermute | solution.py:37
  196.2 1.2 collective-permute-start.37
  197.4 1.5 collective-permute-done.26
  200.2 1.6 collective-permute-done.37
  202.2 3.2 %collective-permute-start.40 = (bf16[40,1280]{1,0:T(8,128)(2,1)S(1)}, bf16[40,1280]{1,0:T(8,128)(2,1)S(1)}, u32[]{:S(2)}, u32[]{:S(2)}) collective-permute-start(bf16[40,1280]{1,0:T(8,128)(2,1)S(1)} %get-tuple-element.117), channel_id=1, source_target_pairs={{0,64},{32,96},{64,0},{96,32},{1,65},{33,97},{65,1},{97,33},{2,66}... | collective-permute-start | bytes 307208 | tf_op jit(solution)/shard_map/over_groups/ppermute | solution.py:36
  207.4 1.3 collective-permute-done.40
  208.7 2.1 collective-permute-done.39
  210.7 1.6 collective-permute-done.38
  214.5 1.3 collective-permute-start.43
  215.8 3.7 %norm_grad.3 = bf16[256,1280]{1,0:T(8,128)(2,1)} custom-call(f32[256,1280]{1,0:T(8,128)} %get-tuple-element.94.mine, bf16[256,1280]{1,0:T(8,128)(2,1)} %collective-permute-done.22.theirs, bf16[256,1280]{1,0:T(8,128)(2,1)} %get-tuple-element.70.ordered, f32[1,1280]{1,0:T(1,128)} %reshape.27.gain, bf16[256,1280]{1,0:T(8,128)(2,1)} %grads_in.1.gown.grads, ...), custom_call_target="tpu_custom_call" | custom-call | flops 3000000000 | bytes 9000000 | tf_op jit(solution)/shard_map/norm_grad/pallas_call | solution.py:108
  219.5 1.4 collective-permute-done.42
  (145 shorter events, 32.5 us)
Async XLA Ops:
  1.5 8.6 %collective-permute-start.9 = (bf16[40,640]{1,0:T(8,128)(2,1)S(1)}, bf16[40,640]{1,0:T(8,128)(2,1)S(1)}, u32[]{:S(2)}, u32[]{:S(2)}) collective-permute-start(bf16[40,640]{1,0:T(8,128)(2,1)S(1)} %get-tuple-element.146), channel_id=1, source_target_pairs={{0,16},{1,0},{2,18},{3,2},{4,20},{5,4},{6,22},{7,6},{8,24},{9,8},{... | collective-permute-start | bytes 153608 | tf_op jit(solution)/shard_map/weights/ppermute | solution.py:53
  4.7 5.4 %collective-permute-start.8 = (bf16[40,640]{1,0:T(8,128)(2,1)S(1)}, bf16[40,640]{1,0:T(8,128)(2,1)S(1)}, u32[]{:S(2)}, u32[]{:S(2)}) collective-permute-start(bf16[40,640]{1,0:T(8,128)(2,1)S(1)} %get-tuple-element.145), channel_id=1, source_target_pairs={{0,0},{1,16},{2,2},{3,18},{4,4},{5,20},{6,6},{7,22},{8,8},{9,24},{... | collective-permute-start | bytes 153608 | tf_op jit(solution)/shard_map/weights/ppermute | solution.py:53
  6.4 3.7 %collective-permute-start = (bf16[40,1920]{1,0:T(8,128)(2,1)S(1)}, bf16[40,1920]{1,0:T(8,128)(2,1)S(1)}, u32[]{:S(2)}, u32[]{:S(2)}) collective-permute-start(bf16[40,1920]{1,0:T(8,128)(2,1)S(1)} %get-tuple-element.126), channel_id=1, source_target_pairs={{0,1},{1,0},{2,3},{3,2},{4,5},{5,4},{6,7},{7,6},{8,9},{9,8},{10,11... | collective-permute-start | bytes 460808 | tf_op jit(solution)/shard_map/weights/ppermute | solution.py:41
  10.2 9.8 %collective-permute-start.3 = (bf16[80,1280]{1,0:T(8,128)(2,1)S(1)}, bf16[80,1280]{1,0:T(8,128)(2,1)S(1)}, u32[]{:S(2)}, u32[]{:S(2)}) collective-permute-start(bf16[80,1280]{1,0:T(8,128)(2,1)S(1)} %get-tuple-element.124), channel_id=1, source_target_pairs={{0,4},{1,5},{2,6},{3,7},{4,0},{5,1},{6,2},{7,3},{8,12},{9,13},{10,... | collective-permute-start | bytes 614408 | tf_op jit(solution)/shard_map/weights/ppermute | solution.py:37
  14.2 9.7 %collective-permute-start.2 = (bf16[80,1280]{1,0:T(8,128)(2,1)S(1)}, bf16[80,1280]{1,0:T(8,128)(2,1)S(1)}, u32[]{:S(2)}, u32[]{:S(2)}) collective-permute-start(bf16[80,1280]{1,0:T(8,128)(2,1)S(1)} %get-tuple-element.124), channel_id=1, source_target_pairs={{0,2},{1,3},{2,4},{3,5},{4,6},{5,7},{6,0},{7,1},{8,10},{9,11},{10,... | collective-permute-start | bytes 614408 | tf_op jit(solution)/shard_map/weights/ppermute | solution.py:37
  15.2 9.4 %collective-permute-start.1 = (bf16[80,1280]{1,0:T(8,128)(2,1)S(1)}, bf16[80,1280]{1,0:T(8,128)(2,1)S(1)}, u32[]{:S(2)}, u32[]{:S(2)}) collective-permute-start(bf16[80,1280]{1,0:T(8,128)(2,1)S(1)} %get-tuple-element.124), channel_id=1, source_target_pairs={{0,6},{1,7},{2,0},{3,1},{4,2},{5,3},{6,4},{7,5},{8,14},{9,15},{10,... | collective-permute-start | bytes 614408 | tf_op jit(solution)/shard_map/weights/ppermute | solution.py:37
  17.5 9.6 %collective-permute-start.12 = (bf16[80,1280]{1,0:T(8,128)(2,1)S(1)}, bf16[80,1280]{1,0:T(8,128)(2,1)S(1)}, u32[]{:S(2)}, u32[]{:S(2)}) collective-permute-start(bf16[80,1280]{1,0:T(8,128)(2,1)S(1)} %get-tuple-element.136), channel_id=1, source_target_pairs={{0,16},{1,17},{2,18},{3,19},{4,20},{5,21},{6,22},{7,23},{8,24},{9,... | collective-permute-start | bytes 614408 | tf_op jit(solution)/shard_map/weights/ppermute | solution.py:37
  19.1 10.6 %collective-permute-start.11 = (bf16[80,1280]{1,0:T(8,128)(2,1)S(1)}, bf16[80,1280]{1,0:T(8,128)(2,1)S(1)}, u32[]{:S(2)}, u32[]{:S(2)}) collective-permute-start(bf16[80,1280]{1,0:T(8,128)(2,1)S(1)} %get-tuple-element.136), channel_id=1, source_target_pairs={{0,8},{1,9},{2,10},{3,11},{4,12},{5,13},{6,14},{7,15},{8,16},{9,17... | collective-permute-start | bytes 614408 | tf_op jit(solution)/shard_map/weights/ppermute | solution.py:37
  20.1 10.0 %collective-permute-start.10 = (bf16[80,1280]{1,0:T(8,128)(2,1)S(1)}, bf16[80,1280]{1,0:T(8,128)(2,1)S(1)}, u32[]{:S(2)}, u32[]{:S(2)}) collective-permute-start(bf16[80,1280]{1,0:T(8,128)(2,1)S(1)} %get-tuple-element.136), channel_id=1, source_target_pairs={{0,24},{1,25},{2,26},{3,27},{4,28},{5,29},{6,30},{7,31},{8,0},{9,1... | collective-permute-start | bytes 614408 | tf_op jit(solution)/shard_map/weights/ppermute | solution.py:37
  24.7 10.8 %copy-start.4 = (bf16[4,80,1280]{2,1,0:T(8,128)(2,1)}, bf16[4,80,1280]{2,1,0:T(8,128)(2,1)S(1)}, u32[]{:S(2)}) copy-start(bf16[4,80,1280]{2,1,0:T(8,128)(2,1)S(1)} %pad_maximum_fusion.a0) | copy-start | bytes 2457604
  24.7 23.3 %collective-permute-start.4 = (bf16[4,80,1280]{2,1,0:T(8,128)(2,1)S(1)}, bf16[4,80,1280]{2,1,0:T(8,128)(2,1)S(1)}, u32[]{:S(2)}, u32[]{:S(2)}) collective-permute-start(bf16[4,80,1280]{2,1,0:T(8,128)(2,1)S(1)} %pad_maximum_fusion.a0), channel_id=1, source_target_pairs={{0,24},{1,25},{2,26},{3,27},{4,28},{5,29},{6,30},{7,31},{8,0},{9,1... | collective-permute-start | bytes 2457608 | tf_op jit(solution)/shard_map/weights/ppermute | solution.py:37
  26.4 20.8 %collective-permute-start.5 = (bf16[4,80,1280]{2,1,0:T(8,128)(2,1)S(1)}, bf16[4,80,1280]{2,1,0:T(8,128)(2,1)S(1)}, u32[]{:S(2)}, u32[]{:S(2)}) collective-permute-start(bf16[4,80,1280]{2,1,0:T(8,128)(2,1)S(1)} %pad_maximum_fusion.a0), channel_id=1, source_target_pairs={{0,8},{1,9},{2,10},{3,11},{4,12},{5,13},{6,14},{7,15},{8,16},{9,17... | collective-permute-start | bytes 2457608 | tf_op jit(solution)/shard_map/weights/ppermute | solution.py:37
  30.2 22.1 %collective-permute-start.13 = (bf16[4,80,1280]{2,1,0:T(8,128)(2,1)S(1)}, bf16[4,80,1280]{2,1,0:T(8,128)(2,1)S(1)}, u32[]{:S(2)}, u32[]{:S(2)}) collective-permute-start(bf16[4,80,1280]{2,1,0:T(8,128)(2,1)S(1)} %pad_maximum_fusion.1.b0), channel_id=1, source_target_pairs={{0,6},{1,7},{2,0},{3,1},{4,2},{5,3},{6,4},{7,5},{8,14},{9,15},{10,... | collective-permute-start | bytes 2457608 | tf_op jit(solution)/shard_map/weights/ppermute | solution.py:37
  30.3 21.1 %collective-permute-start.14 = (bf16[4,80,1280]{2,1,0:T(8,128)(2,1)S(1)}, bf16[4,80,1280]{2,1,0:T(8,128)(2,1)S(1)}, u32[]{:S(2)}, u32[]{:S(2)}) collective-permute-start(bf16[4,80,1280]{2,1,0:T(8,128)(2,1)S(1)} %pad_maximum_fusion.1.b0), channel_id=1, source_target_pairs={{0,2},{1,3},{2,4},{3,5},{4,6},{5,7},{6,0},{7,1},{8,10},{9,11},{10,... | collective-permute-start | bytes 2457608 | tf_op jit(solution)/shard_map/weights/ppermute | solution.py:37
  35.4 20.8 %collective-permute-start.17 = (bf16[256,1408]{1,0:T(8,128)(2,1)}, bf16[256,1408]{1,0:T(8,128)(2,1)}, u32[]{:S(2)}, u32[]{:S(2)}) collective-permute-start(bf16[256,1408]{1,0:T(8,128)(2,1)} %get-tuple-element.56.own), channel_id=1, source_target_pairs={{0,1},{1,0},{2,3},{3,2},{4,5},{5,4},{6,7},{7,6},{8,9},{9,8},{10,11... | collective-permute-start | bytes 2162696 | tf_op jit(solution)/shard_map/prepare/ppermute | solution.py:41
  48.0 11.4 %collective-permute-start.6 = (bf16[2,80,1280]{2,1,0:T(8,128)(2,1)}, bf16[2,80,1280]{2,1,0:T(8,128)(2,1)}, u32[]{:S(2)}, u32[]{:S(2)}) collective-permute-start(bf16[2,80,1280]{2,1,0:T(8,128)(2,1)} %slice.200), channel_id=1, source_target_pairs={{0,8},{1,9},{2,10},{3,11},{4,12},{5,13},{6,14},{7,15},{8,16},{9,17... | collective-permute-start | bytes 1228808 | tf_op jit(solution)/shard_map/weights/ppermute | solution.py:37
  48.0 11.4 %collective-permute-start.7 = (bf16[2,80,1280]{2,1,0:T(8,128)(2,1)S(1)}, bf16[2,80,1280]{2,1,0:T(8,128)(2,1)S(1)}, u32[]{:S(2)}, u32[]{:S(2)}) collective-permute-start(bf16[2,80,1280]{2,1,0:T(8,128)(2,1)S(1)} %slice.201), channel_id=1, source_target_pairs={{0,24},{1,25},{2,26},{3,27},{4,28},{5,29},{6,30},{7,31},{8,0},{9,1... | collective-permute-start | bytes 1228808 | tf_op jit(solution)/shard_map/weights/ppermute | solution.py:37
  51.4 11.1 %collective-permute-start.15 = (bf16[2,80,1280]{2,1,0:T(8,128)(2,1)S(1)}, bf16[2,80,1280]{2,1,0:T(8,128)(2,1)}, u32[]{:S(2)}, u32[]{:S(2)}) collective-permute-start(bf16[2,80,1280]{2,1,0:T(8,128)(2,1)S(1)} %slice.203), channel_id=1, source_target_pairs={{0,2},{1,3},{2,4},{3,5},{4,6},{5,7},{6,0},{7,1},{8,10},{9,11},{10,... | collective-permute-start | bytes 1228808 | tf_op jit(solution)/shard_map/weights/ppermute | solution.py:37
  53.2 9.5 %collective-permute-start.16 = (bf16[2,80,1280]{2,1,0:T(8,128)(2,1)S(1)}, bf16[2,80,1280]{2,1,0:T(8,128)(2,1)S(1)}, u32[]{:S(2)}, u32[]{:S(2)}) collective-permute-start(bf16[2,80,1280]{2,1,0:T(8,128)(2,1)S(1)} %slice.204), channel_id=1, source_target_pairs={{0,6},{1,7},{2,0},{3,1},{4,2},{5,3},{6,4},{7,5},{8,14},{9,15},{10,... | collective-permute-start | bytes 1228808 | tf_op jit(solution)/shard_map/weights/ppermute | solution.py:37
  64.0 31.2 %all-to-all-start = ((bf16[128,4,1280]{2,1,0:T(4,128)(2,1)}), bf16[128,4,1280]{2,1,0:T(4,128)(2,1)S(1)}, u32[]{:S(2)}, u32[]{:S(2)}) async-start(bf16[128,4,1280]{2,1,0:T(4,128)(2,1)} %all_to_all.11), calls=%async_computation | async-start | bytes 2621440 | tf_op jit(solution)/shard_map/grads_in/all_to_all | solution.py:441
  87.1 2.6 %collective-permute-start.18 = (bf16[256,1280]{1,0:T(8,128)(2,1)}, bf16[256,1280]{1,0:T(8,128)(2,1)S(1)}, u32[]{:S(2)}, u32[]{:S(2)}) collective-permute-start(bf16[256,1280]{1,0:T(8,128)(2,1)} %get-tuple-element.69), channel_id=1, source_target_pairs={{0,1},{1,0},{2,3},{3,2},{4,5},{5,4},{6,7},{7,6},{8,9},{9,8},{10,11... | collective-permute-start | bytes 1966088 | tf_op jit(solution)/shard_map/forward/ppermute | solution.py:41
  99.3 2.3 %collective-permute-start.19 = (bf16[256,1280]{1,0:T(8,128)(2,1)}, bf16[256,1280]{1,0:T(8,128)(2,1)S(1)}, u32[]{:S(2)}, u32[]{:S(2)}) collective-permute-start(bf16[256,1280]{1,0:T(8,128)(2,1)} %grads_in.1.gown.grads), channel_id=1, source_target_pairs={{0,1},{1,0},{2,3},{3,2},{4,5},{5,4},{6,7},{7,6},{8,9},{9,8},{10,11... | collective-permute-start | bytes 1966088 | tf_op jit(solution)/shard_map/grads_in/ppermute | solution.py:41
  102.4 30.7 %all-to-all-start.1 = ((bf16[128,4,1280]{2,1,0:T(4,128)(2,1)}), bf16[128,4,1280]{2,1,0:T(4,128)(2,1)S(1)}, u32[]{:S(2)}, u32[]{:S(2)}) async-start(bf16[128,4,1280]{2,1,0:T(4,128)(2,1)} %reshape.29), calls=%async_computation.1 | async-start | bytes 2621440 | tf_op jit(solution)/shard_map/rows_out/all_to_all | solution.py:494
  134.3 20.8 %collective-permute-start.20 = (bf16[4,80,1280]{2,1,0:T(8,128)(2,1)}, bf16[4,80,1280]{2,1,0:T(8,128)(2,1)S(1)}, u32[]{:S(2)}, u32[]{:S(2)}) collective-permute-start(bf16[4,80,1280]{2,1,0:T(8,128)(2,1)} %get-tuple-element.91), channel_id=1, source_target_pairs={{0,8},{1,9},{2,10},{3,11},{4,12},{5,13},{6,14},{7,15},{8,16},{9,17... | collective-permute-start | bytes 2457608 | tf_op jit(solution)/shard_map/weight_grads/ppermute | solution.py:37
  135.0 20.2 %collective-permute-start.21 = (bf16[4,80,1280]{2,1,0:T(8,128)(2,1)}, bf16[4,80,1280]{2,1,0:T(8,128)(2,1)S(1)}, u32[]{:S(2)}, u32[]{:S(2)}) collective-permute-start(bf16[4,80,1280]{2,1,0:T(8,128)(2,1)} %get-tuple-element.92), channel_id=1, source_target_pairs={{0,24},{1,25},{2,26},{3,27},{4,28},{5,29},{6,30},{7,31},{8,0},{9,1... | collective-permute-start | bytes 2457608 | tf_op jit(solution)/shard_map/weight_grads/ppermute | solution.py:37
  137.6 26.2 %collective-permute-start.30 = (bf16[4,80,1280]{2,1,0:T(8,128)(2,1)}, bf16[4,80,1280]{2,1,0:T(8,128)(2,1)S(1)}, u32[]{:S(2)}, u32[]{:S(2)}) collective-permute-start(bf16[4,80,1280]{2,1,0:T(8,128)(2,1)} %get-tuple-element.104), channel_id=1, source_target_pairs={{0,6},{1,7},{2,0},{3,1},{4,2},{5,3},{6,4},{7,5},{8,14},{9,15},{10,... | collective-permute-start | bytes 2457608 | tf_op jit(solution)/shard_map/weight_grads/ppermute | solution.py:37
  139.5 27.3 %collective-permute-start.28 = (bf16[4,80,1280]{2,1,0:T(8,128)(2,1)S(1)}, bf16[4,80,1280]{2,1,0:T(8,128)(2,1)S(1)}, u32[]{:S(2)}, u32[]{:S(2)}) collective-permute-start(bf16[4,80,1280]{2,1,0:T(8,128)(2,1)S(1)} %copy-done.17), channel_id=1, source_target_pairs={{0,2},{1,3},{2,4},{3,5},{4,6},{5,7},{6,0},{7,1},{8,10},{9,11},{10,... | collective-permute-start | bytes 2457608 | tf_op jit(solution)/shard_map/weight_grads/ppermute | solution.py:37
  163.7 52.1 %collective-permute-start.22 = (bf16[256,1280]{1,0:T(8,128)(2,1)}, bf16[256,1280]{1,0:T(8,128)(2,1)}, u32[]{:S(2)}, u32[]{:S(2)}) collective-permute-start(bf16[256,1280]{1,0:T(8,128)(2,1)} %get-tuple-element.95), channel_id=1, source_target_pairs={{0,1},{1,0},{2,3},{3,2},{4,5},{5,4},{6,7},{7,6},{8,9},{9,8},{10,11... | collective-permute-start | bytes 1966088 | tf_op jit(solution)/shard_map/norm_grad/ppermute | solution.py:41
  163.9 12.3 %collective-permute-start.32 = (bf16[2,80,1280]{2,1,0:T(8,128)(2,1)S(1)}, bf16[2,80,1280]{2,1,0:T(8,128)(2,1)S(1)}, u32[]{:S(2)}, u32[]{:S(2)}) collective-permute-start(bf16[2,80,1280]{2,1,0:T(8,128)(2,1)S(1)} %add_convert_fusion.1), channel_id=1, source_target_pairs={{0,6},{1,7},{2,0},{3,1},{4,2},{5,3},{6,4},{7,5},{8,14},{9,15},{10,... | collective-permute-start | bytes 1228808 | tf_op jit(solution)/shard_map/weight_grads/ppermute | solution.py:37
  166.9 12.9 %copy-start.3 = (bf16[4,80,1280]{2,1,0:T(8,128)(2,1)S(1)}, bf16[4,80,1280]{2,1,0:T(8,128)(2,1)}, u32[]{:S(2)}) copy-start(bf16[4,80,1280]{2,1,0:T(8,128)(2,1)} %get-tuple-element.101) | copy-start | bytes 2457604
  166.9 12.8 %collective-permute-start.29 = (bf16[2,80,1280]{2,1,0:T(8,128)(2,1)S(1)}, bf16[2,80,1280]{2,1,0:T(8,128)(2,1)S(1)}, u32[]{:S(2)}, u32[]{:S(2)}) collective-permute-start(bf16[2,80,1280]{2,1,0:T(8,128)(2,1)S(1)} %add_convert_fusion.2), channel_id=1, source_target_pairs={{0,2},{1,3},{2,4},{3,5},{4,6},{5,7},{6,0},{7,1},{8,10},{9,11},{10,... | collective-permute-start | bytes 1228808 | tf_op jit(solution)/shard_map/weight_grads/ppermute | solution.py:37
  167.1 17.3 %collective-permute-start.25 = (bf16[2,80,1280]{2,1,0:T(8,128)(2,1)S(1)}, bf16[2,80,1280]{2,1,0:T(8,128)(2,1)S(1)}, u32[]{:S(2)}, u32[]{:S(2)}) collective-permute-start(bf16[2,80,1280]{2,1,0:T(8,128)(2,1)S(1)} %add_convert_fusion.4), channel_id=1, source_target_pairs={{0,24},{1,25},{2,26},{3,27},{4,28},{5,29},{6,30},{7,31},{8,0},{9,1... | collective-permute-start | bytes 1228808 | tf_op jit(solution)/shard_map/weight_grads/ppermute | solution.py:37
  170.2 14.8 %collective-permute-start.23 = (bf16[2,80,1280]{2,1,0:T(8,128)(2,1)S(1)}, bf16[2,80,1280]{2,1,0:T(8,128)(2,1)S(1)}, u32[]{:S(2)}, u32[]{:S(2)}) collective-permute-start(bf16[2,80,1280]{2,1,0:T(8,128)(2,1)S(1)} %add_convert_fusion.5), channel_id=1, source_target_pairs={{0,8},{1,9},{2,10},{3,11},{4,12},{5,13},{6,14},{7,15},{8,16},{9,17... | collective-permute-start | bytes 1228808 | tf_op jit(solution)/shard_map/weight_grads/ppermute | solution.py:37
  180.1 10.8 %collective-permute-start.34 = (bf16[80,1280]{1,0:T(8,128)(2,1)S(1)}, bf16[80,1280]{1,0:T(8,128)(2,1)S(1)}, u32[]{:S(2)}, u32[]{:S(2)}) collective-permute-start(bf16[80,1280]{1,0:T(8,128)(2,1)S(1)} %get-tuple-element.122), channel_id=1, source_target_pairs={{0,16},{1,17},{2,18},{3,19},{4,20},{5,21},{6,22},{7,23},{8,24},{9,... | collective-permute-start | bytes 614408 | tf_op jit(solution)/shard_map/weight_grads/ppermute | solution.py:37
  182.9 9.9 %collective-permute-start.33 = (bf16[80,1280]{1,0:T(8,128)(2,1)S(1)}, bf16[80,1280]{1,0:T(8,128)(2,1)S(1)}, u32[]{:S(2)}, u32[]{:S(2)}) collective-permute-start(bf16[80,1280]{1,0:T(8,128)(2,1)S(1)} %get-tuple-element.121), channel_id=1, source_target_pairs={{0,24},{1,25},{2,26},{3,27},{4,28},{5,29},{6,30},{7,31},{8,0},{9,1... | collective-permute-start | bytes 614408 | tf_op jit(solution)/shard_map/weight_grads/ppermute | solution.py:37
  184.4 8.8 %collective-permute-start.31 = (bf16[80,1280]{1,0:T(8,128)(2,1)S(1)}, bf16[80,1280]{1,0:T(8,128)(2,1)S(1)}, u32[]{:S(2)}, u32[]{:S(2)}) collective-permute-start(bf16[80,1280]{1,0:T(8,128)(2,1)S(1)} %fusion.9), channel_id=1, source_target_pairs={{0,8},{1,9},{2,10},{3,11},{4,12},{5,13},{6,14},{7,15},{8,16},{9,17... | collective-permute-start | bytes 614408 | tf_op jit(solution)/shard_map/weight_grads/ppermute | solution.py:37
  185.4 10.8 %collective-permute-start.27 = (bf16[80,1280]{1,0:T(8,128)(2,1)S(1)}, bf16[80,1280]{1,0:T(8,128)(2,1)S(1)}, u32[]{:S(2)}, u32[]{:S(2)}) collective-permute-start(bf16[80,1280]{1,0:T(8,128)(2,1)S(1)} %get-tuple-element.120), channel_id=1, source_target_pairs={{0,4},{1,5},{2,6},{3,7},{4,0},{5,1},{6,2},{7,3},{8,12},{9,13},{10,... | collective-permute-start | bytes 614408 | tf_op jit(solution)/shard_map/weight_grads/ppermute | solution.py:37
  190.9 8.0 %collective-permute-start.26 = (bf16[80,1280]{1,0:T(8,128)(2,1)S(1)}, bf16[80,1280]{1,0:T(8,128)(2,1)S(1)}, u32[]{:S(2)}, u32[]{:S(2)}) collective-permute-start(bf16[80,1280]{1,0:T(8,128)(2,1)S(1)} %get-tuple-element.119), channel_id=1, source_target_pairs={{0,6},{1,7},{2,0},{3,1},{4,2},{5,3},{6,4},{7,5},{8,14},{9,15},{10,... | collective-permute-start | bytes 614408 | tf_op jit(solution)/shard_map/weight_grads/ppermute | solution.py:37
  192.8 7.1 %collective-permute-start.24 = (bf16[80,1280]{1,0:T(8,128)(2,1)S(1)}, bf16[80,1280]{1,0:T(8,128)(2,1)S(1)}, u32[]{:S(2)}, u32[]{:S(2)}) collective-permute-start(bf16[80,1280]{1,0:T(8,128)(2,1)S(1)} %fusion.8), channel_id=1, source_target_pairs={{0,2},{1,3},{2,4},{3,5},{4,6},{5,7},{6,0},{7,1},{8,10},{9,11},{10,... | collective-permute-start | bytes 614408 | tf_op jit(solution)/shard_map/weight_grads/ppermute | solution.py:37
  193.3 6.9 %collective-permute-start.36 = (bf16[40,640]{1,0:T(8,128)(2,1)S(1)}, bf16[40,640]{1,0:T(8,128)(2,1)S(1)}, u32[]{:S(2)}, u32[]{:S(2)}) collective-permute-start(bf16[40,640]{1,0:T(8,128)(2,1)S(1)} %get-tuple-element.133), channel_id=1, source_target_pairs={{0,0},{16,1},{2,2},{18,3},{4,4},{20,5},{6,6},{22,7},{8,8},{24,9},{... | collective-permute-start | bytes 153608 | tf_op jit(solution)/shard_map/back_to_rows/ppermute | solution.py:53
  196.2 5.6 %collective-permute-start.37 = (bf16[40,640]{1,0:T(8,128)(2,1)S(1)}, bf16[40,640]{1,0:T(8,128)(2,1)S(1)}, u32[]{:S(2)}, u32[]{:S(2)}) collective-permute-start(bf16[40,640]{1,0:T(8,128)(2,1)S(1)} %get-tuple-element.134), channel_id=1, source_target_pairs={{16,0},{0,1},{18,2},{2,3},{20,4},{4,5},{22,6},{6,7},{24,8},{8,9},{... | collective-permute-start | bytes 153608 | tf_op jit(solution)/shard_map/back_to_rows/ppermute | solution.py:53
  200.1 1.8 collective-permute-start.35
  202.2 6.5 %collective-permute-start.40 = (bf16[40,1280]{1,0:T(8,128)(2,1)S(1)}, bf16[40,1280]{1,0:T(8,128)(2,1)S(1)}, u32[]{:S(2)}, u32[]{:S(2)}) collective-permute-start(bf16[40,1280]{1,0:T(8,128)(2,1)S(1)} %get-tuple-element.117), channel_id=1, source_target_pairs={{0,64},{32,96},{64,0},{96,32},{1,65},{33,97},{65,1},{97,33},{2,66}... | collective-permute-start | bytes 307208 | tf_op jit(solution)/shard_map/over_groups/ppermute | solution.py:36
  205.3 5.4 %collective-permute-start.39 = (bf16[40,1280]{1,0:T(8,128)(2,1)S(1)}, bf16[40,1280]{1,0:T(8,128)(2,1)S(1)}, u32[]{:S(2)}, u32[]{:S(2)}) collective-permute-start(bf16[40,1280]{1,0:T(8,128)(2,1)S(1)} %get-tuple-element.118), channel_id=1, source_target_pairs={{0,96},{32,0},{64,32},{96,64},{1,97},{33,1},{65,33},{97,65},{2,98}... | collective-permute-start | bytes 307208 | tf_op jit(solution)/shard_map/over_groups/ppermute | solution.py:36
  206.5 5.9 %collective-permute-start.38 = (bf16[40,1280]{1,0:T(8,128)(2,1)S(1)}, bf16[40,1280]{1,0:T(8,128)(2,1)S(1)}, u32[]{:S(2)}, u32[]{:S(2)}) collective-permute-start(bf16[40,1280]{1,0:T(8,128)(2,1)S(1)} %get-tuple-element.116), channel_id=1, source_target_pairs={{0,32},{32,64},{64,96},{96,0},{1,33},{33,65},{65,97},{97,1},{2,34}... | collective-permute-start | bytes 307208 | tf_op jit(solution)/shard_map/over_groups/ppermute | solution.py:36
  212.4 7.1 %collective-permute-start.41 = (bf16[40,1280]{1,0:T(8,128)(2,1)S(1)}, bf16[40,1280]{1,0:T(8,128)(2,1)S(1)}, u32[]{:S(2)}, u32[]{:S(2)}) collective-permute-start(bf16[40,1280]{1,0:T(8,128)(2,1)S(1)} %fusion.12), channel_id=1, source_target_pairs={{0,96},{32,0},{64,32},{96,64},{1,97},{33,1},{65,33},{97,65},{2,98}... | collective-permute-start | bytes 307208 | tf_op jit(solution)/shard_map/over_groups/ppermute | solution.py:36
  213.5 7.4 %collective-permute-start.42 = (bf16[40,1280]{1,0:T(8,128)(2,1)S(1)}, bf16[40,1280]{1,0:T(8,128)(2,1)S(1)}, u32[]{:S(2)}, u32[]{:S(2)}) collective-permute-start(bf16[40,1280]{1,0:T(8,128)(2,1)S(1)} %fusion.12), channel_id=1, source_target_pairs={{0,32},{32,64},{64,96},{96,0},{1,33},{33,65},{65,97},{97,1},{2,34}... | collective-permute-start | bytes 307208 | tf_op jit(solution)/shard_map/over_groups/ppermute | solution.py:36
  214.5 6.4 %collective-permute-start.43 = (bf16[40,1280]{1,0:T(8,128)(2,1)S(1)}, bf16[40,1280]{1,0:T(8,128)(2,1)S(1)}, u32[]{:S(2)}, u32[]{:S(2)}) collective-permute-start(bf16[40,1280]{1,0:T(8,128)(2,1)S(1)} %fusion.12), channel_id=1, source_target_pairs={{0,64},{32,96},{64,0},{96,32},{1,65},{33,97},{65,1},{97,33},{2,66}... | collective-permute-start | bytes 307208 | tf_op jit(solution)/shard_map/over_groups/ppermute | solution.py:36
  (20 other events, 90.8 us)

commit v2 on v1

--- a/solution.py
+++ b/solution.py
@@ -15,6 +15,7 @@
 ROWS = 256
 HALF = 640
 HPC = HEADS // 2
+SLOTS = 1024
 BF = jnp.bfloat16
 F32 = jnp.float32
 VMEM_LIMIT = 58 * 1024 * 1024
@@ -39,18 +40,6 @@
 
 def to_sibling(value):
     return lax.ppermute(value, "enc", [(i, i ^ 1) for i in range(32)])
-
-
-def to_halves(value, same, back=False):
-    pairs = []
-    for x in range(4):
-        for z in range(4):
-            for c in range(2):
-                half = c if same else 1 - c
-                source = (x * 4 + z) * 2 + c
-                target = ((x % 2 + 2 * half) * 4 + z) * 2 + x // 2
-                pairs.append((target, source) if back else (source, target))
-    return lax.ppermute(value, "enc", pairs)
 
 
 def gather_line(shard, first):
@@ -116,7 +105,11 @@
     )(*ins)
 
 
-def prepare_kernel(counts, patches, gain, order, owners, naug, gather, ordered):
+def half_of(place, value):
+    return jnp.where(place[2] == 0, value[:, :HALF], value[:, HALF:])
+
+
+def prepare_kernel(place, counts, patches, gain, order, owners, naug, extra, ordered):
     rows = lax.broadcasted_iota(jnp.int32, (ROWS, ROWS), 1)
     perm = (order[...] == rows).astype(BF)
     row = lax.broadcasted_iota(jnp.int32, (ROWS, 128), 0)
@@ -131,18 +124,15 @@
     earlier = (rows < lax.broadcasted_iota(jnp.int32, (ROWS, ROWS), 0)).astype(BF)
     before = dot(earlier, named)
     slot = jnp.sum(before * named.astype(F32), axis=1, keepdims=True).astype(jnp.int32)
-    target = owners[...] * 4 + slot
-    slots = lax.broadcasted_iota(jnp.int32, (ROWS, 512), 1)
-    gather[...] = dot(perm, (target == slots).astype(BF)).astype(BF)
+    target = owners[...] * 8 + place[2] * 4 + slot
+    slots = lax.broadcasted_iota(jnp.int32, (ROWS, SLOTS), 1)
+    extra[:, :SLOTS] = dot(perm, (target == slots).astype(BF)).astype(BF)
     rowsw = dot(perm, patches[...])
     ordered[...] = rowsw.astype(BF)
+    extra[:, SLOTS:] = jnp.where(place[2] == 0, rowsw[:, HALF:], rowsw[:, :HALF]).astype(BF)
     spread = lax.rsqrt(jnp.mean(rowsw * rowsw, axis=1, keepdims=True) + EPSILON)
     naug[:, :D] = (rowsw * spread * gain[...]).astype(BF)
     naug[:, D:] = kinds
-
-
-def pick_kernel(gather, returned, out):
-    out[...] = dot(gather[...], returned[...]).astype(BF)
 
 
 class Copies:
@@ -192,26 +182,31 @@
     return pl.ds(pl.multiple_of(index * size, size), size)
 
 
-def forward_kernel(place, own, sib, a0, a1, a2, a3, a4, b0, b1, b2, b3, b4,
-                   probs_out, qkv_out, attended, mine, theirs,
-                   wqkv, wout, both, scores, probs, qkv, sems):
-    copies = Copies(sems)
+def take_weights(copies, place, parts, wqkv):
     from_a = assemble(
-        place, (a0, a1, a2, a3, a4), "z",
+        place, parts[:5], "z",
         lambda ref, x, z: [copies.start(ref, wqkv.at[at_rows(x * 4 + z, 80), pl.ds(0, 1280)])],
     )
     from_b = assemble(
-        place, (b0, b1, b2, b3, b4), "x",
+        place, parts[5:], "x",
         lambda ref, x, z: [
             copies.start(ref.at[:, pl.ds(0, 640)], wqkv.at[at_rows(x * 4 + z, 80), pl.ds(1280, 640)])
         ],
     )
-    from_b_out = assemble(
-        place, (b0, b1, b2, b3, b4), "x",
-        lambda ref, x, z: [
-            copies.start(ref.at[:, pl.ds(640, 640)], wout.at[at_rows((x % 2) * 4 + z, 80), at_rows(x // 2, 640)])
-        ],
+    return from_a, from_b
+
+
+def take_out(copies, place, parts, wout):
+    return assemble(
+        place, parts, "x",
+        lambda ref, x, z: [copies.start(ref.at[:, pl.ds(640, 640)], wout.at[at_rows(x * 4 + z, 80)])],
     )
+
+
+def forward_kernel(place, own, sib, a0, a1, a2, a3, a4, b0, b1, b2, b3, b4,
+                   probs_out, qkv_out, attended, wqkv, both, scores, probs, qkv, sems):
+    copies = Copies(sems)
+    from_a, from_b = take_weights(copies, place, (a0, a1, a2, a3, a4, b0, b1, b2, b3, b4), wqkv)
     both[:ROWS, :] = own[:, :D]
     both[ROWS:, :] = sib[:, :D]
     wait_all(from_a)
@@ -249,21 +244,27 @@
             attended[rows, h * HD:(h + 1) * HD] = dot_tn(probs[w, h].astype(BF), v).astype(BF)
 
     out_copies.append(copies.start(probs, probs_out))
-    wait_all(from_b_out)
-
-    @pl.loop(0, 5)
-    def _(t):
-        col = at_rows(t, 256)
-        part = dot(attended[...], wout[:, col])
-        mine[:, col] = part[:ROWS]
-        theirs[:, col] = part[ROWS:].astype(BF)
-
     wait_all(out_copies)
 
 
-def embed_kernel(mine, theirs, ordered, gather, out):
-    embeds = (ordered[...].astype(F32) + (mine[...] + theirs[...].astype(F32))).astype(BF)
-    out[...] = dot_tn(gather[...], embeds).astype(BF)
+def embed_kernel(place, attended, other, ordered, extra, sib_extra, b0, b1, b2, b3, b4, out, wout, sems):
+    wait_all(take_out(Copies(sems), place, (b0, b1, b2, b3, b4), wout))
+    here, there = at_rows(place[2], HALF), at_rows(1 - place[2], HALF)
+    mine = dot(attended[:ROWS, :], wout[here, :]) + dot(other[ROWS:, :], wout[there, :])
+    theirs = dot(attended[ROWS:, :], wout[here, :]) + dot(other[:ROWS, :], wout[there, :])
+    mine = (half_of(place, ordered[...].astype(F32)) + mine).astype(BF)
+    theirs = (sib_extra[:, SLOTS:].astype(F32) + theirs).astype(BF)
+    total = dot_tn(extra[:, :SLOTS], mine) + dot_tn(sib_extra[:, :SLOTS], theirs)
+    out[...] = total.astype(BF)
+
+
+def pick_kernel(place, returned, extra, sib_extra, b0, b1, b2, b3, b4, grads, mine, theirs, wout, sems):
+    copies = take_out(Copies(sems), place, (b0, b1, b2, b3, b4), wout)
+    grads[:ROWS, :] = dot(extra[:, :SLOTS], returned[...]).astype(BF)
+    grads[ROWS:, :] = dot(sib_extra[:, :SLOTS], returned[...]).astype(BF)
+    wait_all(copies)
+    mine[...] = dot_nt(grads[...], wout[at_rows(place[2], HALF), :])
+    theirs[...] = dot_nt(grads[...], wout[at_rows(1 - place[2], HALF), :]).astype(BF)
 
 
 def turn_kernel(own, sib, out):
@@ -281,25 +282,26 @@
     return up.at[inner] if inner < 2 else down.at[inner - 2]
 
 
-def backward_kernel(place, gown, gsib, b0, b1, b2, b3, b4, normed_hbm, probs_hbm, qkv_hbm, attended_hbm,
+def backward_kernel(place, grads_hbm, ga_mine, ga_other, normed_hbm, probs_hbm, qkv_hbm, attended_hbm, other_hbm,
                     gqkv_out, aown, aup, adown, alow, ahigh, bown, bup, bdown, blow, bhigh,
-                    wout, grads, gatt, terms, oterms, scores, small, normed_t, attended, attended_t,
+                    grads, gatt, ga, gb, terms, oterms, scores, small, normed_t, attended, other, attended_t,
                     probs, qkv, gqkv, sems):
     copies = Copies(sems)
     grads_in = [
-        copies.start(gown, grads.at[pl.ds(0, ROWS)]),
-        copies.start(gsib, grads.at[pl.ds(ROWS, ROWS)]),
+        copies.start(ga_mine, ga),
+        copies.start(ga_other.at[pl.ds(ROWS, ROWS)], gb.at[pl.ds(0, ROWS)]),
+        copies.start(ga_other.at[pl.ds(0, ROWS)], gb.at[pl.ds(ROWS, ROWS)]),
     ]
-    grads_in += assemble(
-        place, (b0, b1, b2, b3, b4), "x",
-        lambda ref, x, z: [
-            copies.start(ref.at[:, pl.ds(640, 640)], wout.at[at_rows((x % 2) * 4 + z, 80), at_rows(x // 2, 640)])
-        ],
-    )
     first_in = [copies.start(qkv_hbm, qkv), copies.start(probs_hbm, probs)]
-    second_in = [copies.start(attended_hbm, attended), copies.start(normed_hbm, normed_t)]
+    second_in = [
+        copies.start(attended_hbm, attended),
+        copies.start(other_hbm.at[pl.ds(ROWS, ROWS)], other.at[pl.ds(0, ROWS)]),
+        copies.start(other_hbm.at[pl.ds(0, ROWS)], other.at[pl.ds(ROWS, ROWS)]),
+        copies.start(normed_hbm, normed_t),
+        copies.start(grads_hbm, grads),
+    ]
     wait_all(grads_in)
-    gatt[...] = dot_nt(grads[...], wout[...]).astype(BF)
+    gatt[...] = (ga[...] + gb[...].astype(F32)).astype(BF)
     scale = HD ** (-0.5)
     wait_all(first_in)
 
@@ -347,36 +349,23 @@
         ],
         scatter=True,
     )
-    attended_t[...] = attended[...].T
-
-    @pl.loop(0, 5)
-    def _(t):
-        col = at_rows(t, 256)
-        oterms[:, col] = dot(attended_t[...], grads[:, col]).astype(BF)
+    attended_t[at_rows(place[2], HALF), :] = attended[...].T
+    attended_t[at_rows(1 - place[2], HALF), :] = other[...].T
+    for r in range(5):
+        rows = slice(r * 256, (r + 1) * 256)
+        oterms[rows, :] = dot(attended_t[rows, :], grads[...]).astype(BF)
 
     out_copies += assemble(
         place, (bown, bup, bdown, blow, bhigh), "x",
-        lambda ref, x, z: [
-            copies.start(oterms.at[at_rows((x % 2) * 4 + z, 80), at_rows(x // 2, 640)], ref.at[:, pl.ds(640, 640)])
-        ],
+        lambda ref, x, z: [copies.start(oterms.at[at_rows(x * 4 + z, 80)], ref.at[:, pl.ds(640, 640)])],
         scatter=True,
     )
     wait_all(out_copies)
 
 
 def norm_grad_kernel(place, gqkv, a0, a1, a2, a3, a4, b0, b1, b2, b3, b4, mine, theirs, wqkv, sems):
-    copies = Copies(sems)
-    parts = assemble(
-        place, (a0, a1, a2, a3, a4), "z",
-        lambda ref, x, z: [copies.start(ref, wqkv.at[at_rows(x * 4 + z, 80), pl.ds(0, 1280)])],
-    )
-    parts += assemble(
-        place, (b0, b1, b2, b3, b4), "x",
-        lambda ref, x, z: [
-            copies.start(ref.at[:, pl.ds(0, 640)], wqkv.at[at_rows(x * 4 + z, 80), pl.ds(1280, 640)])
-        ],
-    )
-    wait_all(parts)
+    from_a, from_b = take_weights(Copies(sems), place, (a0, a1, a2, a3, a4, b0, b1, b2, b3, b4), wqkv)
+    wait_all(from_a + from_b)
     for t in range(5):
         col = slice(t * 256, (t + 1) * 256)
         part = dot_nt(gqkv[...], wqkv[col, :])
@@ -384,7 +373,7 @@
         theirs[:, col] = part[ROWS:].astype(BF)
 
 
-def finish_kernel(mine, theirs, ordered, gain, grads, order_t, out):
+def finish_kernel(place, mine, theirs, ordered, gain, grads, other, order_t, out):
     rows = lax.broadcasted_iota(jnp.int32, (ROWS, ROWS), 0)
     back = (order_t[...] == rows).astype(BF)
     rowsw = ordered[...].astype(F32)
@@ -393,14 +382,18 @@
     normed = (mine[...] + theirs[...].astype(F32)).astype(BF).astype(F32)
     u = normed * gain[...]
     layer = (u - scaled * jnp.mean(u * scaled, axis=1, keepdims=True)) * spread
-    window = (grads[...].astype(F32) + layer).astype(BF)
-    out[...] = dot(back, window).astype(BF)
+    here, there = grads[:ROWS, :].astype(F32), other[...].astype(F32)
+    first = place[2] == 0
+    window = (jnp.where(first, here, there) + layer[:, :HALF]).astype(BF)
+    out[:, :HALF] = dot(back, window).astype(BF)
+    window = (jnp.where(first, there, here) + layer[:, HALF:]).astype(BF)
+    out[:, HALF:] = dot(back, window).astype(BF)
 
 
 def body(patches, ln_gain, qkv_weight, out_weight, image_counts, window_order, owner_map, owner_grads):
     index = lax.axis_index("enc")
     x, z, core = index // 8, (index // 2) % 4, index % 2
-    place = jnp.stack([x, z])
+    place = jnp.stack([x, z, core])
     gain = ln_gain.reshape(1, D)
     order = window_order.reshape(ROWS, 1)
     order_t = window_order.reshape(1, ROWS)
@@ -409,96 +402,105 @@
     with jax.named_scope("weights"):
 
         def columns(half):
-            return jnp.concatenate([qkv_weight[:, (2 * t + half) * HALF :][:, :HALF] for t in range(3)], axis=1)
+            start = half * HALF
+            parts = [qkv_weight[:, t * D + start :][:, :HALF] for t in range(3)]
+            return jnp.concatenate(parts + [out_weight[:, start : start + HALF]], axis=1)
 
         low, high = columns(0), columns(1)
         got = to_sibling(jnp.where(first_core, high, low))
         keep = jnp.where(first_core, low, high)
-        out_low, out_high = out_weight[:, :HALF], out_weight[:, HALF:]
-        out_same = to_halves(jnp.where(first_core, out_low, out_high), True)
-        out_other = to_halves(jnp.where(first_core, out_high, out_low), False)
-    with jax.named_scope("weights"):
         shard = jnp.where(first_core, jnp.concatenate([keep, got]), jnp.concatenate([got, keep]))
-        out_shard = jnp.where(
-            x < 2, jnp.concatenate([out_same, out_other]), jnp.concatenate([out_other, out_same])
-        )
         line_a = gather_line(shard[:, : 2 * HALF], "z")
-        line_b = gather_line(jnp.concatenate([shard[:, 2 * HALF :], out_shard], axis=1), "x")
+        line_b = gather_line(shard[:, 2 * HALF :], "x")
         part_a = gather_rest(line_a, "x")
         part_b = gather_rest(line_b, "z")
     with jax.named_scope("prepare"):
-        naug, gather, ordered = call(
+        naug, extra, ordered = call(
             prepare_kernel,
-            [((ROWS, D + 128), BF), ((ROWS, 512), BF), ((ROWS, D), BF)],
-            (image_counts, patches, gain, order, owner_map),
-            "svvvv",
-        )
-        nsib = to_sibling(naug)
+            [((ROWS, D + 128), BF), ((ROWS, SLOTS + HALF), BF), ((ROWS, D), BF)],
+            (place, image_counts, patches, gain, order, owner_map),
+            "ssvvvv",
+        )
+        nsib, sib_extra = to_sibling(naug), to_sibling(extra)
         (normed_t,) = call(turn_kernel, [((D, 512), BF)], (naug, nsib), "vv")
-
     with jax.named_scope("grads_in"):
-        owner_grads, part_a, part_b, normed_t = lax.optimization_barrier((owner_grads, part_a, part_b, normed_t))
-        returned = lax.all_to_all(owner_grads, ("grp", "enc"), split_axis=0, concat_axis=0, tiled=True)
+        sent = owner_grads.reshape(64, 8, 2, HALF).transpose(0, 2, 1, 3).reshape(SLOTS, HALF)
+        sent, part_a, part_b, normed_t, sib_extra = lax.optimization_barrier((sent, part_a, part_b, normed_t, sib_extra))
+        returned = lax.all_to_all(sent, ("grp", "enc"), split_axis=0, concat_axis=0, tiled=True)
     with jax.named_scope("forward"):
-        probs, qkv, attended, mine, theirs = call(
+        probs, qkv, attended = call(
             forward_kernel,
-            [((4, HPC, WIN, WIN), F32), ((512, 3 * HALF), BF), ((512, HALF), BF), ((ROWS, D), F32), ((ROWS, D), BF)],
+            [((4, HPC, WIN, WIN), F32), ((512, 3 * HALF), BF), ((512, HALF), BF)],
             (place, naug, nsib, *part_a, *part_b),
             "svv" + "a" * 10,
-            "aavvv",
+            "aav",
             scratch=[
                 pltpu.VMEM((D, 3 * HALF), BF),
-                pltpu.VMEM((HALF, D), BF),
                 pltpu.VMEM((512, D), BF),
                 pltpu.VMEM((HPC, WIN, WIN), F32),
                 pltpu.VMEM((4, HPC, WIN, WIN), F32),
                 pltpu.VMEM((512, 3 * HALF), BF),
-                pltpu.SemaphoreType.DMA((50,)),
+                pltpu.SemaphoreType.DMA((34,)),
             ],
-            us=14,
-        )
-        from_sib = to_sibling(theirs)
-        (outgoing,) = call(embed_kernel, [((512, D), BF)], (mine, from_sib, ordered, gather), "vvvv")
+            us=12,
+        )
+        other = to_sibling(attended)
+        (outgoing,) = call(
+            embed_kernel,
+            [((SLOTS, HALF), BF)],
+            (place, attended, other, ordered, extra, sib_extra, *part_b),
+            "svvvvv" + "a" * 5,
+            scratch=[pltpu.VMEM((D, HALF), BF), pltpu.SemaphoreType.DMA((16,))],
+        )
     with jax.named_scope("grads_in"):
-        returned, _ = lax.optimization_barrier((returned, outgoing))
-        (gown,) = call(pick_kernel, [((ROWS, D), BF)], (gather, returned), "vv")
-        gsib = to_sibling(gown)
+        returned, outgoing = lax.optimization_barrier((returned, outgoing))
+        grads, ga_mine, ga_theirs = call(
+            pick_kernel,
+            [((512, HALF), BF), ((512, HALF), F32), ((512, HALF), BF)],
+            (place, returned, extra, sib_extra, *part_b),
+            "svvv" + "a" * 5,
+            scratch=[pltpu.VMEM((D, HALF), BF), pltpu.SemaphoreType.DMA((16,))],
+        )
+        ga_other = to_sibling(ga_theirs)
     with jax.named_scope("backward"):
-        gown, gsib, outgoing = lax.optimization_barrier((gown, gsib, outgoing.reshape(128, 4, D)))
+        ga_mine, ga_other, outgoing = lax.optimization_barrier((ga_mine, ga_other, outgoing))
         pieces = [((4, 80, D), BF)] * 3 + [((2, 80, D), BF)] * 2
         gqkv, *terms = call(
             backward_kernel,
             [((512, 3 * HALF), BF)] + pieces + pieces,
-            (place, gown, gsib, *part_b, normed_t, probs, qkv, attended),
-            "s" + "a" * 11,
+            (place, grads, ga_mine, ga_other, normed_t, probs, qkv, attended, other),
+            "s" + "a" * 8,
             "a" * 11,
             scratch=[
-                pltpu.VMEM((HALF, D), BF),
-                pltpu.VMEM((512, D), BF),
+                pltpu.VMEM((512, HALF), BF),
+                pltpu.VMEM((512, HALF), BF),
+                pltpu.VMEM((512, HALF), F32),
                 pltpu.VMEM((512, HALF), BF),
                 pltpu.VMEM((D, 3 * HALF), BF),
-                pltpu.VMEM((HALF, D), BF),
+                pltpu.VMEM((D, HALF), BF),
                 pltpu.VMEM((HPC, WIN, WIN), F32),
                 pltpu.VMEM((HPC, WIN, WIN), BF),
                 pltpu.VMEM((D, 512), BF),
                 pltpu.VMEM((512, HALF), BF),
-                pltpu.VMEM((HALF, 512), BF),
+                pltpu.VMEM((512, HALF), BF),
+                pltpu.VMEM((D, 512), BF),
                 pltpu.VMEM((4, HPC, WIN, WIN), F32),
                 pltpu.VMEM((512, 3 * HALF), BF),
                 pltpu.VMEM((512, 3 * HALF), BF),
-                pltpu.SemaphoreType.DMA((72,)),
+                pltpu.SemaphoreType.DMA((60,)),
             ],
             us=21,
         )
     with jax.named_scope("rows_out"):
         owner_rows = lax.all_to_all(outgoing, ("grp", "enc"), split_axis=0, concat_axis=0, tiled=True)
-        owner_rows = owner_rows.reshape(512, D)
         owner_rows, terms = lax.optimization_barrier((owner_rows, terms))
+        owner_rows = owner_rows.reshape(64, 2, 8, HALF).transpose(0, 2, 1, 3).reshape(512, D)
     with jax.named_scope("weight_grads"):
         up_a, down_a = scatter_first(*terms[1:3], "x")
         up_b, down_b = scatter_first(*terms[6:8], "z")
     with jax.named_scope("norm_grad"):
-        gqkv, up_a, down_a = lax.optimization_barrier((gqkv, up_a, down_a))
+        tick = hop(terms[1][0, :16, :128], "y", 1)
+        gqkv, tick = lax.optimization_barrier((gqkv, tick))
         nmine, ntheirs = call(
             norm_grad_kernel,
             [((ROWS, D), F32), ((ROWS, D), BF)],
@@ -508,27 +510,26 @@
             us=8,
         )
     with jax.named_scope("weight_grads"):
+        up_a, down_a, up_b, down_b, ntheirs = lax.optimization_barrier((up_a, down_a, up_b, down_b, ntheirs))
         sum_a = scatter_second(terms[0], up_a, down_a, *terms[3:5], "x", "z")
         sum_b = scatter_second(terms[5], up_b, down_b, *terms[8:], "z", "x")
     with jax.named_scope("norm_grad"):
         nfrom = to_sibling(ntheirs)
+        grads_other = to_sibling(grads[ROWS:])
         (patch_grads,) = call(
-            finish_kernel, [((ROWS, D), BF)], (nmine, nfrom, ordered, gain, gown, order_t), "vvvvvv"
+            finish_kernel,
+            [((ROWS, D), BF)],
+            (place, nmine, nfrom, ordered, gain, grads, grads_other, order_t),
+            "svvvvvvv",
         )
     with jax.named_scope("back_to_rows"):
-        mine = jnp.concatenate([sum_a, sum_b[:, :HALF]], axis=1).astype(BF)
+        mine = jnp.concatenate([sum_a, sum_b], axis=1).astype(BF)
         low, high = mine[:40], mine[40:]
         got = to_sibling(jnp.where(first_core, high, low))
         keep = jnp.where(first_core, low, high)
-        out_terms = sum_b[:, HALF:].astype(BF)
-        low, high = out_terms[:40], out_terms[40:]
-        out_same = to_halves(jnp.where(x < 2, low, high), True, back=True)
-        out_other = to_halves(jnp.where(x < 2, high, low), False, back=True)
         low, high = jnp.where(first_core, keep, got), jnp.where(first_core, got, keep)
-        out_low, out_high = jnp.where(first_core, out_same, out_other), jnp.where(first_core, out_other, out_same)
         blocks = jnp.stack(
-            [jnp.concatenate([low[:, t * HALF : (t + 1) * HALF], high[:, t * HALF : (t + 1) * HALF]], axis=1) for t in range(3)]
-            + [jnp.concatenate([out_low, out_high], axis=1)]
+            [jnp.concatenate([low[:, t * HALF : (t + 1) * HALF], high[:, t * HALF : (t + 1) * HALF]], axis=1) for t in range(4)]
         )
     with jax.named_scope("over_groups"):
         me = lax.axis_index("grp")

time: 224 us -> 213 us (0.951)
  waiting for transfers between devices: 64.6 us -> 56.4 us
  starting transfers between devices: 80.1 us -> 75.4 us
  Pallas kernels: 59.8 us -> 63.8 us
    ppermute x28, waiting for transfers between devices: 51.1 us -> 41.1 us  [hop(): return lax.ppermute(value, 'enc', ring(axis, step))]
    ppermute x4 -> x0, starting transfers between devices: 5.71 us -> none  [to_halves(): return lax.ppermute(value, 'enc', pairs)]
    pallas_call x8, Pallas kernels: 59.8 us -> 63.8 us  [call(): pl.pallas_call(kernel, out_shape=[jax.ShapeDtypeStruct(s, t) for s, t in...]
    unnamed x45 -> x50, local copies, waits for them, and re-layouts: 3.51 us -> 7.11 us
    ppermute x6 -> x8, waiting for transfers between devices: 3.39 us -> 6.86 us  [to_sibling(): return lax.ppermute(value, 'enc', [(i, i ^ 1) for i in range(32)])]
    all_to_all x2 -> x0, local copies, waits for them, and re-layouts: 2.46 us -> none  [body(): lax.all_to_all(owner_grads, ('grp', 'enc'), split_axis=0, concat_axis=0,...]
    reshape x2 -> x0, local copies, waits for them, and re-layouts: 2.42 us -> none  [the longest x1 1.22 us: body(): outgoing.reshape(128, 4, D)]
  transfers between devices with their start and end apart: 46 -> 44, of which waited for: 26 -> 23; matrix products, arithmetic and copies ran while one was open for 4% -> 3% of each run, Pallas kernels for 26% -> 27%
where the time goes in v2:
time: 213 us; the launch traced here: 212 us
  starting transfers between devices  75.4 us (35%)
  Pallas kernels  63.8 us (30%)
  waiting for transfers between devices  56.4 us (26%)
  local copies, waits for them, and re-layouts  10.9 us (5%)
  other arithmetic  4.14 us (2%)
    pallas_call x8, Pallas kernels, call(): pl.pallas_call(kernel, out_shape=[jax.ShapeDtypeStruct(s, t) for s, t in...  63.8 us
    ppermute x28, starting transfers between devices, hop(): return lax.ppermute(value, 'enc', ring(axis, step))  47.6 us
    ppermute x28, waiting for transfers between devices, hop(): return lax.ppermute(value, 'enc', ring(axis, step))  41.1 us
    all_to_all x1, starting transfers between devices, body(): lax.all_to_all(outgoing, ('grp', 'enc'), split_axis=0, concat_axis=0, til...  9.77 us
    ppermute x6, starting transfers between devices, hop(): return lax.ppermute(value, 'grp', [(i, (i + step) % 4) for i in range(4)])  9.7 us
    unnamed x50, local copies, waits for them, and re-layouts  7.11 us
    all_to_all x1, starting transfers between devices, body(): lax.all_to_all(sent, ('grp', 'enc'), split_axis=0, concat_axis=0, tiled=T...  7.1 us
    ppermute x8, waiting for transfers between devices, to_sibling(): return lax.ppermute(value, 'enc', [(i, i ^ 1) for i in range(32)])  6.86 us
  transfers between devices with their start and end apart: 44, of which 23 were waited for; matrix products, arithmetic and copies ran while one was open for 3% of the time, Pallas kernels for 27%

profile of v2, /device:TPU:0, one launch (start us, length us, event | category | flops | bytes accessed | tf_op | source)
XLA Modules:
  0.0 211.9 jit_solution(11823160076866970243)
XLA Ops:
  1.8 1.4 collective-permute-done
  3.5 4.0 %collective-permute-start.3 = (bf16[80,1280]{1,0:T(8,128)(2,1)S(1)}, bf16[80,1280]{1,0:T(8,128)(2,1)S(1)}, u32[]{:S(2)}, u32[]{:S(2)}) collective-permute-start(bf16[80,1280]{1,0:T(8,128)(2,1)S(1)} %get-tuple-element.136), channel_id=1, source_target_pairs={{0,4},{1,5},{2,6},{3,7},{4,0},{5,1},{6,2},{7,3},{8,12},{9,13},{10,... | collective-permute-start | bytes 614408 | tf_op jit(solution)/shard_map/weights/ppermute | solution.py:38
  8.5 2.2 %collective-permute-start.1 = (bf16[80,1280]{1,0:T(8,128)(2,1)S(1)}, bf16[80,1280]{1,0:T(8,128)(2,1)S(1)}, u32[]{:S(2)}, u32[]{:S(2)}) collective-permute-start(bf16[80,1280]{1,0:T(8,128)(2,1)S(1)} %get-tuple-element.136), channel_id=1, source_target_pairs={{0,6},{1,7},{2,0},{3,1},{4,2},{5,3},{6,4},{7,5},{8,14},{9,15},{10,... | collective-permute-start | bytes 614408 | tf_op jit(solution)/shard_map/weights/ppermute | solution.py:38
  10.7 3.0 %collective-permute-start.10 = (bf16[80,1280]{1,0:T(8,128)(2,1)S(1)}, bf16[80,1280]{1,0:T(8,128)(2,1)S(1)}, u32[]{:S(2)}, u32[]{:S(2)}) collective-permute-start(bf16[80,1280]{1,0:T(8,128)(2,1)S(1)} %get-tuple-element.135), channel_id=1, source_target_pairs={{0,16},{1,17},{2,18},{3,19},{4,20},{5,21},{6,22},{7,23},{8,24},{9,... | collective-permute-start | bytes 614408 | tf_op jit(solution)/shard_map/weights/ppermute | solution.py:38
  14.4 2.6 %collective-permute-start.8 = (bf16[80,1280]{1,0:T(8,128)(2,1)S(1)}, bf16[80,1280]{1,0:T(8,128)(2,1)S(1)}, u32[]{:S(2)}, u32[]{:S(2)}) collective-permute-start(bf16[80,1280]{1,0:T(8,128)(2,1)S(1)} %get-tuple-element.135), channel_id=1, source_target_pairs={{0,24},{1,25},{2,26},{3,27},{4,28},{5,29},{6,30},{7,31},{8,0},{9,1... | collective-permute-start | bytes 614408 | tf_op jit(solution)/shard_map/weights/ppermute | solution.py:38
  18.1 1.6 collective-permute-start.5
  22.5 1.7 collective-permute-start.4
  24.4 2.7 %collective-permute-start.11 = (bf16[4,80,1280]{2,1,0:T(8,128)(2,1)S(1)}, bf16[4,80,1280]{2,1,0:T(8,128)(2,1)S(1)}, u32[]{:S(2)}, u32[]{:S(2)}) collective-permute-start(bf16[4,80,1280]{2,1,0:T(8,128)(2,1)S(1)} %pad_maximum_fusion.1.b0), channel_id=1, source_target_pairs={{0,6},{1,7},{2,0},{3,1},{4,2},{5,3},{6,4},{7,5},{8,14},{9,15},{10,... | collective-permute-start | bytes 2457608 | tf_op jit(solution)/shard_map/weights/ppermute | solution.py:38
  27.1 3.5 %prepare.2 = (bf16[256,1408]{1,0:T(8,128)(2,1)}, bf16[256,1664]{1,0:T(8,128)(2,1)}, bf16[256,1280]{1,0:T(8,128)(2,1)}) custom-call(s32[3]{0:T(128)} %pad_add_fusion.place, s32[1,4]{1,0:T(1,128)} %counts.1, bf16[256,1280]{1,0:T(8,128)(2,1)} %patches.1, f32[1,1280]{1,0:T(1,128)} %reshape.37.gain, s32[256,1]{1,0:T(8,128)} %copy.13.order, s32[256,1]{1,0:T(8,128)} %copy.14.owners), custom_call_target="tpu_custom_call" | custom-call | flops 3000000000 | bytes 9000000 | tf_op jit(solution)/shard_map/prepare/pallas_call | solution.py:97
  30.7 9.9 %collective-permute-done.5.a2 = bf16[4,80,1280]{2,1,0:T(8,128)(2,1)} collective-permute-done((bf16[4,80,1280]{2,1,0:T(8,128)(2,1)S(1)}, bf16[4,80,1280]{2,1,0:T(8,128)(2,1)}, u32[]{:S(2)}, u32[]{:S(2)}) %collective-permute-start.5) | collective-permute-done | bytes 819232 | tf_op jit(solution)/shard_map/weights/ppermute | solution.py:38
  41.7 1.6 collective-permute-start.6
  43.3 4.4 %collective-permute-done.12.b2 = bf16[4,80,1280]{2,1,0:T(8,128)(2,1)S(1)} collective-permute-done((bf16[4,80,1280]{2,1,0:T(8,128)(2,1)S(1)}, bf16[4,80,1280]{2,1,0:T(8,128)(2,1)S(1)}, u32[]{:S(2)}, u32[]{:S(2)}) %collective-permute-start.12) | collective-permute-done | bytes 819232 | tf_op jit(solution)/shard_map/weights/ppermute | solution.py:38
  47.7 1.5 collective-permute-start.7
  49.4 3.3 %collective-permute-start.14 = (bf16[2,80,1280]{2,1,0:T(8,128)(2,1)S(1)}, bf16[2,80,1280]{2,1,0:T(8,128)(2,1)S(1)}, u32[]{:S(2)}, u32[]{:S(2)}) collective-permute-start(bf16[2,80,1280]{2,1,0:T(8,128)(2,1)S(1)} %slice.200), channel_id=1, source_target_pairs={{0,6},{1,7},{2,0},{3,1},{4,2},{5,3},{6,4},{7,5},{8,14},{9,15},{10,... | collective-permute-start | bytes 1228808 | tf_op jit(solution)/shard_map/weights/ppermute | solution.py:38
  52.7 2.8 %prepare.3.normed_hbm = bf16[1280,512]{1,0:T(8,128)(2,1)} custom-call(bf16[256,1408]{1,0:T(8,128)(2,1)} %get-tuple-element.60.own, bf16[256,1408]{1,0:T(8,128)(2,1)} %collective-permute-done.15.sib), custom_call_target="tpu_custom_call" | custom-call | flops 3000000000 | bytes 9000000 | tf_op jit(solution)/shard_map/prepare/pallas_call | solution.py:97
  55.5 1.7 collective-permute-done.7.a4
  57.3 2.6 %collective-permute-done.13.b3 = bf16[2,80,1280]{2,1,0:T(8,128)(2,1)S(1)} collective-permute-done((bf16[2,80,1280]{2,1,0:T(8,128)(2,1)S(1)}, bf16[2,80,1280]{2,1,0:T(8,128)(2,1)S(1)}, u32[]{:S(2)}, u32[]{:S(2)}) %collective-permute-start.13) | collective-permute-done | bytes 409632 | tf_op jit(solution)/shard_map/weights/ppermute | solution.py:38
  61.5 7.1 %all-to-all-start = ((bf16[128,8,640]{2,1,0:T(8,128)(2,1)}), bf16[128,8,640]{2,1,0:T(8,128)(2,1)S(1)}, u32[]{:S(2)}, u32[]{:S(2)}) async-start(bf16[128,8,640]{2,1,0:T(8,128)(2,1)} %bitcast.15), calls=%async_computation | async-start | bytes 2621440 | tf_op jit(solution)/shard_map/grads_in/all_to_all | solution.py:429
  68.6 12.3 %forward.2 = (f32[4,8,128,128]{3,2,1,0:T(8,128)}, bf16[512,1920]{1,0:T(8,128)(2,1)}, bf16[512,640]{1,0:T(8,128)(2,1)}) custom-call(s32[3]{0:T(128)} %pad_add_fusion.place, bf16[256,1408]{1,0:T(8,128)(2,1)} %get-tuple-element.60.own, bf16[256,1408]{1,0:T(8,128)(2,1)} %collective-permute-done.15.sib, bf16[4,80,1280]{2,1,0:T(8,128)(2,1)} %copy-done.3, ...), custom_call_target="tpu_custom_call" | custom-call | flops 12000000000 | bytes 36000000 | tf_op jit(solution)/shard_map/forward/pallas_call | solution.py:97
  81.2 2.3 %collective-permute-done.17.other.other_hbm = bf16[512,640]{1,0:T(8,128)(2,1)S(1)} collective-permute-done((bf16[512,640]{1,0:T(8,128)(2,1)}, bf16[512,640]{1,0:T(8,128)(2,1)S(1)}, u32[]{:S(2)}, u32[]{:S(2)}) %collective-permute-start.17) | collective-permute-done | bytes 655392 | tf_op jit(solution)/shard_map/forward/ppermute | solution.py:42
  84.3 7.0 %forward.3 = bf16[1024,640]{1,0:T(8,128)(2,1)} custom-call(s32[3]{0:T(128)} %pad_add_fusion.place, bf16[512,640]{1,0:T(8,128)(2,1)} %get-tuple-element.73.attended.attended_hbm, bf16[512,640]{1,0:T(8,128)(2,1)} %copy-done.17, bf16[256,1280]{1,0:T(8,128)(2,1)} %get-tuple-element.74.ordered, bf16[256,1664]{1,0:T(8,128)(2,1)} %get-tuple-element.61.extra, ...), custom_call_target="tpu_custom_call" | custom-call | flops 3000000000 | bytes 9000000 | tf_op jit(solution)/shard_map/forward/pallas_call | solution.py:97
  91.3 1.1 copy-done
  92.4 5.7 %grads_in.1 = (bf16[512,640]{1,0:T(8,128)(2,1)}, f32[512,640]{1,0:T(8,128)}, bf16[512,640]{1,0:T(8,128)(2,1)}) custom-call(s32[3]{0:T(128)} %pad_add_fusion.place, bf16[1024,640]{1,0:T(8,128)(2,1)} %bitcast.79, bf16[256,1664]{1,0:T(8,128)(2,1)} %get-tuple-element.61.extra, bf16[256,1664]{1,0:T(8,128)(2,1)} %copy-done.16, bf16[4,80,1280]{2,1,0:T(8,128)(2,1)} %copy-done.4, ...), custom_call_target="tpu_custom_call" | custom-call | flops 3000000000 | bytes 9000000 | tf_op jit(solution)/shard_map/grads_in/pallas_call | solution.py:97
  98.3 2.2 %collective-permute-done.18.ga_other = bf16[512,640]{1,0:T(8,128)(2,1)S(1)} collective-permute-done((bf16[512,640]{1,0:T(8,128)(2,1)}, bf16[512,640]{1,0:T(8,128)(2,1)S(1)}, u32[]{:S(2)}, u32[]{:S(2)}) %collective-permute-start.18) | collective-permute-done | bytes 655392 | tf_op jit(solution)/shard_map/grads_in/ppermute | solution.py:42
  101.4 9.8 %all-to-all-start.1 = ((bf16[128,8,640]{2,1,0:T(8,128)(2,1)}), bf16[128,8,640]{2,1,0:T(8,128)(2,1)S(1)}, u32[]{:S(2)}, u32[]{:S(2)}) async-start(bf16[128,8,640]{2,1,0:T(8,128)(2,1)} %bitcast.17), calls=%async_computation.1 | async-start | bytes 2621440 | tf_op jit(solution)/shard_map/rows_out/all_to_all | solution.py:495
  111.2 20.1 %backward.1 = (bf16[512,1920]{1,0:T(8,128)(2,1)}, bf16[4,80,1280]{2,1,0:T(8,128)(2,1)}, bf16[4,80,1280]{2,1,0:T(8,128)(2,1)}, bf16[4,80,1280]{2,1,0:T(8,128)(2,1...) custom-call(s32[3]{0:T(128)} %pad_add_fusion.place, ...), custom_call_target="tpu_custom_call" | custom-call | flops 20999999488 | bytes 63000000 | tf_op jit(solution)/shard_map/backward/pallas_call | solution.py:97
  131.3 1.9 all-to-all-done.1
  134.0 2.5 %collective-permute-start.20 = (bf16[4,80,1280]{2,1,0:T(8,128)(2,1)}, bf16[4,80,1280]{2,1,0:T(8,128)(2,1)S(1)}, u32[]{:S(2)}, u32[]{:S(2)}) collective-permute-start(bf16[4,80,1280]{2,1,0:T(8,128)(2,1)} %get-tuple-element.101), channel_id=1, source_target_pairs={{0,24},{1,25},{2,26},{3,27},{4,28},{5,29},{6,30},{7,31},{8,0},{9,1... | collective-permute-start | bytes 2457608 | tf_op jit(solution)/shard_map/weight_grads/ppermute | solution.py:38
  136.8 2.9 %collective-permute-start.22 = (bf16[4,80,1280]{2,1,0:T(8,128)(2,1)}, bf16[4,80,1280]{2,1,0:T(8,128)(2,1)S(1)}, u32[]{:S(2)}, u32[]{:S(2)}) collective-permute-start(bf16[4,80,1280]{2,1,0:T(8,128)(2,1)} %get-tuple-element.103), channel_id=1, source_target_pairs={{0,6},{1,7},{2,0},{3,1},{4,2},{5,3},{6,4},{7,5},{8,14},{9,15},{10,... | collective-permute-start | bytes 2457608 | tf_op jit(solution)/shard_map/weight_grads/ppermute | solution.py:38
  139.7 8.5 %norm_grad.2 = (f32[256,1280]{1,0:T(8,128)}, bf16[256,1280]{1,0:T(8,128)(2,1)}) custom-call(s32[3]{0:T(128)} %pad_add_fusion.place, bf16[512,1920]{1,0:T(8,128)(2,1)} %get-tuple-element.98.gqkv, bf16[4,80,1280]{2,1,0:T(8,128)(2,1)} %copy-done.3, bf16[4,80,1280]{2,1,0:T(8,128)(2,1)} %copy-done.9, bf16[4,80,1280]{2,1,0:T(8,128)(2,1)} %collective-permute-done.5.a2, ...), custom_call_target="tpu_custom_call" | custom-call | flops 8000000000 | bytes 24000000 | tf_op jit(solution)/shard_map/norm_grad/pallas_call | solution.py:97
  148.2 5.9 %collective-permute-done.19 = bf16[4,80,1280]{2,1,0:T(8,128)(2,1)S(1)} collective-permute-done((bf16[4,80,1280]{2,1,0:T(8,128)(2,1)}, bf16[4,80,1280]{2,1,0:T(8,128)(2,1)S(1)}, u32[]{:S(2)}, u32[]{:S(2)}) %collective-permute-start.19) | collective-permute-done | bytes 819232 | tf_op jit(solution)/shard_map/weight_grads/ppermute | solution.py:38
  154.1 2.7 %collective-permute-done.21 = bf16[4,80,1280]{2,1,0:T(8,128)(2,1)S(1)} collective-permute-done((bf16[4,80,1280]{2,1,0:T(8,128)(2,1)}, bf16[4,80,1280]{2,1,0:T(8,128)(2,1)S(1)}, u32[]{:S(2)}, u32[]{:S(2)}) %collective-permute-start.21) | collective-permute-done | bytes 819232 | tf_op jit(solution)/shard_map/weight_grads/ppermute | solution.py:38
  156.9 3.0 %collective-permute-start.32 = (bf16[2,80,1280]{2,1,0:T(8,128)(2,1)S(1)}, bf16[2,80,1280]{2,1,0:T(8,128)(2,1)S(1)}, u32[]{:S(2)}, u32[]{:S(2)}) collective-permute-start(bf16[2,80,1280]{2,1,0:T(8,128)(2,1)S(1)} %add_convert_fusion.1), channel_id=1, source_target_pairs={{0,6},{1,7},{2,0},{3,1},{4,2},{5,3},{6,4},{7,5},{8,14},{9,15},{10,... | collective-permute-start | bytes 1228808 | tf_op jit(solution)/shard_map/weight_grads/ppermute | solution.py:38
  160.8 1.7 collective-permute-start.25
  162.5 3.8 %collective-permute-done.32 = bf16[2,80,1280]{2,1,0:T(8,128)(2,1)S(1)} collective-permute-done((bf16[2,80,1280]{2,1,0:T(8,128)(2,1)S(1)}, bf16[2,80,1280]{2,1,0:T(8,128)(2,1)S(1)}, u32[]{:S(2)}, u32[]{:S(2)}) %collective-permute-start.32) | collective-permute-done | bytes 409632 | tf_op jit(solution)/shard_map/weight_grads/ppermute | solution.py:38
  166.3 3.6 %collective-permute-done.30 = bf16[2,80,1280]{2,1,0:T(8,128)(2,1)S(1)} collective-permute-done((bf16[2,80,1280]{2,1,0:T(8,128)(2,1)S(1)}, bf16[2,80,1280]{2,1,0:T(8,128)(2,1)S(1)}, u32[]{:S(2)}, u32[]{:S(2)}) %collective-permute-start.30) | collective-permute-done | bytes 409632 | tf_op jit(solution)/shard_map/weight_grads/ppermute | solution.py:38
  170.3 1.9 collective-permute-start.34
  172.7 1.6 collective-permute-start.31
  174.7 3.6 %collective-permute-start.29 = (bf16[80,1280]{1,0:T(8,128)(2,1)S(1)}, bf16[80,1280]{1,0:T(8,128)(2,1)S(1)}, u32[]{:S(2)}, u32[]{:S(2)}) collective-permute-start(bf16[80,1280]{1,0:T(8,128)(2,1)S(1)} %get-tuple-element.130), channel_id=1, source_target_pairs={{0,4},{1,5},{2,6},{3,7},{4,0},{5,1},{6,2},{7,3},{8,12},{9,13},{10,... | collective-permute-start | bytes 614408 | tf_op jit(solution)/shard_map/weight_grads/ppermute | solution.py:38
  179.0 1.4 collective-permute-start.26
  180.6 1.6 collective-permute-done.29
  182.1 3.6 %collective-permute-done.28 = bf16[80,1280]{1,0:T(8,128)(2,1)S(1)} collective-permute-done((bf16[80,1280]{1,0:T(8,128)(2,1)S(1)}, bf16[80,1280]{1,0:T(8,128)(2,1)S(1)}, u32[]{:S(2)}, u32[]{:S(2)}) %collective-permute-start.28) | collective-permute-done | bytes 204832 | tf_op jit(solution)/shard_map/weight_grads/ppermute | solution.py:38
  188.1 4.4 %collective-permute-start.38 = (bf16[40,1280]{1,0:T(8,128)(2,1)S(1)}, bf16[40,1280]{1,0:T(8,128)(2,1)S(1)}, u32[]{:S(2)}, u32[]{:S(2)}) collective-permute-start(bf16[40,1280]{1,0:T(8,128)(2,1)S(1)} %get-tuple-element.127), channel_id=1, source_target_pairs={{0,64},{32,96},{64,0},{96,32},{1,65},{33,97},{65,1},{97,33},{2,66}... | collective-permute-start | bytes 307208 | tf_op jit(solution)/shard_map/over_groups/ppermute | solution.py:37
  192.5 2.5 %collective-permute-start.37 = (bf16[40,1280]{1,0:T(8,128)(2,1)S(1)}, bf16[40,1280]{1,0:T(8,128)(2,1)S(1)}, u32[]{:S(2)}, u32[]{:S(2)}) collective-permute-start(bf16[40,1280]{1,0:T(8,128)(2,1)S(1)} %get-tuple-element.128), channel_id=1, source_target_pairs={{0,96},{32,0},{64,32},{96,64},{1,97},{33,1},{65,33},{97,65},{2,98}... | collective-permute-start | bytes 307208 | tf_op jit(solution)/shard_map/over_groups/ppermute | solution.py:37
  195.7 3.2 %collective-permute-done.37 = bf16[40,1280]{1,0:T(8,128)(2,1)S(1)} collective-permute-done((bf16[40,1280]{1,0:T(8,128)(2,1)S(1)}, bf16[40,1280]{1,0:T(8,128)(2,1)S(1)}, u32[]{:S(2)}, u32[]{:S(2)}) %collective-permute-start.37) | collective-permute-done | bytes 102432 | tf_op jit(solution)/shard_map/over_groups/ppermute | solution.py:37
  198.9 1.9 collective-permute-done.36
  201.8 1.3 collective-permute-start.40
  204.5 4.0 %norm_grad.3 = bf16[256,1280]{1,0:T(8,128)(2,1)} custom-call(s32[3]{0:T(128)} %pad_add_fusion.place, f32[256,1280]{1,0:T(8,128)} %get-tuple-element.99.mine, bf16[256,1280]{1,0:T(8,128)(2,1)} %collective-permute-done.23.theirs, bf16[256,1280]{1,0:T(8,128)(2,1)} %get-tuple-element.74.ordered, f32[1,1280]{1,0:T(1,128)} %reshape.37.gain, ...), custom_call_target="tpu_custom_call" | custom-call | flops 3000000000 | bytes 9000000 | tf_op jit(solution)/shard_map/norm_grad/pallas_call | solution.py:97
  (137 shorter events, 24.9 us)
Async XLA Ops:
  1.8 1.5 collective-permute-start
  3.4 16.9 %copy-start.13 = (f32[1280]{0:T(1024)S(1)}, f32[1280]{0:T(1024)}, u32[]{:S(2)}) copy-start(f32[1280]{0:T(1024)} %param.9) | copy-start | bytes 15364
  3.4 17.5 %copy-start.15 = (s32[2,128]{1,0:T(2,128)S(1)}, s32[2,128]{1,0:T(2,128)}, u32[]{:S(2)}) copy-start(s32[2,128]{1,0:T(2,128)} %param.13) | copy-start | bytes 3076
  3.4 18.3 %copy-start.14 = (s32[256,1]{0,1:T(1,128)S(1)}, s32[256,1]{0,1:T(1,128)}, u32[]{:S(2)}) copy-start(s32[256,1]{0,1:T(1,128)} %param.14) | copy-start | bytes 3076
  3.5 10.9 %collective-permute-start.3 = (bf16[80,1280]{1,0:T(8,128)(2,1)S(1)}, bf16[80,1280]{1,0:T(8,128)(2,1)S(1)}, u32[]{:S(2)}, u32[]{:S(2)}) collective-permute-start(bf16[80,1280]{1,0:T(8,128)(2,1)S(1)} %get-tuple-element.136), channel_id=1, source_target_pairs={{0,4},{1,5},{2,6},{3,7},{4,0},{5,1},{6,2},{7,3},{8,12},{9,13},{10,... | collective-permute-start | bytes 614408 | tf_op jit(solution)/shard_map/weights/ppermute | solution.py:38
  7.5 9.8 %collective-permute-start.2 = (bf16[80,1280]{1,0:T(8,128)(2,1)S(1)}, bf16[80,1280]{1,0:T(8,128)(2,1)S(1)}, u32[]{:S(2)}, u32[]{:S(2)}) collective-permute-start(bf16[80,1280]{1,0:T(8,128)(2,1)S(1)} %get-tuple-element.136), channel_id=1, source_target_pairs={{0,2},{1,3},{2,4},{3,5},{4,6},{5,7},{6,0},{7,1},{8,10},{9,11},{10,... | collective-permute-start | bytes 614408 | tf_op jit(solution)/shard_map/weights/ppermute | solution.py:38
  8.5 9.5 %collective-permute-start.1 = (bf16[80,1280]{1,0:T(8,128)(2,1)S(1)}, bf16[80,1280]{1,0:T(8,128)(2,1)S(1)}, u32[]{:S(2)}, u32[]{:S(2)}) collective-permute-start(bf16[80,1280]{1,0:T(8,128)(2,1)S(1)} %get-tuple-element.136), channel_id=1, source_target_pairs={{0,6},{1,7},{2,0},{3,1},{4,2},{5,3},{6,4},{7,5},{8,14},{9,15},{10,... | collective-permute-start | bytes 614408 | tf_op jit(solution)/shard_map/weights/ppermute | solution.py:38
  10.7 13.5 %collective-permute-start.10 = (bf16[80,1280]{1,0:T(8,128)(2,1)S(1)}, bf16[80,1280]{1,0:T(8,128)(2,1)S(1)}, u32[]{:S(2)}, u32[]{:S(2)}) collective-permute-start(bf16[80,1280]{1,0:T(8,128)(2,1)S(1)} %get-tuple-element.135), channel_id=1, source_target_pairs={{0,16},{1,17},{2,18},{3,19},{4,20},{5,21},{6,22},{7,23},{8,24},{9,... | collective-permute-start | bytes 614408 | tf_op jit(solution)/shard_map/weights/ppermute | solution.py:38
  13.8 10.5 %collective-permute-start.9 = (bf16[80,1280]{1,0:T(8,128)(2,1)S(1)}, bf16[80,1280]{1,0:T(8,128)(2,1)S(1)}, u32[]{:S(2)}, u32[]{:S(2)}) collective-permute-start(bf16[80,1280]{1,0:T(8,128)(2,1)S(1)} %get-tuple-element.135), channel_id=1, source_target_pairs={{0,8},{1,9},{2,10},{3,11},{4,12},{5,13},{6,14},{7,15},{8,16},{9,17... | collective-permute-start | bytes 614408 | tf_op jit(solution)/shard_map/weights/ppermute | solution.py:38
  14.4 9.9 %collective-permute-start.8 = (bf16[80,1280]{1,0:T(8,128)(2,1)S(1)}, bf16[80,1280]{1,0:T(8,128)(2,1)S(1)}, u32[]{:S(2)}, u32[]{:S(2)}) collective-permute-start(bf16[80,1280]{1,0:T(8,128)(2,1)S(1)} %get-tuple-element.135), channel_id=1, source_target_pairs={{0,24},{1,25},{2,26},{3,27},{4,28},{5,29},{6,30},{7,31},{8,0},{9,1... | collective-permute-start | bytes 614408 | tf_op jit(solution)/shard_map/weights/ppermute | solution.py:38
  18.1 22.5 %collective-permute-start.5 = (bf16[4,80,1280]{2,1,0:T(8,128)(2,1)S(1)}, bf16[4,80,1280]{2,1,0:T(8,128)(2,1)}, u32[]{:S(2)}, u32[]{:S(2)}) collective-permute-start(bf16[4,80,1280]{2,1,0:T(8,128)(2,1)S(1)} %pad_maximum_fusion.a0), channel_id=1, source_target_pairs={{0,8},{1,9},{2,10},{3,11},{4,12},{5,13},{6,14},{7,15},{8,16},{9,17... | collective-permute-start | bytes 2457608 | tf_op jit(solution)/shard_map/weights/ppermute | solution.py:38
  22.5 19.2 %collective-permute-start.4 = (bf16[4,80,1280]{2,1,0:T(8,128)(2,1)S(1)}, bf16[4,80,1280]{2,1,0:T(8,128)(2,1)S(1)}, u32[]{:S(2)}, u32[]{:S(2)}) collective-permute-start(bf16[4,80,1280]{2,1,0:T(8,128)(2,1)S(1)} %pad_maximum_fusion.a0), channel_id=1, source_target_pairs={{0,24},{1,25},{2,26},{3,27},{4,28},{5,29},{6,30},{7,31},{8,0},{9,1... | collective-permute-start | bytes 2457608 | tf_op jit(solution)/shard_map/weights/ppermute | solution.py:38
  24.4 24.9 %collective-permute-start.11 = (bf16[4,80,1280]{2,1,0:T(8,128)(2,1)S(1)}, bf16[4,80,1280]{2,1,0:T(8,128)(2,1)S(1)}, u32[]{:S(2)}, u32[]{:S(2)}) collective-permute-start(bf16[4,80,1280]{2,1,0:T(8,128)(2,1)S(1)} %pad_maximum_fusion.1.b0), channel_id=1, source_target_pairs={{0,6},{1,7},{2,0},{3,1},{4,2},{5,3},{6,4},{7,5},{8,14},{9,15},{10,... | collective-permute-start | bytes 2457608 | tf_op jit(solution)/shard_map/weights/ppermute | solution.py:38
  27.1 20.5 %collective-permute-start.12 = (bf16[4,80,1280]{2,1,0:T(8,128)(2,1)S(1)}, bf16[4,80,1280]{2,1,0:T(8,128)(2,1)S(1)}, u32[]{:S(2)}, u32[]{:S(2)}) collective-permute-start(bf16[4,80,1280]{2,1,0:T(8,128)(2,1)S(1)} %pad_maximum_fusion.1.b0), channel_id=1, source_target_pairs={{0,2},{1,3},{2,4},{3,5},{4,6},{5,7},{6,0},{7,1},{8,10},{9,11},{10,... | collective-permute-start | bytes 2457608 | tf_op jit(solution)/shard_map/weights/ppermute | solution.py:38
  30.6 18.8 %collective-permute-start.15 = (bf16[256,1408]{1,0:T(8,128)(2,1)}, bf16[256,1408]{1,0:T(8,128)(2,1)}, u32[]{:S(2)}, u32[]{:S(2)}) collective-permute-start(bf16[256,1408]{1,0:T(8,128)(2,1)} %get-tuple-element.60.own), channel_id=1, source_target_pairs={{0,1},{1,0},{2,3},{3,2},{4,5},{5,4},{6,7},{7,6},{8,9},{9,8},{10,11... | collective-permute-start | bytes 2162696 | tf_op jit(solution)/shard_map/prepare/ppermute | solution.py:42
  40.6 14.9 %collective-permute-start.16 = (bf16[256,1664]{1,0:T(8,128)(2,1)}, bf16[256,1664]{1,0:T(8,128)(2,1)S(1)}, u32[]{:S(2)}, u32[]{:S(2)}) collective-permute-start(bf16[256,1664]{1,0:T(8,128)(2,1)} %get-tuple-element.61.extra), channel_id=1, source_target_pairs={{0,1},{1,0},{2,3},{3,2},{4,5},{5,4},{6,7},{7,6},{8,9},{9,8},{10,11... | collective-permute-start | bytes 2555912 | tf_op jit(solution)/shard_map/prepare/ppermute | solution.py:42
  41.7 13.8 %collective-permute-start.6 = (bf16[2,80,1280]{2,1,0:T(8,128)(2,1)S(1)}, bf16[2,80,1280]{2,1,0:T(8,128)(2,1)S(1)}, u32[]{:S(2)}, u32[]{:S(2)}) collective-permute-start(bf16[2,80,1280]{2,1,0:T(8,128)(2,1)S(1)} %slice.196), channel_id=1, source_target_pairs={{0,8},{1,9},{2,10},{3,11},{4,12},{5,13},{6,14},{7,15},{8,16},{9,17... | collective-permute-start | bytes 1228808 | tf_op jit(solution)/shard_map/weights/ppermute | solution.py:38
  47.7 9.6 %collective-permute-start.7 = (bf16[2,80,1280]{2,1,0:T(8,128)(2,1)S(1)}, bf16[2,80,1280]{2,1,0:T(8,128)(2,1)S(1)}, u32[]{:S(2)}, u32[]{:S(2)}) collective-permute-start(bf16[2,80,1280]{2,1,0:T(8,128)(2,1)S(1)} %slice.197), channel_id=1, source_target_pairs={{0,24},{1,25},{2,26},{3,27},{4,28},{5,29},{6,30},{7,31},{8,0},{9,1... | collective-permute-start | bytes 1228808 | tf_op jit(solution)/shard_map/weights/ppermute | solution.py:38
  49.3 10.6 %collective-permute-start.13 = (bf16[2,80,1280]{2,1,0:T(8,128)(2,1)S(1)}, bf16[2,80,1280]{2,1,0:T(8,128)(2,1)S(1)}, u32[]{:S(2)}, u32[]{:S(2)}) collective-permute-start(bf16[2,80,1280]{2,1,0:T(8,128)(2,1)S(1)} %slice.199), channel_id=1, source_target_pairs={{0,2},{1,3},{2,4},{3,5},{4,6},{5,7},{6,0},{7,1},{8,10},{9,11},{10,... | collective-permute-start | bytes 1228808 | tf_op jit(solution)/shard_map/weights/ppermute | solution.py:38
  49.4 10.5 %collective-permute-start.14 = (bf16[2,80,1280]{2,1,0:T(8,128)(2,1)S(1)}, bf16[2,80,1280]{2,1,0:T(8,128)(2,1)S(1)}, u32[]{:S(2)}, u32[]{:S(2)}) collective-permute-start(bf16[2,80,1280]{2,1,0:T(8,128)(2,1)S(1)} %slice.200), channel_id=1, source_target_pairs={{0,6},{1,7},{2,0},{3,1},{4,2},{5,3},{6,4},{7,5},{8,14},{9,15},{10,... | collective-permute-start | bytes 1228808 | tf_op jit(solution)/shard_map/weights/ppermute | solution.py:38
  61.5 29.8 %all-to-all-start = ((bf16[128,8,640]{2,1,0:T(8,128)(2,1)}), bf16[128,8,640]{2,1,0:T(8,128)(2,1)S(1)}, u32[]{:S(2)}, u32[]{:S(2)}) async-start(bf16[128,8,640]{2,1,0:T(8,128)(2,1)} %bitcast.15), calls=%async_computation | async-start | bytes 2621440 | tf_op jit(solution)/shard_map/grads_in/all_to_all | solution.py:429
  80.9 2.6 %collective-permute-start.17 = (bf16[512,640]{1,0:T(8,128)(2,1)}, bf16[512,640]{1,0:T(8,128)(2,1)S(1)}, u32[]{:S(2)}, u32[]{:S(2)}) collective-permute-start(bf16[512,640]{1,0:T(8,128)(2,1)} %get-tuple-element.73.attended.attended_hbm), channel_id=1, source_target_pairs={{0,1},{1,0},{2,3},{3,2},{4,5},{5,4},{6,7},{7,6},{8,9},{9,8},{10,11... | collective-permute-start | bytes 1966088 | tf_op jit(solution)/shard_map/forward/ppermute | solution.py:42
  98.1 2.4 %collective-permute-start.18 = (bf16[512,640]{1,0:T(8,128)(2,1)}, bf16[512,640]{1,0:T(8,128)(2,1)S(1)}, u32[]{:S(2)}, u32[]{:S(2)}) collective-permute-start(bf16[512,640]{1,0:T(8,128)(2,1)} %get-tuple-element.78), channel_id=1, source_target_pairs={{0,1},{1,0},{2,3},{3,2},{4,5},{5,4},{6,7},{7,6},{8,9},{9,8},{10,11... | collective-permute-start | bytes 1966088 | tf_op jit(solution)/shard_map/grads_in/ppermute | solution.py:42
  101.4 31.8 %all-to-all-start.1 = ((bf16[128,8,640]{2,1,0:T(8,128)(2,1)}), bf16[128,8,640]{2,1,0:T(8,128)(2,1)S(1)}, u32[]{:S(2)}, u32[]{:S(2)}) async-start(bf16[128,8,640]{2,1,0:T(8,128)(2,1)} %bitcast.17), calls=%async_computation.1 | async-start | bytes 2621440 | tf_op jit(solution)/shard_map/rows_out/all_to_all | solution.py:495
  133.3 20.8 %collective-permute-start.19 = (bf16[4,80,1280]{2,1,0:T(8,128)(2,1)}, bf16[4,80,1280]{2,1,0:T(8,128)(2,1)S(1)}, u32[]{:S(2)}, u32[]{:S(2)}) collective-permute-start(bf16[4,80,1280]{2,1,0:T(8,128)(2,1)} %get-tuple-element.100), channel_id=1, source_target_pairs={{0,8},{1,9},{2,10},{3,11},{4,12},{5,13},{6,14},{7,15},{8,16},{9,17... | collective-permute-start | bytes 2457608 | tf_op jit(solution)/shard_map/weight_grads/ppermute | solution.py:38
  134.0 20.2 %collective-permute-start.20 = (bf16[4,80,1280]{2,1,0:T(8,128)(2,1)}, bf16[4,80,1280]{2,1,0:T(8,128)(2,1)S(1)}, u32[]{:S(2)}, u32[]{:S(2)}) collective-permute-start(bf16[4,80,1280]{2,1,0:T(8,128)(2,1)} %get-tuple-element.101), channel_id=1, source_target_pairs={{0,24},{1,25},{2,26},{3,27},{4,28},{5,29},{6,30},{7,31},{8,0},{9,1... | collective-permute-start | bytes 2457608 | tf_op jit(solution)/shard_map/weight_grads/ppermute | solution.py:38
  136.5 20.3 %collective-permute-start.21 = (bf16[4,80,1280]{2,1,0:T(8,128)(2,1)}, bf16[4,80,1280]{2,1,0:T(8,128)(2,1)S(1)}, u32[]{:S(2)}, u32[]{:S(2)}) collective-permute-start(bf16[4,80,1280]{2,1,0:T(8,128)(2,1)} %get-tuple-element.102), channel_id=1, source_target_pairs={{0,2},{1,3},{2,4},{3,5},{4,6},{5,7},{6,0},{7,1},{8,10},{9,11},{10,... | collective-permute-start | bytes 2457608 | tf_op jit(solution)/shard_map/weight_grads/ppermute | solution.py:38
  136.8 20.0 %collective-permute-start.22 = (bf16[4,80,1280]{2,1,0:T(8,128)(2,1)}, bf16[4,80,1280]{2,1,0:T(8,128)(2,1)S(1)}, u32[]{:S(2)}, u32[]{:S(2)}) collective-permute-start(bf16[4,80,1280]{2,1,0:T(8,128)(2,1)} %get-tuple-element.103), channel_id=1, source_target_pairs={{0,6},{1,7},{2,0},{3,1},{4,2},{5,3},{6,4},{7,5},{8,14},{9,15},{10,... | collective-permute-start | bytes 2457608 | tf_op jit(solution)/shard_map/weight_grads/ppermute | solution.py:38
  139.7 17.1 %copy-start.8 = (bf16[2,80,1280]{2,1,0:T(8,128)(2,1)S(1)}, bf16[2,80,1280]{2,1,0:T(8,128)(2,1)}, u32[]{:S(2)}) copy-start(bf16[2,80,1280]{2,1,0:T(8,128)(2,1)} %get-tuple-element.115) | copy-start | bytes 1228804
  156.9 9.4 %collective-permute-start.32 = (bf16[2,80,1280]{2,1,0:T(8,128)(2,1)S(1)}, bf16[2,80,1280]{2,1,0:T(8,128)(2,1)S(1)}, u32[]{:S(2)}, u32[]{:S(2)}) collective-permute-start(bf16[2,80,1280]{2,1,0:T(8,128)(2,1)S(1)} %add_convert_fusion.1), channel_id=1, source_target_pairs={{0,6},{1,7},{2,0},{3,1},{4,2},{5,3},{6,4},{7,5},{8,14},{9,15},{10,... | collective-permute-start | bytes 1228808 | tf_op jit(solution)/shard_map/weight_grads/ppermute | solution.py:38
  160.0 9.9 %collective-permute-start.30 = (bf16[2,80,1280]{2,1,0:T(8,128)(2,1)S(1)}, bf16[2,80,1280]{2,1,0:T(8,128)(2,1)S(1)}, u32[]{:S(2)}, u32[]{:S(2)}) collective-permute-start(bf16[2,80,1280]{2,1,0:T(8,128)(2,1)S(1)} %add_convert_fusion.2), channel_id=1, source_target_pairs={{0,2},{1,3},{2,4},{3,5},{4,6},{5,7},{6,0},{7,1},{8,10},{9,11},{10,... | collective-permute-start | bytes 1228808 | tf_op jit(solution)/shard_map/weight_grads/ppermute | solution.py:38
  160.3 14.1 %collective-permute-start.27 = (bf16[2,80,1280]{2,1,0:T(8,128)(2,1)S(1)}, bf16[2,80,1280]{2,1,0:T(8,128)(2,1)S(1)}, u32[]{:S(2)}, u32[]{:S(2)}) collective-permute-start(bf16[2,80,1280]{2,1,0:T(8,128)(2,1)S(1)} %add_convert_fusion.4), channel_id=1, source_target_pairs={{0,24},{1,25},{2,26},{3,27},{4,28},{5,29},{6,30},{7,31},{8,0},{9,1... | collective-permute-start | bytes 1228808 | tf_op jit(solution)/shard_map/weight_grads/ppermute | solution.py:38
  160.8 13.5 %collective-permute-start.25 = (bf16[2,80,1280]{2,1,0:T(8,128)(2,1)S(1)}, bf16[2,80,1280]{2,1,0:T(8,128)(2,1)S(1)}, u32[]{:S(2)}, u32[]{:S(2)}) collective-permute-start(bf16[2,80,1280]{2,1,0:T(8,128)(2,1)S(1)} %add_convert_fusion.5), channel_id=1, source_target_pairs={{0,8},{1,9},{2,10},{3,11},{4,12},{5,13},{6,14},{7,15},{8,16},{9,17... | collective-permute-start | bytes 1228808 | tf_op jit(solution)/shard_map/weight_grads/ppermute | solution.py:38
  170.3 8.7 %collective-permute-start.34 = (bf16[80,1280]{1,0:T(8,128)(2,1)S(1)}, bf16[80,1280]{1,0:T(8,128)(2,1)S(1)}, u32[]{:S(2)}, u32[]{:S(2)}) collective-permute-start(bf16[80,1280]{1,0:T(8,128)(2,1)S(1)} %get-tuple-element.132), channel_id=1, source_target_pairs={{0,16},{1,17},{2,18},{3,19},{4,20},{5,21},{6,22},{7,23},{8,24},{9,... | collective-permute-start | bytes 614408 | tf_op jit(solution)/shard_map/weight_grads/ppermute | solution.py:38
  172.2 8.2 %collective-permute-start.33 = (bf16[80,1280]{1,0:T(8,128)(2,1)S(1)}, bf16[80,1280]{1,0:T(8,128)(2,1)S(1)}, u32[]{:S(2)}, u32[]{:S(2)}) collective-permute-start(bf16[80,1280]{1,0:T(8,128)(2,1)S(1)} %get-tuple-element.131), channel_id=1, source_target_pairs={{0,24},{1,25},{2,26},{3,27},{4,28},{5,29},{6,30},{7,31},{8,0},{9,1... | collective-permute-start | bytes 614408 | tf_op jit(solution)/shard_map/weight_grads/ppermute | solution.py:38
  172.7 7.7 %collective-permute-start.31 = (bf16[80,1280]{1,0:T(8,128)(2,1)S(1)}, bf16[80,1280]{1,0:T(8,128)(2,1)S(1)}, u32[]{:S(2)}, u32[]{:S(2)}) collective-permute-start(bf16[80,1280]{1,0:T(8,128)(2,1)S(1)} %fusion.10), channel_id=1, source_target_pairs={{0,8},{1,9},{2,10},{3,11},{4,12},{5,13},{6,14},{7,15},{8,16},{9,17... | collective-permute-start | bytes 614408 | tf_op jit(solution)/shard_map/weight_grads/ppermute | solution.py:38
  174.7 7.4 %collective-permute-start.29 = (bf16[80,1280]{1,0:T(8,128)(2,1)S(1)}, bf16[80,1280]{1,0:T(8,128)(2,1)S(1)}, u32[]{:S(2)}, u32[]{:S(2)}) collective-permute-start(bf16[80,1280]{1,0:T(8,128)(2,1)S(1)} %get-tuple-element.130), channel_id=1, source_target_pairs={{0,4},{1,5},{2,6},{3,7},{4,0},{5,1},{6,2},{7,3},{8,12},{9,13},{10,... | collective-permute-start | bytes 614408 | tf_op jit(solution)/shard_map/weight_grads/ppermute | solution.py:38
  178.3 7.4 %collective-permute-start.28 = (bf16[80,1280]{1,0:T(8,128)(2,1)S(1)}, bf16[80,1280]{1,0:T(8,128)(2,1)S(1)}, u32[]{:S(2)}, u32[]{:S(2)}) collective-permute-start(bf16[80,1280]{1,0:T(8,128)(2,1)S(1)} %get-tuple-element.129), channel_id=1, source_target_pairs={{0,6},{1,7},{2,0},{3,1},{4,2},{5,3},{6,4},{7,5},{8,14},{9,15},{10,... | collective-permute-start | bytes 614408 | tf_op jit(solution)/shard_map/weight_grads/ppermute | solution.py:38
  179.0 7.0 %collective-permute-start.26 = (bf16[80,1280]{1,0:T(8,128)(2,1)S(1)}, bf16[80,1280]{1,0:T(8,128)(2,1)S(1)}, u32[]{:S(2)}, u32[]{:S(2)}) collective-permute-start(bf16[80,1280]{1,0:T(8,128)(2,1)S(1)} %fusion.9), channel_id=1, source_target_pairs={{0,2},{1,3},{2,4},{3,5},{4,6},{5,7},{6,0},{7,1},{8,10},{9,11},{10,... | collective-permute-start | bytes 614408 | tf_op jit(solution)/shard_map/weight_grads/ppermute | solution.py:38
  186.2 1.5 collective-permute-start.35
  186.4 17.4 %collective-permute-start.23 = (bf16[256,1280]{1,0:T(8,128)(2,1)}, bf16[256,1280]{1,0:T(8,128)(2,1)}, u32[]{:S(2)}, u32[]{:S(2)}) collective-permute-start(bf16[256,1280]{1,0:T(8,128)(2,1)} %get-tuple-element.105), channel_id=1, source_target_pairs={{0,1},{1,0},{2,3},{3,2},{4,5},{5,4},{6,7},{7,6},{8,9},{9,8},{10,11... | collective-permute-start | bytes 1966088 | tf_op jit(solution)/shard_map/norm_grad/ppermute | solution.py:42
  188.1 7.6 %collective-permute-start.38 = (bf16[40,1280]{1,0:T(8,128)(2,1)S(1)}, bf16[40,1280]{1,0:T(8,128)(2,1)S(1)}, u32[]{:S(2)}, u32[]{:S(2)}) collective-permute-start(bf16[40,1280]{1,0:T(8,128)(2,1)S(1)} %get-tuple-element.127), channel_id=1, source_target_pairs={{0,64},{32,96},{64,0},{96,32},{1,65},{33,97},{65,1},{97,33},{2,66}... | collective-permute-start | bytes 307208 | tf_op jit(solution)/shard_map/over_groups/ppermute | solution.py:37
  192.5 6.4 %collective-permute-start.37 = (bf16[40,1280]{1,0:T(8,128)(2,1)S(1)}, bf16[40,1280]{1,0:T(8,128)(2,1)S(1)}, u32[]{:S(2)}, u32[]{:S(2)}) collective-permute-start(bf16[40,1280]{1,0:T(8,128)(2,1)S(1)} %get-tuple-element.128), channel_id=1, source_target_pairs={{0,96},{32,0},{64,32},{96,64},{1,97},{33,1},{65,33},{97,65},{2,98}... | collective-permute-start | bytes 307208 | tf_op jit(solution)/shard_map/over_groups/ppermute | solution.py:37
  195.0 5.9 %collective-permute-start.36 = (bf16[40,1280]{1,0:T(8,128)(2,1)S(1)}, bf16[40,1280]{1,0:T(8,128)(2,1)S(1)}, u32[]{:S(2)}, u32[]{:S(2)}) collective-permute-start(bf16[40,1280]{1,0:T(8,128)(2,1)S(1)} %get-tuple-element.126), channel_id=1, source_target_pairs={{0,32},{32,64},{64,96},{96,0},{1,33},{33,65},{65,97},{97,1},{2,34}... | collective-permute-start | bytes 307208 | tf_op jit(solution)/shard_map/over_groups/ppermute | solution.py:37
  195.0 8.7 %collective-permute-start.24 = (bf16[256,640]{1,0:T(8,128)(2,1)S(1)}, bf16[256,640]{1,0:T(8,128)(2,1)S(1)}, u32[]{:S(2)}, u32[]{:S(2)}) collective-permute-start(bf16[256,640]{1,0:T(8,128)(2,1)S(1)} %slice.164), channel_id=1, source_target_pairs={{0,1},{1,0},{2,3},{3,2},{4,5},{5,4},{6,7},{7,6},{8,9},{9,8},{10,11... | collective-permute-start | bytes 983048 | tf_op jit(solution)/shard_map/norm_grad/ppermute | solution.py:42
  200.9 7.5 %collective-permute-start.39 = (bf16[40,1280]{1,0:T(8,128)(2,1)S(1)}, bf16[40,1280]{1,0:T(8,128)(2,1)S(1)}, u32[]{:S(2)}, u32[]{:S(2)}) collective-permute-start(bf16[40,1280]{1,0:T(8,128)(2,1)S(1)} %fusion.13), channel_id=1, source_target_pairs={{0,96},{32,0},{64,32},{96,64},{1,97},{33,1},{65,33},{97,65},{2,98}... | collective-permute-start | bytes 307208 | tf_op jit(solution)/shard_map/over_groups/ppermute | solution.py:37
  201.8 6.7 %collective-permute-start.40 = (bf16[40,1280]{1,0:T(8,128)(2,1)S(1)}, bf16[40,1280]{1,0:T(8,128)(2,1)S(1)}, u32[]{:S(2)}, u32[]{:S(2)}) collective-permute-start(bf16[40,1280]{1,0:T(8,128)(2,1)S(1)} %fusion.13), channel_id=1, source_target_pairs={{0,32},{32,64},{64,96},{96,0},{1,33},{33,65},{65,97},{97,1},{2,34}... | collective-permute-start | bytes 307208 | tf_op jit(solution)/shard_map/over_groups/ppermute | solution.py:37
  203.0 6.2 %collective-permute-start.41 = (bf16[40,1280]{1,0:T(8,128)(2,1)S(1)}, bf16[40,1280]{1,0:T(8,128)(2,1)S(1)}, u32[]{:S(2)}, u32[]{:S(2)}) collective-permute-start(bf16[40,1280]{1,0:T(8,128)(2,1)S(1)} %fusion.13), channel_id=1, source_target_pairs={{0,64},{32,96},{64,0},{96,32},{1,65},{33,97},{65,1},{97,33},{2,66}... | collective-permute-start | bytes 307208 | tf_op jit(solution)/shard_map/over_groups/ppermute | solution.py:37
  (20 other events, 108.6 us)

commit v3 on v2

--- a/solution.py
+++ b/solution.py
@@ -231,17 +231,18 @@
         local = at_rows(w % 2, WIN)
         kinds = jnp.where(w < 2, own[local, D:].astype(F32), sib[local, D:].astype(F32)).astype(BF)
         allowed = dot_nt(kinds, kinds) > 0.5
-        for h in range(HPC):
-            q = qkv[rows, h * HD:(h + 1) * HD]
-            k = qkv[rows, HALF + h * HD:HALF + (h + 1) * HD]
-            scores[h] = dot_nt(k, q)
-        for h in range(HPC):
-            s = jnp.where(allowed, scores[h] * scale, -1e30)
-            e = jnp.exp(s - jnp.max(s, axis=0, keepdims=True))
-            probs[w, h] = e * (1.0 / jnp.sum(e, axis=0, keepdims=True))
-        for h in range(HPC):
-            v = qkv[rows, 2 * HALF + h * HD:2 * HALF + (h + 1) * HD]
-            attended[rows, h * HD:(h + 1) * HD] = dot_tn(probs[w, h].astype(BF), v).astype(BF)
+        outs = []
+        for group in range(0, HPC, 8):
+            heads = [(h, h * HD, (h + 1) * HD) for h in range(group, group + 8)]
+            for h, a, b in heads:
+                scores[h] = dot_nt(qkv[rows, HALF + a:HALF + b], qkv[rows, a:b])
+            for h, a, b in heads:
+                s = jnp.where(allowed, scores[h] * scale, -1e30)
+                e = jnp.exp(s - jnp.max(s, axis=0, keepdims=True))
+                probs[w, h] = e * (1.0 / jnp.sum(e, axis=0, keepdims=True))
+            for h, a, b in heads:
+                outs.append(dot_tn(probs[w, h].astype(BF), qkv[rows, 2 * HALF + a:2 * HALF + b]).astype(BF))
+        attended[rows, :] = jnp.concatenate(outs, axis=1)
 
     out_copies.append(copies.start(probs, probs_out))
     wait_all(out_copies)
@@ -308,21 +309,24 @@
     @pl.loop(0, 4)
     def _(w):
         rows = at_rows(w, WIN)
-        for h in range(HPC):
-            a, b = h * HD, (h + 1) * HD
-            scores[h] = dot_nt(qkv[rows, 2 * HALF + a:2 * HALF + b], gatt[rows, a:b])
-        for h in range(HPC):
-            a, b = h * HD, (h + 1) * HD
-            gqkv[rows, 2 * HALF + a:2 * HALF + b] = dot(probs[w, h].astype(BF), gatt[rows, a:b]).astype(BF)
-        for h in range(HPC):
-            p = probs[w, h]
-            g = scores[h]
-            inner = jnp.sum(p * g, axis=0, keepdims=True)
-            small[h] = (p * (g - inner) * scale).astype(BF)
-        for h in range(HPC):
-            a, b = h * HD, (h + 1) * HD
-            gqkv[rows, HALF + a:HALF + b] = dot(small[h], qkv[rows, a:b]).astype(BF)
-            gqkv[rows, a:b] = dot_tn(small[h], qkv[rows, HALF + a:HALF + b]).astype(BF)
+        to_query, to_key, to_value = [], [], []
+        for group in range(0, HPC, 8):
+            heads = [(h, h * HD, (h + 1) * HD) for h in range(group, group + 8)]
+            for h, a, b in heads:
+                scores[h] = dot_nt(qkv[rows, 2 * HALF + a:2 * HALF + b], gatt[rows, a:b])
+            for h, a, b in heads:
+                to_value.append(dot(probs[w, h].astype(BF), gatt[rows, a:b]).astype(BF))
+            for h, a, b in heads:
+                p = probs[w, h]
+                g = scores[h]
+                inner = jnp.sum(p * g, axis=0, keepdims=True)
+                small[h] = (p * (g - inner) * scale).astype(BF)
+            for h, a, b in heads:
+                to_key.append(dot(small[h], qkv[rows, a:b]).astype(BF))
+                to_query.append(dot_tn(small[h], qkv[rows, HALF + a:HALF + b]).astype(BF))
+        gqkv[rows, :HALF] = jnp.concatenate(to_query, axis=1)
+        gqkv[rows, HALF:2 * HALF] = jnp.concatenate(to_key, axis=1)
+        gqkv[rows, 2 * HALF:] = jnp.concatenate(to_value, axis=1)
 
     out_copies = [copies.start(gqkv, gqkv_out)]
     wait_all(second_in)
@@ -461,9 +465,9 @@
             "svvv" + "a" * 5,
             scratch=[pltpu.VMEM((D, HALF), BF), pltpu.SemaphoreType.DMA((16,))],
         )
+        ga_mine, ga_theirs, outgoing = lax.optimization_barrier((ga_mine, ga_theirs, outgoing))
         ga_other = to_sibling(ga_theirs)
     with jax.named_scope("backward"):
-        ga_mine, ga_other, outgoing = lax.optimization_barrier((ga_mine, ga_other, outgoing))
         pieces = [((4, 80, D), BF)] * 3 + [((2, 80, D), BF)] * 2
         gqkv, *terms = call(
             backward_kernel,
@@ -489,11 +493,10 @@
                 pltpu.VMEM((512, 3 * HALF), BF),
                 pltpu.SemaphoreType.DMA((60,)),
             ],
-            us=21,
+            us=1,
         )
     with jax.named_scope("rows_out"):
         owner_rows = lax.all_to_all(outgoing, ("grp", "enc"), split_axis=0, concat_axis=0, tiled=True)
-        owner_rows, terms = lax.optimization_barrier((owner_rows, terms))
         owner_rows = owner_rows.reshape(64, 2, 8, HALF).transpose(0, 2, 1, 3).reshape(512, D)
     with jax.named_scope("weight_grads"):
         up_a, down_a = scatter_first(*terms[1:3], "x")
@@ -507,10 +510,12 @@
             (place, gqkv, *part_a, *part_b),
             "sv" + "a" * 10,
             scratch=[pltpu.VMEM((D, 3 * HALF), BF), pltpu.SemaphoreType.DMA((32,))],
-            us=8,
+            us=1,
         )
     with jax.named_scope("weight_grads"):
-        up_a, down_a, up_b, down_b, ntheirs = lax.optimization_barrier((up_a, down_a, up_b, down_b, ntheirs))
+        up_a, down_a, up_b, down_b, ntheirs, owner_rows = lax.optimization_barrier(
+            (up_a, down_a, up_b, down_b, ntheirs, owner_rows)
+        )
         sum_a = scatter_second(terms[0], up_a, down_a, *terms[3:5], "x", "z")
         sum_b = scatter_second(terms[5], up_b, down_b, *terms[8:], "z", "x")
     with jax.named_scope("norm_grad"):

time: 213 us -> 205 us (0.962)
  waiting for transfers between devices: 56.4 us -> 49.9 us
  Pallas kernels: 63.8 us -> 58 us
  other arithmetic: 4.14 us -> 7.4 us
    pallas_call x8, Pallas kernels: 63.8 us -> 58 us  [call(): pl.pallas_call(kernel, out_shape=[jax.ShapeDtypeStruct(s, t) for s, t in...]
    ppermute x8, waiting for transfers between devices: 6.86 us -> 4.69 us  [to_sibling(): return lax.ppermute(value, 'enc', [(i, i ^ 1) for i in range(32)])]
    unnamed x50 -> x48, local copies, waits for them, and re-layouts: 7.11 us -> 7.27 us
  transfers between devices with their start and end apart: 44 -> 44, of which waited for: 23 -> 26; matrix products, arithmetic and copies ran while one was open for 3% -> 3% of each run, Pallas kernels for 27% -> 26%
where the time goes in v3:
time: 205 us; the launch traced here: 204 us
  starting transfers between devices  77 us (38%)
  Pallas kernels  58 us (28%)
  waiting for transfers between devices  49.9 us (24%)
  local copies, waits for them, and re-layouts  10.1 us (5%)
  other arithmetic  7.4 us (4%)
    pallas_call x8, Pallas kernels, call(): pl.pallas_call(kernel, out_shape=[jax.ShapeDtypeStruct(s, t) for s, t in...  58 us
    ppermute x28, starting transfers between devices, hop(): return lax.ppermute(value, 'enc', ring(axis, step))  47.9 us
    ppermute x28, waiting for transfers between devices, hop(): return lax.ppermute(value, 'enc', ring(axis, step))  40.7 us
    all_to_all x1, starting transfers between devices, body(): lax.all_to_all(outgoing, ('grp', 'enc'), split_axis=0, concat_axis=0, til...  9.79 us
    ppermute x6, starting transfers between devices, hop(): return lax.ppermute(value, 'grp', [(i, (i + step) % 4) for i in range(4)])  9.16 us
    all_to_all x1, starting transfers between devices, body(): lax.all_to_all(sent, ('grp', 'enc'), split_axis=0, concat_axis=0, tiled=T...  8.88 us
    unnamed x48, local copies, waits for them, and re-layouts  7.27 us
    ppermute x8, waiting for transfers between devices, to_sibling(): return lax.ppermute(value, 'enc', [(i, i ^ 1) for i in range(32)])  4.69 us
  transfers between devices with their start and end apart: 44, of which 26 were waited for; matrix products, arithmetic and copies ran while one was open for 3% of the time, Pallas kernels for 26%

profile of v3, /device:TPU:0, one launch (start us, length us, event | category | flops | bytes accessed | tf_op | source)
XLA Modules:
  0.0 203.6 jit_solution(2764986121254088235)
XLA Ops:
  1.8 1.4 collective-permute-done
  3.5 2.9 %collective-permute-start.8 = (bf16[80,1280]{1,0:T(8,128)(2,1)S(1)}, bf16[80,1280]{1,0:T(8,128)(2,1)S(1)}, u32[]{:S(2)}, u32[]{:S(2)}) collective-permute-start(bf16[80,1280]{1,0:T(8,128)(2,1)S(1)} %get-tuple-element.115), channel_id=1, source_target_pairs={{0,24},{1,25},{2,26},{3,27},{4,28},{5,29},{6,30},{7,31},{8,0},{9,1... | collective-permute-start | bytes 614408 | tf_op jit(solution)/shard_map/weights/ppermute | solution.py:38
  6.4 2.3 %collective-permute-start.10 = (bf16[80,1280]{1,0:T(8,128)(2,1)S(1)}, bf16[80,1280]{1,0:T(8,128)(2,1)S(1)}, u32[]{:S(2)}, u32[]{:S(2)}) collective-permute-start(bf16[80,1280]{1,0:T(8,128)(2,1)S(1)} %get-tuple-element.115), channel_id=1, source_target_pairs={{0,16},{1,17},{2,18},{3,19},{4,20},{5,21},{6,22},{7,23},{8,24},{9,... | collective-permute-start | bytes 614408 | tf_op jit(solution)/shard_map/weights/ppermute | solution.py:38
  8.7 4.0 %collective-permute-start.1 = (bf16[80,1280]{1,0:T(8,128)(2,1)S(1)}, bf16[80,1280]{1,0:T(8,128)(2,1)S(1)}, u32[]{:S(2)}, u32[]{:S(2)}) collective-permute-start(bf16[80,1280]{1,0:T(8,128)(2,1)S(1)} %get-tuple-element.116), channel_id=1, source_target_pairs={{0,6},{1,7},{2,0},{3,1},{4,2},{5,3},{6,4},{7,5},{8,14},{9,15},{10,... | collective-permute-start | bytes 614408 | tf_op jit(solution)/shard_map/weights/ppermute | solution.py:38
  12.7 2.7 %collective-permute-done.8 = bf16[80,1280]{1,0:T(8,128)(2,1)S(1)} collective-permute-done((bf16[80,1280]{1,0:T(8,128)(2,1)S(1)}, bf16[80,1280]{1,0:T(8,128)(2,1)S(1)}, u32[]{:S(2)}, u32[]{:S(2)}) %collective-permute-start.8) | collective-permute-done | bytes 204832 | tf_op jit(solution)/shard_map/weights/ppermute | solution.py:38
  15.4 3.9 %collective-permute-start.3 = (bf16[80,1280]{1,0:T(8,128)(2,1)S(1)}, bf16[80,1280]{1,0:T(8,128)(2,1)S(1)}, u32[]{:S(2)}, u32[]{:S(2)}) collective-permute-start(bf16[80,1280]{1,0:T(8,128)(2,1)S(1)} %get-tuple-element.116), channel_id=1, source_target_pairs={{0,4},{1,5},{2,6},{3,7},{4,0},{5,1},{6,2},{7,3},{8,12},{9,13},{10,... | collective-permute-start | bytes 614408 | tf_op jit(solution)/shard_map/weights/ppermute | solution.py:38
  19.4 1.5 collective-permute-start.12
  23.8 2.3 %collective-permute-start.11 = (bf16[4,80,1280]{2,1,0:T(8,128)(2,1)S(1)}, bf16[4,80,1280]{2,1,0:T(8,128)(2,1)S(1)}, u32[]{:S(2)}, u32[]{:S(2)}) collective-permute-start(bf16[4,80,1280]{2,1,0:T(8,128)(2,1)S(1)} %pad_maximum_fusion.1.b0), channel_id=1, source_target_pairs={{0,6},{1,7},{2,0},{3,1},{4,2},{5,3},{6,4},{7,5},{8,14},{9,15},{10,... | collective-permute-start | bytes 2457608 | tf_op jit(solution)/shard_map/weights/ppermute | solution.py:38
  26.2 1.7 collective-permute-start.5
  27.8 1.7 collective-permute-start.4
  29.5 3.5 %prepare.2 = (bf16[256,1408]{1,0:T(8,128)(2,1)}, bf16[256,1664]{1,0:T(8,128)(2,1)}, bf16[256,1280]{1,0:T(8,128)(2,1)}) custom-call(s32[3]{0:T(128)} %pad_add_fusion.place, s32[1,4]{1,0:T(1,128)} %counts.1, bf16[256,1280]{1,0:T(8,128)(2,1)} %patches.1, f32[1,1280]{1,0:T(1,128)} %reshape.38.gain, s32[256,1]{1,0:T(8,128)} %copy.13.order, s32[256,1]{1,0:T(8,128)} %copy.14.owners), custom_call_target="tpu_custom_call" | custom-call | flops 3000000000 | bytes 9000000 | tf_op jit(solution)/shard_map/prepare/pallas_call | solution.py:97
  33.1 8.7 %collective-permute-done.12.b2 = bf16[4,80,1280]{2,1,0:T(8,128)(2,1)S(1)} collective-permute-done((bf16[4,80,1280]{2,1,0:T(8,128)(2,1)S(1)}, bf16[4,80,1280]{2,1,0:T(8,128)(2,1)S(1)}, u32[]{:S(2)}, u32[]{:S(2)}) %collective-permute-start.12) | collective-permute-done | bytes 819232 | tf_op jit(solution)/shard_map/weights/ppermute | solution.py:38
  42.1 1.5 collective-permute-start.13
  43.7 2.7 %collective-permute-done.5.a2 = bf16[4,80,1280]{2,1,0:T(8,128)(2,1)S(1)} collective-permute-done((bf16[4,80,1280]{2,1,0:T(8,128)(2,1)S(1)}, bf16[4,80,1280]{2,1,0:T(8,128)(2,1)S(1)}, u32[]{:S(2)}, u32[]{:S(2)}) %collective-permute-start.5) | collective-permute-done | bytes 819232 | tf_op jit(solution)/shard_map/weights/ppermute | solution.py:38
  46.3 1.6 collective-permute-start.14
  49.1 3.0 %collective-permute-start.7 = (bf16[2,80,1280]{2,1,0:T(8,128)(2,1)S(1)}, bf16[2,80,1280]{2,1,0:T(8,128)(2,1)S(1)}, u32[]{:S(2)}, u32[]{:S(2)}) collective-permute-start(bf16[2,80,1280]{2,1,0:T(8,128)(2,1)S(1)} %slice.197), channel_id=1, source_target_pairs={{0,24},{1,25},{2,26},{3,27},{4,28},{5,29},{6,30},{7,31},{8,0},{9,1... | collective-permute-start | bytes 1228808 | tf_op jit(solution)/shard_map/weights/ppermute | solution.py:38
  52.2 2.8 %prepare.3.normed_hbm = bf16[1280,512]{1,0:T(8,128)(2,1)} custom-call(bf16[256,1408]{1,0:T(8,128)(2,1)} %get-tuple-element.50.own, bf16[256,1408]{1,0:T(8,128)(2,1)} %copy-done.21), custom_call_target="tpu_custom_call" | custom-call | flops 3000000000 | bytes 9000000 | tf_op jit(solution)/shard_map/prepare/pallas_call | solution.py:97
  55.6 2.6 %collective-permute-done.6.a3 = bf16[2,80,1280]{2,1,0:T(8,128)(2,1)S(1)} collective-permute-done((bf16[2,80,1280]{2,1,0:T(8,128)(2,1)S(1)}, bf16[2,80,1280]{2,1,0:T(8,128)(2,1)S(1)}, u32[]{:S(2)}, u32[]{:S(2)}) %collective-permute-start.6) | collective-permute-done | bytes 409632 | tf_op jit(solution)/shard_map/weights/ppermute | solution.py:38
  60.0 8.9 %all-to-all-start = ((bf16[128,8,640]{2,1,0:T(8,128)(2,1)}), bf16[128,8,640]{2,1,0:T(8,128)(2,1)S(1)}, u32[]{:S(2)}, u32[]{:S(2)}) async-start(bf16[128,8,640]{2,1,0:T(8,128)(2,1)} %bitcast.15), calls=%async_computation | async-start | bytes 2621440 | tf_op jit(solution)/shard_map/grads_in/all_to_all | solution.py:433
  68.9 12.3 %forward.2 = (f32[4,8,128,128]{3,2,1,0:T(8,128)}, bf16[512,1920]{1,0:T(8,128)(2,1)}, bf16[512,640]{1,0:T(8,128)(2,1)}) custom-call(s32[3]{0:T(128)} %pad_add_fusion.place, bf16[256,1408]{1,0:T(8,128)(2,1)} %get-tuple-element.50.own, bf16[256,1408]{1,0:T(8,128)(2,1)} %copy-done.21, bf16[4,80,1280]{2,1,0:T(8,128)(2,1)} %copy-done.1, ...), custom_call_target="tpu_custom_call" | custom-call | flops 12000000000 | bytes 36000000 | tf_op jit(solution)/shard_map/forward/pallas_call | solution.py:97
  81.5 2.3 %collective-permute-done.17.other.other_hbm = bf16[512,640]{1,0:T(8,128)(2,1)S(1)} collective-permute-done((bf16[512,640]{1,0:T(8,128)(2,1)}, bf16[512,640]{1,0:T(8,128)(2,1)S(1)}, u32[]{:S(2)}, u32[]{:S(2)}) %collective-permute-start.17) | collective-permute-done | bytes 655392 | tf_op jit(solution)/shard_map/forward/ppermute | solution.py:42
  84.7 7.0 %forward.3 = bf16[1024,640]{1,0:T(8,128)(2,1)} custom-call(s32[3]{0:T(128)} %pad_add_fusion.place, bf16[512,640]{1,0:T(8,128)(2,1)} %get-tuple-element.63.attended.attended_hbm, bf16[512,640]{1,0:T(8,128)(2,1)} %copy-done.10, bf16[256,1280]{1,0:T(8,128)(2,1)} %get-tuple-element.64.ordered, bf16[256,1664]{1,0:T(8,128)(2,1)} %get-tuple-element.51.extra, ...), custom_call_target="tpu_custom_call" | custom-call | flops 3000000000 | bytes 9000000 | tf_op jit(solution)/shard_map/forward/pallas_call | solution.py:97
  92.7 5.7 %grads_in.1 = (bf16[512,640]{1,0:T(8,128)(2,1)}, f32[512,640]{1,0:T(8,128)}, bf16[512,640]{1,0:T(8,128)(2,1)}) custom-call(s32[3]{0:T(128)} %pad_add_fusion.place, bf16[1024,640]{1,0:T(8,128)(2,1)} %bitcast.78, bf16[256,1664]{1,0:T(8,128)(2,1)} %get-tuple-element.51.extra, bf16[256,1664]{1,0:T(8,128)(2,1)} %collective-permute-done.16.sib_extra, ...), custom_call_target="tpu_custom_call" | custom-call | flops 3000000000 | bytes 9000000 | tf_op jit(solution)/shard_map/grads_in/pallas_call | solution.py:97
  98.6 9.8 %all-to-all-start.1 = ((bf16[128,8,640]{2,1,0:T(8,128)(2,1)}), bf16[128,8,640]{2,1,0:T(8,128)(2,1)S(1)}, u32[]{:S(2)}, u32[]{:S(2)}) async-start(bf16[128,8,640]{2,1,0:T(8,128)(2,1)} %bitcast.17), calls=%async_computation.1 | async-start | bytes 2621440 | tf_op jit(solution)/shard_map/rows_out/all_to_all | solution.py:499
  109.3 14.4 %backward.1 = (bf16[512,1920]{1,0:T(8,128)(2,1)}, bf16[4,80,1280]{2,1,0:T(8,128)(2,1)}, bf16[4,80,1280]{2,1,0:T(8,128)(2,1)}, bf16[4,80,1280]{2,1,0:T(8,128)(2,1...) custom-call(s32[3]{0:T(128)} %pad_add_fusion.place, ...), custom_call_target="tpu_custom_call" | custom-call | flops 1000000000 | bytes 3000000 | tf_op jit(solution)/shard_map/backward/pallas_call | solution.py:97
  124.8 2.3 %collective-permute-start.20 = (bf16[4,80,1280]{2,1,0:T(8,128)(2,1)}, bf16[4,80,1280]{2,1,0:T(8,128)(2,1)}, u32[]{:S(2)}, u32[]{:S(2)}) collective-permute-start(bf16[4,80,1280]{2,1,0:T(8,128)(2,1)} %get-tuple-element.77), channel_id=1, source_target_pairs={{0,24},{1,25},{2,26},{3,27},{4,28},{5,29},{6,30},{7,31},{8,0},{9,1... | collective-permute-start | bytes 2457608 | tf_op jit(solution)/shard_map/weight_grads/ppermute | solution.py:38
  128.1 2.2 %collective-permute-start.22 = (bf16[4,80,1280]{2,1,0:T(8,128)(2,1)}, bf16[4,80,1280]{2,1,0:T(8,128)(2,1)S(1)}, u32[]{:S(2)}, u32[]{:S(2)}) collective-permute-start(bf16[4,80,1280]{2,1,0:T(8,128)(2,1)} %get-tuple-element.79), channel_id=1, source_target_pairs={{0,6},{1,7},{2,0},{3,1},{4,2},{5,3},{6,4},{7,5},{8,14},{9,15},{10,... | collective-permute-start | bytes 2457608 | tf_op jit(solution)/shard_map/weight_grads/ppermute | solution.py:38
  130.3 8.4 %norm_grad.2 = (f32[256,1280]{1,0:T(8,128)}, bf16[256,1280]{1,0:T(8,128)(2,1)}) custom-call(s32[3]{0:T(128)} %pad_add_fusion.place, bf16[512,1920]{1,0:T(8,128)(2,1)} %get-tuple-element.80.gqkv, bf16[4,80,1280]{2,1,0:T(8,128)(2,1)} %copy-done.1, bf16[4,80,1280]{2,1,0:T(8,128)(2,1)} %copy-done.5, bf16[4,80,1280]{2,1,0:T(8,128)(2,1)} %copy-done.4, ...), custom_call_target="tpu_custom_call" | custom-call | flops 1000000000 | bytes 3000000 | tf_op jit(solution)/shard_map/norm_grad/pallas_call | solution.py:97
  138.8 6.2 %collective-permute-done.19 = bf16[4,80,1280]{2,1,0:T(8,128)(2,1)} collective-permute-done((bf16[4,80,1280]{2,1,0:T(8,128)(2,1)}, bf16[4,80,1280]{2,1,0:T(8,128)(2,1)}, u32[]{:S(2)}, u32[]{:S(2)}) %collective-permute-start.19) | collective-permute-done | bytes 819232 | tf_op jit(solution)/shard_map/weight_grads/ppermute | solution.py:38
  145.1 3.0 %collective-permute-done.21 = bf16[4,80,1280]{2,1,0:T(8,128)(2,1)S(1)} collective-permute-done((bf16[4,80,1280]{2,1,0:T(8,128)(2,1)}, bf16[4,80,1280]{2,1,0:T(8,128)(2,1)S(1)}, u32[]{:S(2)}, u32[]{:S(2)}) %collective-permute-start.21) | collective-permute-done | bytes 819232 | tf_op jit(solution)/shard_map/weight_grads/ppermute | solution.py:38
  150.9 2.9 %collective-permute-start.27 = (bf16[2,80,1280]{2,1,0:T(8,128)(2,1)S(1)}, bf16[2,80,1280]{2,1,0:T(8,128)(2,1)S(1)}, u32[]{:S(2)}, u32[]{:S(2)}) collective-permute-start(bf16[2,80,1280]{2,1,0:T(8,128)(2,1)S(1)} %add_convert_fusion.4), channel_id=1, source_target_pairs={{0,24},{1,25},{2,26},{3,27},{4,28},{5,29},{6,30},{7,31},{8,0},{9,1... | collective-permute-start | bytes 1228808 | tf_op jit(solution)/shard_map/weight_grads/ppermute | solution.py:38
  153.9 1.5 collective-permute-start.30
  155.6 1.9 collective-permute-start.32
  157.4 3.1 %collective-permute-done.25 = bf16[2,80,1280]{2,1,0:T(8,128)(2,1)S(1)} collective-permute-done((bf16[2,80,1280]{2,1,0:T(8,128)(2,1)S(1)}, bf16[2,80,1280]{2,1,0:T(8,128)(2,1)S(1)}, u32[]{:S(2)}, u32[]{:S(2)}) %collective-permute-start.25) | collective-permute-done | bytes 409632 | tf_op jit(solution)/shard_map/weight_grads/ppermute | solution.py:38
  162.7 2.5 %collective-permute-start.28 = (bf16[80,1280]{1,0:T(8,128)(2,1)S(1)}, bf16[80,1280]{1,0:T(8,128)(2,1)S(1)}, u32[]{:S(2)}, u32[]{:S(2)}) collective-permute-start(bf16[80,1280]{1,0:T(8,128)(2,1)S(1)} %get-tuple-element.109), channel_id=1, source_target_pairs={{0,6},{1,7},{2,0},{3,1},{4,2},{5,3},{6,4},{7,5},{8,14},{9,15},{10,... | collective-permute-start | bytes 614408 | tf_op jit(solution)/shard_map/weight_grads/ppermute | solution.py:38
  167.2 3.8 %collective-permute-start.33 = (bf16[80,1280]{1,0:T(8,128)(2,1)S(1)}, bf16[80,1280]{1,0:T(8,128)(2,1)S(1)}, u32[]{:S(2)}, u32[]{:S(2)}) collective-permute-start(bf16[80,1280]{1,0:T(8,128)(2,1)S(1)} %get-tuple-element.111), channel_id=1, source_target_pairs={{0,24},{1,25},{2,26},{3,27},{4,28},{5,29},{6,30},{7,31},{8,0},{9,1... | collective-permute-start | bytes 614408 | tf_op jit(solution)/shard_map/weight_grads/ppermute | solution.py:38
  171.0 1.8 collective-permute-done.28
  173.2 2.0 collective-permute-done.26
  176.4 1.9 collective-permute-done.34
  178.3 2.1 %collective-permute-done.31 = bf16[80,1280]{1,0:T(8,128)(2,1)S(1)} collective-permute-done((bf16[80,1280]{1,0:T(8,128)(2,1)S(1)}, bf16[80,1280]{1,0:T(8,128)(2,1)S(1)}, u32[]{:S(2)}, u32[]{:S(2)}) %collective-permute-start.31) | collective-permute-done | bytes 204832 | tf_op jit(solution)/shard_map/weight_grads/ppermute | solution.py:38
  182.4 1.6 collective-permute-start.36
  184.0 1.7 collective-permute-start.37
  185.7 1.9 collective-permute-start.38
  188.6 1.5 collective-permute-done.37
  190.1 1.8 collective-permute-done.38
  192.0 1.9 collective-permute-start.39
  194.1 1.9 collective-permute-start.41
  196.7 4.0 %norm_grad.3 = bf16[256,1280]{1,0:T(8,128)(2,1)} custom-call(s32[3]{0:T(128)} %pad_add_fusion.place, f32[256,1280]{1,0:T(8,128)} %get-tuple-element.84.mine, bf16[256,1280]{1,0:T(8,128)(2,1)} %collective-permute-done.23.theirs, bf16[256,1280]{1,0:T(8,128)(2,1)} %get-tuple-element.64.ordered, f32[1,1280]{1,0:T(1,128)} %reshape.38.gain, ...), custom_call_target="tpu_custom_call" | custom-call | flops 3000000000 | bytes 9000000 | tf_op jit(solution)/shard_map/norm_grad/pallas_call | solution.py:97
  (135 shorter events, 29.4 us)
Async XLA Ops:
  1.8 1.5 collective-permute-start
  3.4 18.2 %copy-start.18 = (f32[1280]{0:T(1024)S(1)}, f32[1280]{0:T(1024)}, u32[]{:S(2)}) copy-start(f32[1280]{0:T(1024)} %param.9) | copy-start | bytes 15364
  3.4 18.8 %copy-start.20 = (s32[2,128]{1,0:T(2,128)S(1)}, s32[2,128]{1,0:T(2,128)}, u32[]{:S(2)}) copy-start(s32[2,128]{1,0:T(2,128)} %param.13) | copy-start | bytes 3076
  3.4 19.6 %copy-start.19 = (s32[256,1]{0,1:T(1,128)S(1)}, s32[256,1]{0,1:T(1,128)}, u32[]{:S(2)}) copy-start(s32[256,1]{0,1:T(1,128)} %param.14) | copy-start | bytes 3076
  3.5 11.9 %collective-permute-start.8 = (bf16[80,1280]{1,0:T(8,128)(2,1)S(1)}, bf16[80,1280]{1,0:T(8,128)(2,1)S(1)}, u32[]{:S(2)}, u32[]{:S(2)}) collective-permute-start(bf16[80,1280]{1,0:T(8,128)(2,1)S(1)} %get-tuple-element.115), channel_id=1, source_target_pairs={{0,24},{1,25},{2,26},{3,27},{4,28},{5,29},{6,30},{7,31},{8,0},{9,1... | collective-permute-start | bytes 614408 | tf_op jit(solution)/shard_map/weights/ppermute | solution.py:38
  6.4 12.9 %collective-permute-start.9 = (bf16[80,1280]{1,0:T(8,128)(2,1)S(1)}, bf16[80,1280]{1,0:T(8,128)(2,1)S(1)}, u32[]{:S(2)}, u32[]{:S(2)}) collective-permute-start(bf16[80,1280]{1,0:T(8,128)(2,1)S(1)} %get-tuple-element.115), channel_id=1, source_target_pairs={{0,8},{1,9},{2,10},{3,11},{4,12},{5,13},{6,14},{7,15},{8,16},{9,17... | collective-permute-start | bytes 614408 | tf_op jit(solution)/shard_map/weights/ppermute | solution.py:38
  6.4 12.9 %collective-permute-start.10 = (bf16[80,1280]{1,0:T(8,128)(2,1)S(1)}, bf16[80,1280]{1,0:T(8,128)(2,1)S(1)}, u32[]{:S(2)}, u32[]{:S(2)}) collective-permute-start(bf16[80,1280]{1,0:T(8,128)(2,1)S(1)} %get-tuple-element.115), channel_id=1, source_target_pairs={{0,16},{1,17},{2,18},{3,19},{4,20},{5,21},{6,22},{7,23},{8,24},{9,... | collective-permute-start | bytes 614408 | tf_op jit(solution)/shard_map/weights/ppermute | solution.py:38
  8.7 17.4 %collective-permute-start.1 = (bf16[80,1280]{1,0:T(8,128)(2,1)S(1)}, bf16[80,1280]{1,0:T(8,128)(2,1)S(1)}, u32[]{:S(2)}, u32[]{:S(2)}) collective-permute-start(bf16[80,1280]{1,0:T(8,128)(2,1)S(1)} %get-tuple-element.116), channel_id=1, source_target_pairs={{0,6},{1,7},{2,0},{3,1},{4,2},{5,3},{6,4},{7,5},{8,14},{9,15},{10,... | collective-permute-start | bytes 614408 | tf_op jit(solution)/shard_map/weights/ppermute | solution.py:38
  12.7 13.4 %collective-permute-start.2 = (bf16[80,1280]{1,0:T(8,128)(2,1)S(1)}, bf16[80,1280]{1,0:T(8,128)(2,1)S(1)}, u32[]{:S(2)}, u32[]{:S(2)}) collective-permute-start(bf16[80,1280]{1,0:T(8,128)(2,1)S(1)} %get-tuple-element.116), channel_id=1, source_target_pairs={{0,2},{1,3},{2,4},{3,5},{4,6},{5,7},{6,0},{7,1},{8,10},{9,11},{10,... | collective-permute-start | bytes 614408 | tf_op jit(solution)/shard_map/weights/ppermute | solution.py:38
  15.4 10.7 %collective-permute-start.3 = (bf16[80,1280]{1,0:T(8,128)(2,1)S(1)}, bf16[80,1280]{1,0:T(8,128)(2,1)S(1)}, u32[]{:S(2)}, u32[]{:S(2)}) collective-permute-start(bf16[80,1280]{1,0:T(8,128)(2,1)S(1)} %get-tuple-element.116), channel_id=1, source_target_pairs={{0,4},{1,5},{2,6},{3,7},{4,0},{5,1},{6,2},{7,3},{8,12},{9,13},{10,... | collective-permute-start | bytes 614408 | tf_op jit(solution)/shard_map/weights/ppermute | solution.py:38
  19.4 22.4 %collective-permute-start.12 = (bf16[4,80,1280]{2,1,0:T(8,128)(2,1)S(1)}, bf16[4,80,1280]{2,1,0:T(8,128)(2,1)S(1)}, u32[]{:S(2)}, u32[]{:S(2)}) collective-permute-start(bf16[4,80,1280]{2,1,0:T(8,128)(2,1)S(1)} %pad_maximum_fusion.1.b0), channel_id=1, source_target_pairs={{0,2},{1,3},{2,4},{3,5},{4,6},{5,7},{6,0},{7,1},{8,10},{9,11},{10,... | collective-permute-start | bytes 2457608 | tf_op jit(solution)/shard_map/weights/ppermute | solution.py:38
  23.8 18.3 %collective-permute-start.11 = (bf16[4,80,1280]{2,1,0:T(8,128)(2,1)S(1)}, bf16[4,80,1280]{2,1,0:T(8,128)(2,1)S(1)}, u32[]{:S(2)}, u32[]{:S(2)}) collective-permute-start(bf16[4,80,1280]{2,1,0:T(8,128)(2,1)S(1)} %pad_maximum_fusion.1.b0), channel_id=1, source_target_pairs={{0,6},{1,7},{2,0},{3,1},{4,2},{5,3},{6,4},{7,5},{8,14},{9,15},{10,... | collective-permute-start | bytes 2457608 | tf_op jit(solution)/shard_map/weights/ppermute | solution.py:38
  26.2 20.2 %collective-permute-start.5 = (bf16[4,80,1280]{2,1,0:T(8,128)(2,1)S(1)}, bf16[4,80,1280]{2,1,0:T(8,128)(2,1)S(1)}, u32[]{:S(2)}, u32[]{:S(2)}) collective-permute-start(bf16[4,80,1280]{2,1,0:T(8,128)(2,1)S(1)} %pad_maximum_fusion.a0), channel_id=1, source_target_pairs={{0,8},{1,9},{2,10},{3,11},{4,12},{5,13},{6,14},{7,15},{8,16},{9,17... | collective-permute-start | bytes 2457608 | tf_op jit(solution)/shard_map/weights/ppermute | solution.py:38
  27.8 20.1 %collective-permute-start.4 = (bf16[4,80,1280]{2,1,0:T(8,128)(2,1)S(1)}, bf16[4,80,1280]{2,1,0:T(8,128)(2,1)S(1)}, u32[]{:S(2)}, u32[]{:S(2)}) collective-permute-start(bf16[4,80,1280]{2,1,0:T(8,128)(2,1)S(1)} %pad_maximum_fusion.a0), channel_id=1, source_target_pairs={{0,24},{1,25},{2,26},{3,27},{4,28},{5,29},{6,30},{7,31},{8,0},{9,1... | collective-permute-start | bytes 2457608 | tf_op jit(solution)/shard_map/weights/ppermute | solution.py:38
  33.0 15.1 %collective-permute-start.15 = (bf16[256,1408]{1,0:T(8,128)(2,1)}, bf16[256,1408]{1,0:T(8,128)(2,1)S(1)}, u32[]{:S(2)}, u32[]{:S(2)}) collective-permute-start(bf16[256,1408]{1,0:T(8,128)(2,1)} %get-tuple-element.50.own), channel_id=1, source_target_pairs={{0,1},{1,0},{2,3},{3,2},{4,5},{5,4},{6,7},{7,6},{8,9},{9,8},{10,11... | collective-permute-start | bytes 2162696 | tf_op jit(solution)/shard_map/prepare/ppermute | solution.py:42
  41.9 13.1 %collective-permute-start.16 = (bf16[256,1664]{1,0:T(8,128)(2,1)}, bf16[256,1664]{1,0:T(8,128)(2,1)}, u32[]{:S(2)}, u32[]{:S(2)}) collective-permute-start(bf16[256,1664]{1,0:T(8,128)(2,1)} %get-tuple-element.51.extra), channel_id=1, source_target_pairs={{0,1},{1,0},{2,3},{3,2},{4,5},{5,4},{6,7},{7,6},{8,9},{9,8},{10,11... | collective-permute-start | bytes 2555912 | tf_op jit(solution)/shard_map/prepare/ppermute | solution.py:42
  42.1 13.0 %collective-permute-start.13 = (bf16[2,80,1280]{2,1,0:T(8,128)(2,1)S(1)}, bf16[2,80,1280]{2,1,0:T(8,128)(2,1)S(1)}, u32[]{:S(2)}, u32[]{:S(2)}) collective-permute-start(bf16[2,80,1280]{2,1,0:T(8,128)(2,1)S(1)} %slice.199), channel_id=1, source_target_pairs={{0,2},{1,3},{2,4},{3,5},{4,6},{5,7},{6,0},{7,1},{8,10},{9,11},{10,... | collective-permute-start | bytes 1228808 | tf_op jit(solution)/shard_map/weights/ppermute | solution.py:38
  46.3 9.3 %collective-permute-start.14 = (bf16[2,80,1280]{2,1,0:T(8,128)(2,1)S(1)}, bf16[2,80,1280]{2,1,0:T(8,128)(2,1)}, u32[]{:S(2)}, u32[]{:S(2)}) collective-permute-start(bf16[2,80,1280]{2,1,0:T(8,128)(2,1)S(1)} %slice.200), channel_id=1, source_target_pairs={{0,6},{1,7},{2,0},{3,1},{4,2},{5,3},{6,4},{7,5},{8,14},{9,15},{10,... | collective-permute-start | bytes 1228808 | tf_op jit(solution)/shard_map/weights/ppermute | solution.py:38
  48.0 10.3 %collective-permute-start.6 = (bf16[2,80,1280]{2,1,0:T(8,128)(2,1)S(1)}, bf16[2,80,1280]{2,1,0:T(8,128)(2,1)S(1)}, u32[]{:S(2)}, u32[]{:S(2)}) collective-permute-start(bf16[2,80,1280]{2,1,0:T(8,128)(2,1)S(1)} %slice.196), channel_id=1, source_target_pairs={{0,8},{1,9},{2,10},{3,11},{4,12},{5,13},{6,14},{7,15},{8,16},{9,17... | collective-permute-start | bytes 1228808 | tf_op jit(solution)/shard_map/weights/ppermute | solution.py:38
  49.1 10.1 %collective-permute-start.7 = (bf16[2,80,1280]{2,1,0:T(8,128)(2,1)S(1)}, bf16[2,80,1280]{2,1,0:T(8,128)(2,1)S(1)}, u32[]{:S(2)}, u32[]{:S(2)}) collective-permute-start(bf16[2,80,1280]{2,1,0:T(8,128)(2,1)S(1)} %slice.197), channel_id=1, source_target_pairs={{0,24},{1,25},{2,26},{3,27},{4,28},{5,29},{6,30},{7,31},{8,0},{9,1... | collective-permute-start | bytes 1228808 | tf_op jit(solution)/shard_map/weights/ppermute | solution.py:38
  60.0 31.6 %all-to-all-start = ((bf16[128,8,640]{2,1,0:T(8,128)(2,1)}), bf16[128,8,640]{2,1,0:T(8,128)(2,1)S(1)}, u32[]{:S(2)}, u32[]{:S(2)}) async-start(bf16[128,8,640]{2,1,0:T(8,128)(2,1)} %bitcast.15), calls=%async_computation | async-start | bytes 2621440 | tf_op jit(solution)/shard_map/grads_in/all_to_all | solution.py:433
  81.2 2.6 %collective-permute-start.17 = (bf16[512,640]{1,0:T(8,128)(2,1)}, bf16[512,640]{1,0:T(8,128)(2,1)S(1)}, u32[]{:S(2)}, u32[]{:S(2)}) collective-permute-start(bf16[512,640]{1,0:T(8,128)(2,1)} %get-tuple-element.63.attended.attended_hbm), channel_id=1, source_target_pairs={{0,1},{1,0},{2,3},{3,2},{4,5},{5,4},{6,7},{7,6},{8,9},{9,8},{10,11... | collective-permute-start | bytes 1966088 | tf_op jit(solution)/shard_map/forward/ppermute | solution.py:42
  98.4 10.0 %collective-permute-start.18 = (bf16[512,640]{1,0:T(8,128)(2,1)}, bf16[512,640]{1,0:T(8,128)(2,1)S(1)}, u32[]{:S(2)}, u32[]{:S(2)}) collective-permute-start(bf16[512,640]{1,0:T(8,128)(2,1)} %get-tuple-element.72), channel_id=1, source_target_pairs={{0,1},{1,0},{2,3},{3,2},{4,5},{5,4},{6,7},{7,6},{8,9},{9,8},{10,11... | collective-permute-start | bytes 1966088 | tf_op jit(solution)/shard_map/grads_in/ppermute | solution.py:42
  98.6 40.1 %all-to-all-start.1 = ((bf16[128,8,640]{2,1,0:T(8,128)(2,1)}), bf16[128,8,640]{2,1,0:T(8,128)(2,1)S(1)}, u32[]{:S(2)}, u32[]{:S(2)}) async-start(bf16[128,8,640]{2,1,0:T(8,128)(2,1)} %bitcast.17), calls=%async_computation.1 | async-start | bytes 2621440 | tf_op jit(solution)/shard_map/rows_out/all_to_all | solution.py:499
  123.8 21.2 %collective-permute-start.19 = (bf16[4,80,1280]{2,1,0:T(8,128)(2,1)}, bf16[4,80,1280]{2,1,0:T(8,128)(2,1)}, u32[]{:S(2)}, u32[]{:S(2)}) collective-permute-start(bf16[4,80,1280]{2,1,0:T(8,128)(2,1)} %get-tuple-element.76), channel_id=1, source_target_pairs={{0,8},{1,9},{2,10},{3,11},{4,12},{5,13},{6,14},{7,15},{8,16},{9,17... | collective-permute-start | bytes 2457608 | tf_op jit(solution)/shard_map/weight_grads/ppermute | solution.py:38
  124.8 20.3 %collective-permute-start.20 = (bf16[4,80,1280]{2,1,0:T(8,128)(2,1)}, bf16[4,80,1280]{2,1,0:T(8,128)(2,1)}, u32[]{:S(2)}, u32[]{:S(2)}) collective-permute-start(bf16[4,80,1280]{2,1,0:T(8,128)(2,1)} %get-tuple-element.77), channel_id=1, source_target_pairs={{0,24},{1,25},{2,26},{3,27},{4,28},{5,29},{6,30},{7,31},{8,0},{9,1... | collective-permute-start | bytes 2457608 | tf_op jit(solution)/shard_map/weight_grads/ppermute | solution.py:38
  127.1 21.0 %collective-permute-start.21 = (bf16[4,80,1280]{2,1,0:T(8,128)(2,1)}, bf16[4,80,1280]{2,1,0:T(8,128)(2,1)S(1)}, u32[]{:S(2)}, u32[]{:S(2)}) collective-permute-start(bf16[4,80,1280]{2,1,0:T(8,128)(2,1)} %get-tuple-element.78), channel_id=1, source_target_pairs={{0,2},{1,3},{2,4},{3,5},{4,6},{5,7},{6,0},{7,1},{8,10},{9,11},{10,... | collective-permute-start | bytes 2457608 | tf_op jit(solution)/shard_map/weight_grads/ppermute | solution.py:38
  128.1 20.0 %collective-permute-start.22 = (bf16[4,80,1280]{2,1,0:T(8,128)(2,1)}, bf16[4,80,1280]{2,1,0:T(8,128)(2,1)S(1)}, u32[]{:S(2)}, u32[]{:S(2)}) collective-permute-start(bf16[4,80,1280]{2,1,0:T(8,128)(2,1)} %get-tuple-element.79), channel_id=1, source_target_pairs={{0,6},{1,7},{2,0},{3,1},{4,2},{5,3},{6,4},{7,5},{8,14},{9,15},{10,... | collective-permute-start | bytes 2457608 | tf_op jit(solution)/shard_map/weight_grads/ppermute | solution.py:38
  138.7 15.1 %copy-start.13 = (bf16[2,80,1280]{2,1,0:T(8,128)(2,1)S(1)}, bf16[2,80,1280]{2,1,0:T(8,128)(2,1)}, u32[]{:S(2)}) copy-start(bf16[2,80,1280]{2,1,0:T(8,128)(2,1)} %get-tuple-element.92) | copy-start | bytes 1228804
  149.3 11.2 %collective-permute-start.25 = (bf16[2,80,1280]{2,1,0:T(8,128)(2,1)S(1)}, bf16[2,80,1280]{2,1,0:T(8,128)(2,1)S(1)}, u32[]{:S(2)}, u32[]{:S(2)}) collective-permute-start(bf16[2,80,1280]{2,1,0:T(8,128)(2,1)S(1)} %add_convert_fusion.5), channel_id=1, source_target_pairs={{0,8},{1,9},{2,10},{3,11},{4,12},{5,13},{6,14},{7,15},{8,16},{9,17... | collective-permute-start | bytes 1228808 | tf_op jit(solution)/shard_map/weight_grads/ppermute | solution.py:38
  150.9 10.3 %collective-permute-start.27 = (bf16[2,80,1280]{2,1,0:T(8,128)(2,1)S(1)}, bf16[2,80,1280]{2,1,0:T(8,128)(2,1)S(1)}, u32[]{:S(2)}, u32[]{:S(2)}) collective-permute-start(bf16[2,80,1280]{2,1,0:T(8,128)(2,1)S(1)} %add_convert_fusion.4), channel_id=1, source_target_pairs={{0,24},{1,25},{2,26},{3,27},{4,28},{5,29},{6,30},{7,31},{8,0},{9,1... | collective-permute-start | bytes 1228808 | tf_op jit(solution)/shard_map/weight_grads/ppermute | solution.py:38
  153.9 12.9 %collective-permute-start.30 = (bf16[2,80,1280]{2,1,0:T(8,128)(2,1)S(1)}, bf16[2,80,1280]{2,1,0:T(8,128)(2,1)S(1)}, u32[]{:S(2)}, u32[]{:S(2)}) collective-permute-start(bf16[2,80,1280]{2,1,0:T(8,128)(2,1)S(1)} %add_convert_fusion.2), channel_id=1, source_target_pairs={{0,2},{1,3},{2,4},{3,5},{4,6},{5,7},{6,0},{7,1},{8,10},{9,11},{10,... | collective-permute-start | bytes 1228808 | tf_op jit(solution)/shard_map/weight_grads/ppermute | solution.py:38
  155.6 11.3 %collective-permute-start.32 = (bf16[2,80,1280]{2,1,0:T(8,128)(2,1)S(1)}, bf16[2,80,1280]{2,1,0:T(8,128)(2,1)S(1)}, u32[]{:S(2)}, u32[]{:S(2)}) collective-permute-start(bf16[2,80,1280]{2,1,0:T(8,128)(2,1)S(1)} %add_convert_fusion.1), channel_id=1, source_target_pairs={{0,6},{1,7},{2,0},{3,1},{4,2},{5,3},{6,4},{7,5},{8,14},{9,15},{10,... | collective-permute-start | bytes 1228808 | tf_op jit(solution)/shard_map/weight_grads/ppermute | solution.py:38
  162.7 10.2 %collective-permute-start.28 = (bf16[80,1280]{1,0:T(8,128)(2,1)S(1)}, bf16[80,1280]{1,0:T(8,128)(2,1)S(1)}, u32[]{:S(2)}, u32[]{:S(2)}) collective-permute-start(bf16[80,1280]{1,0:T(8,128)(2,1)S(1)} %get-tuple-element.109), channel_id=1, source_target_pairs={{0,6},{1,7},{2,0},{3,1},{4,2},{5,3},{6,4},{7,5},{8,14},{9,15},{10,... | collective-permute-start | bytes 614408 | tf_op jit(solution)/shard_map/weight_grads/ppermute | solution.py:38
  165.2 8.0 %collective-permute-start.29 = (bf16[80,1280]{1,0:T(8,128)(2,1)S(1)}, bf16[80,1280]{1,0:T(8,128)(2,1)S(1)}, u32[]{:S(2)}, u32[]{:S(2)}) collective-permute-start(bf16[80,1280]{1,0:T(8,128)(2,1)S(1)} %get-tuple-element.110), channel_id=1, source_target_pairs={{0,4},{1,5},{2,6},{3,7},{4,0},{5,1},{6,2},{7,3},{8,12},{9,13},{10,... | collective-permute-start | bytes 614408 | tf_op jit(solution)/shard_map/weight_grads/ppermute | solution.py:38
  165.9 9.3 %collective-permute-start.26 = (bf16[80,1280]{1,0:T(8,128)(2,1)S(1)}, bf16[80,1280]{1,0:T(8,128)(2,1)S(1)}, u32[]{:S(2)}, u32[]{:S(2)}) collective-permute-start(bf16[80,1280]{1,0:T(8,128)(2,1)S(1)} %fusion.9), channel_id=1, source_target_pairs={{0,2},{1,3},{2,4},{3,5},{4,6},{5,7},{6,0},{7,1},{8,10},{9,11},{10,... | collective-permute-start | bytes 614408 | tf_op jit(solution)/shard_map/weight_grads/ppermute | solution.py:38
  167.2 9.2 %collective-permute-start.33 = (bf16[80,1280]{1,0:T(8,128)(2,1)S(1)}, bf16[80,1280]{1,0:T(8,128)(2,1)S(1)}, u32[]{:S(2)}, u32[]{:S(2)}) collective-permute-start(bf16[80,1280]{1,0:T(8,128)(2,1)S(1)} %get-tuple-element.111), channel_id=1, source_target_pairs={{0,24},{1,25},{2,26},{3,27},{4,28},{5,29},{6,30},{7,31},{8,0},{9,1... | collective-permute-start | bytes 614408 | tf_op jit(solution)/shard_map/weight_grads/ppermute | solution.py:38
  170.9 7.3 %collective-permute-start.34 = (bf16[80,1280]{1,0:T(8,128)(2,1)S(1)}, bf16[80,1280]{1,0:T(8,128)(2,1)S(1)}, u32[]{:S(2)}, u32[]{:S(2)}) collective-permute-start(bf16[80,1280]{1,0:T(8,128)(2,1)S(1)} %get-tuple-element.112), channel_id=1, source_target_pairs={{0,16},{1,17},{2,18},{3,19},{4,20},{5,21},{6,22},{7,23},{8,24},{9,... | collective-permute-start | bytes 614408 | tf_op jit(solution)/shard_map/weight_grads/ppermute | solution.py:38
  172.8 7.6 %collective-permute-start.31 = (bf16[80,1280]{1,0:T(8,128)(2,1)S(1)}, bf16[80,1280]{1,0:T(8,128)(2,1)S(1)}, u32[]{:S(2)}, u32[]{:S(2)}) collective-permute-start(bf16[80,1280]{1,0:T(8,128)(2,1)S(1)} %fusion.10), channel_id=1, source_target_pairs={{0,8},{1,9},{2,10},{3,11},{4,12},{5,13},{6,14},{7,15},{8,16},{9,17... | collective-permute-start | bytes 614408 | tf_op jit(solution)/shard_map/weight_grads/ppermute | solution.py:38
  180.5 1.5 collective-permute-start.35
  180.7 15.3 %collective-permute-start.23 = (bf16[256,1280]{1,0:T(8,128)(2,1)}, bf16[256,1280]{1,0:T(8,128)(2,1)}, u32[]{:S(2)}, u32[]{:S(2)}) collective-permute-start(bf16[256,1280]{1,0:T(8,128)(2,1)} %get-tuple-element.85), channel_id=1, source_target_pairs={{0,1},{1,0},{2,3},{3,2},{4,5},{5,4},{6,7},{7,6},{8,9},{9,8},{10,11... | collective-permute-start | bytes 1966088 | tf_op jit(solution)/shard_map/norm_grad/ppermute | solution.py:42
  182.4 6.2 %collective-permute-start.36 = (bf16[40,1280]{1,0:T(8,128)(2,1)S(1)}, bf16[40,1280]{1,0:T(8,128)(2,1)S(1)}, u32[]{:S(2)}, u32[]{:S(2)}) collective-permute-start(bf16[40,1280]{1,0:T(8,128)(2,1)S(1)} %get-tuple-element.106), channel_id=1, source_target_pairs={{0,32},{32,64},{64,96},{96,0},{1,33},{33,65},{65,97},{97,1},{2,34}... | collective-permute-start | bytes 307208 | tf_op jit(solution)/shard_map/over_groups/ppermute | solution.py:37
  184.0 6.1 %collective-permute-start.37 = (bf16[40,1280]{1,0:T(8,128)(2,1)S(1)}, bf16[40,1280]{1,0:T(8,128)(2,1)S(1)}, u32[]{:S(2)}, u32[]{:S(2)}) collective-permute-start(bf16[40,1280]{1,0:T(8,128)(2,1)S(1)} %get-tuple-element.108), channel_id=1, source_target_pairs={{0,96},{32,0},{64,32},{96,64},{1,97},{33,1},{65,33},{97,65},{2,98}... | collective-permute-start | bytes 307208 | tf_op jit(solution)/shard_map/over_groups/ppermute | solution.py:37
  185.7 6.2 %collective-permute-start.38 = (bf16[40,1280]{1,0:T(8,128)(2,1)S(1)}, bf16[40,1280]{1,0:T(8,128)(2,1)S(1)}, u32[]{:S(2)}, u32[]{:S(2)}) collective-permute-start(bf16[40,1280]{1,0:T(8,128)(2,1)S(1)} %get-tuple-element.107), channel_id=1, source_target_pairs={{0,64},{32,96},{64,0},{96,32},{1,65},{33,97},{65,1},{97,33},{2,66}... | collective-permute-start | bytes 307208 | tf_op jit(solution)/shard_map/over_groups/ppermute | solution.py:37
  187.7 8.3 %collective-permute-start.24 = (bf16[256,640]{1,0:T(8,128)(2,1)S(1)}, bf16[256,640]{1,0:T(8,128)(2,1)S(1)}, u32[]{:S(2)}, u32[]{:S(2)}) collective-permute-start(bf16[256,640]{1,0:T(8,128)(2,1)S(1)} %slice.164), channel_id=1, source_target_pairs={{0,1},{1,0},{2,3},{3,2},{4,5},{5,4},{6,7},{7,6},{8,9},{9,8},{10,11... | collective-permute-start | bytes 983048 | tf_op jit(solution)/shard_map/norm_grad/ppermute | solution.py:42
  192.0 8.6 %collective-permute-start.39 = (bf16[40,1280]{1,0:T(8,128)(2,1)S(1)}, bf16[40,1280]{1,0:T(8,128)(2,1)S(1)}, u32[]{:S(2)}, u32[]{:S(2)}) collective-permute-start(bf16[40,1280]{1,0:T(8,128)(2,1)S(1)} %fusion.13), channel_id=1, source_target_pairs={{0,96},{32,0},{64,32},{96,64},{1,97},{33,1},{65,33},{97,65},{2,98}... | collective-permute-start | bytes 307208 | tf_op jit(solution)/shard_map/over_groups/ppermute | solution.py:37
  193.9 7.0 %collective-permute-start.40 = (bf16[40,1280]{1,0:T(8,128)(2,1)S(1)}, bf16[40,1280]{1,0:T(8,128)(2,1)S(1)}, u32[]{:S(2)}, u32[]{:S(2)}) collective-permute-start(bf16[40,1280]{1,0:T(8,128)(2,1)S(1)} %fusion.13), channel_id=1, source_target_pairs={{0,32},{32,64},{64,96},{96,0},{1,33},{33,65},{65,97},{97,1},{2,34}... | collective-permute-start | bytes 307208 | tf_op jit(solution)/shard_map/over_groups/ppermute | solution.py:37
  194.1 6.8 %collective-permute-start.41 = (bf16[40,1280]{1,0:T(8,128)(2,1)S(1)}, bf16[40,1280]{1,0:T(8,128)(2,1)S(1)}, u32[]{:S(2)}, u32[]{:S(2)}) collective-permute-start(bf16[40,1280]{1,0:T(8,128)(2,1)S(1)} %fusion.13), channel_id=1, source_target_pairs={{0,64},{32,96},{64,0},{96,32},{1,65},{33,97},{65,1},{97,33},{2,66}... | collective-permute-start | bytes 307208 | tf_op jit(solution)/shard_map/over_groups/ppermute | solution.py:37
  (19 other events, 104.4 us)

commit v4 on v3

--- a/solution.py
+++ b/solution.py
@@ -293,16 +293,28 @@
         copies.start(ga_other.at[pl.ds(ROWS, ROWS)], gb.at[pl.ds(0, ROWS)]),
         copies.start(ga_other.at[pl.ds(0, ROWS)], gb.at[pl.ds(ROWS, ROWS)]),
     ]
-    first_in = [copies.start(qkv_hbm, qkv), copies.start(probs_hbm, probs)]
     second_in = [
         copies.start(attended_hbm, attended),
         copies.start(other_hbm.at[pl.ds(ROWS, ROWS)], other.at[pl.ds(0, ROWS)]),
         copies.start(other_hbm.at[pl.ds(0, ROWS)], other.at[pl.ds(ROWS, ROWS)]),
-        copies.start(normed_hbm, normed_t),
         copies.start(grads_hbm, grads),
     ]
+    first_in = [copies.start(qkv_hbm, qkv), copies.start(probs_hbm, probs)]
+    last_in = copies.start(normed_hbm, normed_t)
     wait_all(grads_in)
     gatt[...] = (ga[...] + gb[...].astype(F32)).astype(BF)
+    wait_all(second_in)
+    attended_t[at_rows(place[2], HALF), :] = attended[...].T
+    attended_t[at_rows(1 - place[2], HALF), :] = other[...].T
+    for r in range(5):
+        rows = slice(r * 256, (r + 1) * 256)
+        oterms[rows, :] = dot(attended_t[rows, :], grads[...]).astype(BF)
+
+    out_copies = assemble(
+        place, (bown, bup, bdown, blow, bhigh), "x",
+        lambda ref, x, z: [copies.start(oterms.at[at_rows(x * 4 + z, 80)], ref.at[:, pl.ds(640, 640)])],
+        scatter=True,
+    )
     scale = HD ** (-0.5)
     wait_all(first_in)
 
@@ -328,8 +340,8 @@
         gqkv[rows, HALF:2 * HALF] = jnp.concatenate(to_key, axis=1)
         gqkv[rows, 2 * HALF:] = jnp.concatenate(to_value, axis=1)
 
-    out_copies = [copies.start(gqkv, gqkv_out)]
-    wait_all(second_in)
+    out_copies.append(copies.start(gqkv, gqkv_out))
+    last_in.wait()
 
     def weigh(col):
         terms[:, col] = dot(normed_t[...], gqkv[:, col]).astype(BF)
@@ -351,17 +363,6 @@
         lambda ref, x, z: [
             copies.start(terms.at[at_rows(x * 4 + z, 80), pl.ds(1280, 640)], ref.at[:, pl.ds(0, 640)])
         ],
-        scatter=True,
-    )
-    attended_t[at_rows(place[2], HALF), :] = attended[...].T
-    attended_t[at_rows(1 - place[2], HALF), :] = other[...].T
-    for r in range(5):
-        rows = slice(r * 256, (r + 1) * 256)
-        oterms[rows, :] = dot(attended_t[rows, :], grads[...]).astype(BF)
-
-    out_copies += assemble(
-        place, (bown, bup, bdown, blow, bhigh), "x",
-        lambda ref, x, z: [copies.start(oterms.at[at_rows(x * 4 + z, 80)], ref.at[:, pl.ds(640, 640)])],
         scatter=True,
     )
     wait_all(out_copies)
@@ -497,7 +498,6 @@
         )
     with jax.named_scope("rows_out"):
         owner_rows = lax.all_to_all(outgoing, ("grp", "enc"), split_axis=0, concat_axis=0, tiled=True)
-        owner_rows = owner_rows.reshape(64, 2, 8, HALF).transpose(0, 2, 1, 3).reshape(512, D)
     with jax.named_scope("weight_grads"):
         up_a, down_a = scatter_first(*terms[1:3], "x")
         up_b, down_b = scatter_first(*terms[6:8], "z")
@@ -513,9 +513,7 @@
             us=1,
         )
     with jax.named_scope("weight_grads"):
-        up_a, down_a, up_b, down_b, ntheirs, owner_rows = lax.optimization_barrier(
-            (up_a, down_a, up_b, down_b, ntheirs, owner_rows)
-        )
+        up_a, down_a, ntheirs, owner_rows = lax.optimization_barrier((up_a, down_a, ntheirs, owner_rows))
         sum_a = scatter_second(terms[0], up_a, down_a, *terms[3:5], "x", "z")
         sum_b = scatter_second(terms[5], up_b, down_b, *terms[8:], "z", "x")
     with jax.named_scope("norm_grad"):
@@ -536,6 +534,9 @@
         blocks = jnp.stack(
             [jnp.concatenate([low[:, t * HALF : (t + 1) * HALF], high[:, t * HALF : (t + 1) * HALF]], axis=1) for t in range(4)]
         )
+    with jax.named_scope("rows_out"):
+        owner_rows = owner_rows.reshape(64, 2, 8, HALF).transpose(0, 2, 1, 3).reshape(512, D)
+        blocks, owner_rows = lax.optimization_barrier((blocks, owner_rows))
     with jax.named_scope("over_groups"):
         me = lax.axis_index("grp")
 

time: 205 us -> 203 us (level)
    ppermute x28, waiting for transfers between devices: 40.7 us -> 38.7 us  [hop(): return lax.ppermute(value, 'enc', ring(axis, step))]
  transfers between devices with their start and end apart: 44 -> 44, of which waited for: 26 -> 25; matrix products, arithmetic and copies ran while one was open for 3% -> 4% of each run, Pallas kernels for 26% -> 26%
where the time goes in v4:
time: 203 us; the launch traced here: 202 us
  starting transfers between devices  77.9 us (38%)
  Pallas kernels  57.8 us (28%)
  waiting for transfers between devices  47.9 us (24%)
  local copies, waits for them, and re-layouts  10.1 us (5%)
  other arithmetic  7.41 us (4%)
    pallas_call x8, Pallas kernels, call(): pl.pallas_call(kernel, out_shape=[jax.ShapeDtypeStruct(s, t) for s, t in...  57.8 us
    ppermute x28, starting transfers between devices, hop(): return lax.ppermute(value, 'enc', ring(axis, step))  48.9 us
    ppermute x28, waiting for transfers between devices, hop(): return lax.ppermute(value, 'enc', ring(axis, step))  38.7 us
    all_to_all x1, starting transfers between devices, body(): lax.all_to_all(outgoing, ('grp', 'enc'), split_axis=0, concat_axis=0, til...  9.79 us
    ppermute x6, starting transfers between devices, hop(): return lax.ppermute(value, 'grp', [(i, (i + step) % 4) for i in range(4)])  9.08 us
    all_to_all x1, starting transfers between devices, body(): lax.all_to_all(sent, ('grp', 'enc'), split_axis=0, concat_axis=0, tiled=T...  8.88 us
    unnamed x48, local copies, waits for them, and re-layouts  7.27 us
    ppermute x8, waiting for transfers between devices, to_sibling(): return lax.ppermute(value, 'enc', [(i, i ^ 1) for i in range(32)])  4.69 us
  transfers between devices with their start and end apart: 44, of which 25 were waited for; matrix products, arithmetic and copies ran while one was open for 4% of the time, Pallas kernels for 26%

profile of v4, /device:TPU:0, one launch (start us, length us, event | category | flops | bytes accessed | tf_op | source)
XLA Modules:
  0.0 202.3 jit_solution(16596438306815586018)
XLA Ops:
  1.8 1.4 collective-permute-done
  3.5 2.9 %collective-permute-start.8 = (bf16[80,1280]{1,0:T(8,128)(2,1)S(1)}, bf16[80,1280]{1,0:T(8,128)(2,1)S(1)}, u32[]{:S(2)}, u32[]{:S(2)}) collective-permute-start(bf16[80,1280]{1,0:T(8,128)(2,1)S(1)} %get-tuple-element.115), channel_id=1, source_target_pairs={{0,24},{1,25},{2,26},{3,27},{4,28},{5,29},{6,30},{7,31},{8,0},{9,1... | collective-permute-start | bytes 614408 | tf_op jit(solution)/shard_map/weights/ppermute | solution.py:38
  6.4 2.3 %collective-permute-start.10 = (bf16[80,1280]{1,0:T(8,128)(2,1)S(1)}, bf16[80,1280]{1,0:T(8,128)(2,1)S(1)}, u32[]{:S(2)}, u32[]{:S(2)}) collective-permute-start(bf16[80,1280]{1,0:T(8,128)(2,1)S(1)} %get-tuple-element.115), channel_id=1, source_target_pairs={{0,16},{1,17},{2,18},{3,19},{4,20},{5,21},{6,22},{7,23},{8,24},{9,... | collective-permute-start | bytes 614408 | tf_op jit(solution)/shard_map/weights/ppermute | solution.py:38
  8.7 4.0 %collective-permute-start.1 = (bf16[80,1280]{1,0:T(8,128)(2,1)S(1)}, bf16[80,1280]{1,0:T(8,128)(2,1)S(1)}, u32[]{:S(2)}, u32[]{:S(2)}) collective-permute-start(bf16[80,1280]{1,0:T(8,128)(2,1)S(1)} %get-tuple-element.116), channel_id=1, source_target_pairs={{0,6},{1,7},{2,0},{3,1},{4,2},{5,3},{6,4},{7,5},{8,14},{9,15},{10,... | collective-permute-start | bytes 614408 | tf_op jit(solution)/shard_map/weights/ppermute | solution.py:38
  12.7 2.7 %collective-permute-done.8 = bf16[80,1280]{1,0:T(8,128)(2,1)S(1)} collective-permute-done((bf16[80,1280]{1,0:T(8,128)(2,1)S(1)}, bf16[80,1280]{1,0:T(8,128)(2,1)S(1)}, u32[]{:S(2)}, u32[]{:S(2)}) %collective-permute-start.8) | collective-permute-done | bytes 204832 | tf_op jit(solution)/shard_map/weights/ppermute | solution.py:38
  15.4 3.9 %collective-permute-start.3 = (bf16[80,1280]{1,0:T(8,128)(2,1)S(1)}, bf16[80,1280]{1,0:T(8,128)(2,1)S(1)}, u32[]{:S(2)}, u32[]{:S(2)}) collective-permute-start(bf16[80,1280]{1,0:T(8,128)(2,1)S(1)} %get-tuple-element.116), channel_id=1, source_target_pairs={{0,4},{1,5},{2,6},{3,7},{4,0},{5,1},{6,2},{7,3},{8,12},{9,13},{10,... | collective-permute-start | bytes 614408 | tf_op jit(solution)/shard_map/weights/ppermute | solution.py:38
  19.4 1.5 collective-permute-start.12
  23.8 2.3 %collective-permute-start.11 = (bf16[4,80,1280]{2,1,0:T(8,128)(2,1)S(1)}, bf16[4,80,1280]{2,1,0:T(8,128)(2,1)S(1)}, u32[]{:S(2)}, u32[]{:S(2)}) collective-permute-start(bf16[4,80,1280]{2,1,0:T(8,128)(2,1)S(1)} %pad_maximum_fusion.1.b0), channel_id=1, source_target_pairs={{0,6},{1,7},{2,0},{3,1},{4,2},{5,3},{6,4},{7,5},{8,14},{9,15},{10,... | collective-permute-start | bytes 2457608 | tf_op jit(solution)/shard_map/weights/ppermute | solution.py:38
  26.2 1.7 collective-permute-start.5
  27.8 1.7 collective-permute-start.4
  29.5 3.5 %prepare.2 = (bf16[256,1408]{1,0:T(8,128)(2,1)}, bf16[256,1664]{1,0:T(8,128)(2,1)}, bf16[256,1280]{1,0:T(8,128)(2,1)}) custom-call(s32[3]{0:T(128)} %pad_add_fusion.place, s32[1,4]{1,0:T(1,128)} %counts.1, bf16[256,1280]{1,0:T(8,128)(2,1)} %patches.1, f32[1,1280]{1,0:T(1,128)} %reshape.37.gain, s32[256,1]{1,0:T(8,128)} %copy.13.order, s32[256,1]{1,0:T(8,128)} %copy.14.owners), custom_call_target="tpu_custom_call" | custom-call | flops 3000000000 | bytes 9000000 | tf_op jit(solution)/shard_map/prepare/pallas_call | solution.py:97
  33.1 8.7 %collective-permute-done.12.b2 = bf16[4,80,1280]{2,1,0:T(8,128)(2,1)S(1)} collective-permute-done((bf16[4,80,1280]{2,1,0:T(8,128)(2,1)S(1)}, bf16[4,80,1280]{2,1,0:T(8,128)(2,1)S(1)}, u32[]{:S(2)}, u32[]{:S(2)}) %collective-permute-start.12) | collective-permute-done | bytes 819232 | tf_op jit(solution)/shard_map/weights/ppermute | solution.py:38
  42.1 1.5 collective-permute-start.13
  43.7 2.7 %collective-permute-done.5.a2 = bf16[4,80,1280]{2,1,0:T(8,128)(2,1)S(1)} collective-permute-done((bf16[4,80,1280]{2,1,0:T(8,128)(2,1)S(1)}, bf16[4,80,1280]{2,1,0:T(8,128)(2,1)S(1)}, u32[]{:S(2)}, u32[]{:S(2)}) %collective-permute-start.5) | collective-permute-done | bytes 819232 | tf_op jit(solution)/shard_map/weights/ppermute | solution.py:38
  46.3 1.6 collective-permute-start.14
  49.1 3.0 %collective-permute-start.7 = (bf16[2,80,1280]{2,1,0:T(8,128)(2,1)S(1)}, bf16[2,80,1280]{2,1,0:T(8,128)(2,1)S(1)}, u32[]{:S(2)}, u32[]{:S(2)}) collective-permute-start(bf16[2,80,1280]{2,1,0:T(8,128)(2,1)S(1)} %slice.197), channel_id=1, source_target_pairs={{0,24},{1,25},{2,26},{3,27},{4,28},{5,29},{6,30},{7,31},{8,0},{9,1... | collective-permute-start | bytes 1228808 | tf_op jit(solution)/shard_map/weights/ppermute | solution.py:38
  52.2 2.8 %prepare.3.normed_hbm = bf16[1280,512]{1,0:T(8,128)(2,1)} custom-call(bf16[256,1408]{1,0:T(8,128)(2,1)} %get-tuple-element.50.own, bf16[256,1408]{1,0:T(8,128)(2,1)} %copy-done.21), custom_call_target="tpu_custom_call" | custom-call | flops 3000000000 | bytes 9000000 | tf_op jit(solution)/shard_map/prepare/pallas_call | solution.py:97
  55.6 2.6 %collective-permute-done.6.a3 = bf16[2,80,1280]{2,1,0:T(8,128)(2,1)S(1)} collective-permute-done((bf16[2,80,1280]{2,1,0:T(8,128)(2,1)S(1)}, bf16[2,80,1280]{2,1,0:T(8,128)(2,1)S(1)}, u32[]{:S(2)}, u32[]{:S(2)}) %collective-permute-start.6) | collective-permute-done | bytes 409632 | tf_op jit(solution)/shard_map/weights/ppermute | solution.py:38
  60.0 8.9 %all-to-all-start = ((bf16[128,8,640]{2,1,0:T(8,128)(2,1)}), bf16[128,8,640]{2,1,0:T(8,128)(2,1)S(1)}, u32[]{:S(2)}, u32[]{:S(2)}) async-start(bf16[128,8,640]{2,1,0:T(8,128)(2,1)} %bitcast.15), calls=%async_computation | async-start | bytes 2621440 | tf_op jit(solution)/shard_map/grads_in/all_to_all | solution.py:434
  68.9 12.3 %forward.2 = (f32[4,8,128,128]{3,2,1,0:T(8,128)}, bf16[512,1920]{1,0:T(8,128)(2,1)}, bf16[512,640]{1,0:T(8,128)(2,1)}) custom-call(s32[3]{0:T(128)} %pad_add_fusion.place, bf16[256,1408]{1,0:T(8,128)(2,1)} %get-tuple-element.50.own, bf16[256,1408]{1,0:T(8,128)(2,1)} %copy-done.21, bf16[4,80,1280]{2,1,0:T(8,128)(2,1)} %copy-done.1, ...), custom_call_target="tpu_custom_call" | custom-call | flops 12000000000 | bytes 36000000 | tf_op jit(solution)/shard_map/forward/pallas_call | solution.py:97
  81.5 2.3 %collective-permute-done.17.other.other_hbm = bf16[512,640]{1,0:T(8,128)(2,1)S(1)} collective-permute-done((bf16[512,640]{1,0:T(8,128)(2,1)}, bf16[512,640]{1,0:T(8,128)(2,1)S(1)}, u32[]{:S(2)}, u32[]{:S(2)}) %collective-permute-start.17) | collective-permute-done | bytes 655392 | tf_op jit(solution)/shard_map/forward/ppermute | solution.py:42
  84.7 7.0 %forward.3 = bf16[1024,640]{1,0:T(8,128)(2,1)} custom-call(s32[3]{0:T(128)} %pad_add_fusion.place, bf16[512,640]{1,0:T(8,128)(2,1)} %get-tuple-element.63.attended.attended_hbm, bf16[512,640]{1,0:T(8,128)(2,1)} %copy-done.10, bf16[256,1280]{1,0:T(8,128)(2,1)} %get-tuple-element.64.ordered, bf16[256,1664]{1,0:T(8,128)(2,1)} %get-tuple-element.51.extra, ...), custom_call_target="tpu_custom_call" | custom-call | flops 3000000000 | bytes 9000000 | tf_op jit(solution)/shard_map/forward/pallas_call | solution.py:97
  92.7 5.7 %grads_in.1 = (bf16[512,640]{1,0:T(8,128)(2,1)}, f32[512,640]{1,0:T(8,128)}, bf16[512,640]{1,0:T(8,128)(2,1)}) custom-call(s32[3]{0:T(128)} %pad_add_fusion.place, bf16[1024,640]{1,0:T(8,128)(2,1)} %bitcast.79, bf16[256,1664]{1,0:T(8,128)(2,1)} %get-tuple-element.51.extra, bf16[256,1664]{1,0:T(8,128)(2,1)} %collective-permute-done.16.sib_extra, ...), custom_call_target="tpu_custom_call" | custom-call | flops 3000000000 | bytes 9000000 | tf_op jit(solution)/shard_map/grads_in/pallas_call | solution.py:97
  98.6 9.8 %all-to-all-start.1 = ((bf16[128,8,640]{2,1,0:T(8,128)(2,1)}), bf16[128,8,640]{2,1,0:T(8,128)(2,1)S(1)}, u32[]{:S(2)}, u32[]{:S(2)}) async-start(bf16[128,8,640]{2,1,0:T(8,128)(2,1)} %bitcast.17), calls=%async_computation.1 | async-start | bytes 2621440 | tf_op jit(solution)/shard_map/rows_out/all_to_all | solution.py:500
  109.3 14.2 %backward.1 = (bf16[512,1920]{1,0:T(8,128)(2,1)}, bf16[4,80,1280]{2,1,0:T(8,128)(2,1)}, bf16[4,80,1280]{2,1,0:T(8,128)(2,1)}, bf16[4,80,1280]{2,1,0:T(8,128)(2,1...) custom-call(s32[3]{0:T(128)} %pad_add_fusion.place, ...), custom_call_target="tpu_custom_call" | custom-call | flops 1000000000 | bytes 3000000 | tf_op jit(solution)/shard_map/backward/pallas_call | solution.py:97
  124.5 2.3 %collective-permute-start.20 = (bf16[4,80,1280]{2,1,0:T(8,128)(2,1)}, bf16[4,80,1280]{2,1,0:T(8,128)(2,1)}, u32[]{:S(2)}, u32[]{:S(2)}) collective-permute-start(bf16[4,80,1280]{2,1,0:T(8,128)(2,1)} %get-tuple-element.79), channel_id=1, source_target_pairs={{0,24},{1,25},{2,26},{3,27},{4,28},{5,29},{6,30},{7,31},{8,0},{9,1... | collective-permute-start | bytes 2457608 | tf_op jit(solution)/shard_map/weight_grads/ppermute | solution.py:38
  127.9 2.2 %collective-permute-start.28 = (bf16[4,80,1280]{2,1,0:T(8,128)(2,1)}, bf16[4,80,1280]{2,1,0:T(8,128)(2,1)S(1)}, u32[]{:S(2)}, u32[]{:S(2)}) collective-permute-start(bf16[4,80,1280]{2,1,0:T(8,128)(2,1)} %get-tuple-element.89), channel_id=1, source_target_pairs={{0,6},{1,7},{2,0},{3,1},{4,2},{5,3},{6,4},{7,5},{8,14},{9,15},{10,... | collective-permute-start | bytes 2457608 | tf_op jit(solution)/shard_map/weight_grads/ppermute | solution.py:38
  130.1 8.4 %norm_grad.2 = (f32[256,1280]{1,0:T(8,128)}, bf16[256,1280]{1,0:T(8,128)(2,1)}) custom-call(s32[3]{0:T(128)} %pad_add_fusion.place, bf16[512,1920]{1,0:T(8,128)(2,1)} %get-tuple-element.80.gqkv, bf16[4,80,1280]{2,1,0:T(8,128)(2,1)} %copy-done.1, bf16[4,80,1280]{2,1,0:T(8,128)(2,1)} %copy-done.5, bf16[4,80,1280]{2,1,0:T(8,128)(2,1)} %copy-done.4, ...), custom_call_target="tpu_custom_call" | custom-call | flops 1000000000 | bytes 3000000 | tf_op jit(solution)/shard_map/norm_grad/pallas_call | solution.py:97
  138.5 6.2 %collective-permute-done.19 = bf16[4,80,1280]{2,1,0:T(8,128)(2,1)} collective-permute-done((bf16[4,80,1280]{2,1,0:T(8,128)(2,1)}, bf16[4,80,1280]{2,1,0:T(8,128)(2,1)}, u32[]{:S(2)}, u32[]{:S(2)}) %collective-permute-start.19) | collective-permute-done | bytes 819232 | tf_op jit(solution)/shard_map/weight_grads/ppermute | solution.py:38
  146.1 1.5 collective-permute-start.21
  148.8 1.8 collective-permute-start.23
  150.7 1.7 collective-permute-start.27
  152.5 1.8 collective-permute-start.30
  154.4 3.4 %collective-permute-done.21 = bf16[2,80,1280]{2,1,0:T(8,128)(2,1)S(1)} collective-permute-done((bf16[2,80,1280]{2,1,0:T(8,128)(2,1)S(1)}, bf16[2,80,1280]{2,1,0:T(8,128)(2,1)S(1)}, u32[]{:S(2)}, u32[]{:S(2)}) %collective-permute-start.21) | collective-permute-done | bytes 409632 | tf_op jit(solution)/shard_map/weight_grads/ppermute | solution.py:38
  160.4 3.4 %collective-permute-start.24 = (bf16[80,1280]{1,0:T(8,128)(2,1)S(1)}, bf16[80,1280]{1,0:T(8,128)(2,1)S(1)}, u32[]{:S(2)}, u32[]{:S(2)}) collective-permute-start(bf16[80,1280]{1,0:T(8,128)(2,1)S(1)} %get-tuple-element.109), channel_id=1, source_target_pairs={{0,6},{1,7},{2,0},{3,1},{4,2},{5,3},{6,4},{7,5},{8,14},{9,15},{10,... | collective-permute-start | bytes 614408 | tf_op jit(solution)/shard_map/weight_grads/ppermute | solution.py:38
  165.7 3.4 %collective-permute-start.31 = (bf16[80,1280]{1,0:T(8,128)(2,1)S(1)}, bf16[80,1280]{1,0:T(8,128)(2,1)S(1)}, u32[]{:S(2)}, u32[]{:S(2)}) collective-permute-start(bf16[80,1280]{1,0:T(8,128)(2,1)S(1)} %get-tuple-element.111), channel_id=1, source_target_pairs={{0,24},{1,25},{2,26},{3,27},{4,28},{5,29},{6,30},{7,31},{8,0},{9,1... | collective-permute-start | bytes 614408 | tf_op jit(solution)/shard_map/weight_grads/ppermute | solution.py:38
  169.1 2.0 collective-permute-done.24
  172.2 1.9 collective-permute-done.22
  175.3 1.7 collective-permute-done.32
  176.9 2.1 %collective-permute-done.29 = bf16[80,1280]{1,0:T(8,128)(2,1)S(1)} collective-permute-done((bf16[80,1280]{1,0:T(8,128)(2,1)S(1)}, bf16[80,1280]{1,0:T(8,128)(2,1)S(1)}, u32[]{:S(2)}, u32[]{:S(2)}) %collective-permute-start.29) | collective-permute-done | bytes 204832 | tf_op jit(solution)/shard_map/weight_grads/ppermute | solution.py:38
  181.1 1.6 collective-permute-start.36
  182.6 1.7 collective-permute-start.37
  184.4 1.8 collective-permute-start.38
  187.3 1.5 collective-permute-done.37
  188.8 1.8 collective-permute-done.38
  190.6 2.0 collective-permute-start.39
  192.7 1.8 collective-permute-start.41
  195.3 4.0 %norm_grad.3 = bf16[256,1280]{1,0:T(8,128)(2,1)} custom-call(s32[3]{0:T(128)} %pad_add_fusion.place, f32[256,1280]{1,0:T(8,128)} %get-tuple-element.93.mine, bf16[256,1280]{1,0:T(8,128)(2,1)} %collective-permute-done.34.theirs, bf16[256,1280]{1,0:T(8,128)(2,1)} %get-tuple-element.64.ordered, f32[1,1280]{1,0:T(1,128)} %reshape.37.gain, ...), custom_call_target="tpu_custom_call" | custom-call | flops 3000000000 | bytes 9000000 | tf_op jit(solution)/shard_map/norm_grad/pallas_call | solution.py:97
  (135 shorter events, 30.0 us)
Async XLA Ops:
  1.8 1.5 collective-permute-start
  3.4 18.2 %copy-start.18 = (f32[1280]{0:T(1024)S(1)}, f32[1280]{0:T(1024)}, u32[]{:S(2)}) copy-start(f32[1280]{0:T(1024)} %param.9) | copy-start | bytes 15364
  3.4 18.8 %copy-start.20 = (s32[2,128]{1,0:T(2,128)S(1)}, s32[2,128]{1,0:T(2,128)}, u32[]{:S(2)}) copy-start(s32[2,128]{1,0:T(2,128)} %param.13) | copy-start | bytes 3076
  3.4 19.6 %copy-start.19 = (s32[256,1]{0,1:T(1,128)S(1)}, s32[256,1]{0,1:T(1,128)}, u32[]{:S(2)}) copy-start(s32[256,1]{0,1:T(1,128)} %param.14) | copy-start | bytes 3076
  3.5 11.9 %collective-permute-start.8 = (bf16[80,1280]{1,0:T(8,128)(2,1)S(1)}, bf16[80,1280]{1,0:T(8,128)(2,1)S(1)}, u32[]{:S(2)}, u32[]{:S(2)}) collective-permute-start(bf16[80,1280]{1,0:T(8,128)(2,1)S(1)} %get-tuple-element.115), channel_id=1, source_target_pairs={{0,24},{1,25},{2,26},{3,27},{4,28},{5,29},{6,30},{7,31},{8,0},{9,1... | collective-permute-start | bytes 614408 | tf_op jit(solution)/shard_map/weights/ppermute | solution.py:38
  6.4 12.9 %collective-permute-start.9 = (bf16[80,1280]{1,0:T(8,128)(2,1)S(1)}, bf16[80,1280]{1,0:T(8,128)(2,1)S(1)}, u32[]{:S(2)}, u32[]{:S(2)}) collective-permute-start(bf16[80,1280]{1,0:T(8,128)(2,1)S(1)} %get-tuple-element.115), channel_id=1, source_target_pairs={{0,8},{1,9},{2,10},{3,11},{4,12},{5,13},{6,14},{7,15},{8,16},{9,17... | collective-permute-start | bytes 614408 | tf_op jit(solution)/shard_map/weights/ppermute | solution.py:38
  6.4 12.9 %collective-permute-start.10 = (bf16[80,1280]{1,0:T(8,128)(2,1)S(1)}, bf16[80,1280]{1,0:T(8,128)(2,1)S(1)}, u32[]{:S(2)}, u32[]{:S(2)}) collective-permute-start(bf16[80,1280]{1,0:T(8,128)(2,1)S(1)} %get-tuple-element.115), channel_id=1, source_target_pairs={{0,16},{1,17},{2,18},{3,19},{4,20},{5,21},{6,22},{7,23},{8,24},{9,... | collective-permute-start | bytes 614408 | tf_op jit(solution)/shard_map/weights/ppermute | solution.py:38
  8.7 17.4 %collective-permute-start.1 = (bf16[80,1280]{1,0:T(8,128)(2,1)S(1)}, bf16[80,1280]{1,0:T(8,128)(2,1)S(1)}, u32[]{:S(2)}, u32[]{:S(2)}) collective-permute-start(bf16[80,1280]{1,0:T(8,128)(2,1)S(1)} %get-tuple-element.116), channel_id=1, source_target_pairs={{0,6},{1,7},{2,0},{3,1},{4,2},{5,3},{6,4},{7,5},{8,14},{9,15},{10,... | collective-permute-start | bytes 614408 | tf_op jit(solution)/shard_map/weights/ppermute | solution.py:38
  12.7 13.4 %collective-permute-start.2 = (bf16[80,1280]{1,0:T(8,128)(2,1)S(1)}, bf16[80,1280]{1,0:T(8,128)(2,1)S(1)}, u32[]{:S(2)}, u32[]{:S(2)}) collective-permute-start(bf16[80,1280]{1,0:T(8,128)(2,1)S(1)} %get-tuple-element.116), channel_id=1, source_target_pairs={{0,2},{1,3},{2,4},{3,5},{4,6},{5,7},{6,0},{7,1},{8,10},{9,11},{10,... | collective-permute-start | bytes 614408 | tf_op jit(solution)/shard_map/weights/ppermute | solution.py:38
  15.4 10.7 %collective-permute-start.3 = (bf16[80,1280]{1,0:T(8,128)(2,1)S(1)}, bf16[80,1280]{1,0:T(8,128)(2,1)S(1)}, u32[]{:S(2)}, u32[]{:S(2)}) collective-permute-start(bf16[80,1280]{1,0:T(8,128)(2,1)S(1)} %get-tuple-element.116), channel_id=1, source_target_pairs={{0,4},{1,5},{2,6},{3,7},{4,0},{5,1},{6,2},{7,3},{8,12},{9,13},{10,... | collective-permute-start | bytes 614408 | tf_op jit(solution)/shard_map/weights/ppermute | solution.py:38
  19.4 13.6 %copy-start = (bf16[4,80,1280]{2,1,0:T(8,128)(2,1)}, bf16[4,80,1280]{2,1,0:T(8,128)(2,1)S(1)}, u32[]{:S(2)}) copy-start(bf16[4,80,1280]{2,1,0:T(8,128)(2,1)S(1)} %pad_maximum_fusion.1.b0) | copy-start | bytes 2457604
  19.4 22.4 %collective-permute-start.12 = (bf16[4,80,1280]{2,1,0:T(8,128)(2,1)S(1)}, bf16[4,80,1280]{2,1,0:T(8,128)(2,1)S(1)}, u32[]{:S(2)}, u32[]{:S(2)}) collective-permute-start(bf16[4,80,1280]{2,1,0:T(8,128)(2,1)S(1)} %pad_maximum_fusion.1.b0), channel_id=1, source_target_pairs={{0,2},{1,3},{2,4},{3,5},{4,6},{5,7},{6,0},{7,1},{8,10},{9,11},{10,... | collective-permute-start | bytes 2457608 | tf_op jit(solution)/shard_map/weights/ppermute | solution.py:38
  23.8 18.3 %collective-permute-start.11 = (bf16[4,80,1280]{2,1,0:T(8,128)(2,1)S(1)}, bf16[4,80,1280]{2,1,0:T(8,128)(2,1)S(1)}, u32[]{:S(2)}, u32[]{:S(2)}) collective-permute-start(bf16[4,80,1280]{2,1,0:T(8,128)(2,1)S(1)} %pad_maximum_fusion.1.b0), channel_id=1, source_target_pairs={{0,6},{1,7},{2,0},{3,1},{4,2},{5,3},{6,4},{7,5},{8,14},{9,15},{10,... | collective-permute-start | bytes 2457608 | tf_op jit(solution)/shard_map/weights/ppermute | solution.py:38
  26.2 20.2 %collective-permute-start.5 = (bf16[4,80,1280]{2,1,0:T(8,128)(2,1)S(1)}, bf16[4,80,1280]{2,1,0:T(8,128)(2,1)S(1)}, u32[]{:S(2)}, u32[]{:S(2)}) collective-permute-start(bf16[4,80,1280]{2,1,0:T(8,128)(2,1)S(1)} %pad_maximum_fusion.a0), channel_id=1, source_target_pairs={{0,8},{1,9},{2,10},{3,11},{4,12},{5,13},{6,14},{7,15},{8,16},{9,17... | collective-permute-start | bytes 2457608 | tf_op jit(solution)/shard_map/weights/ppermute | solution.py:38
  27.8 20.1 %collective-permute-start.4 = (bf16[4,80,1280]{2,1,0:T(8,128)(2,1)S(1)}, bf16[4,80,1280]{2,1,0:T(8,128)(2,1)S(1)}, u32[]{:S(2)}, u32[]{:S(2)}) collective-permute-start(bf16[4,80,1280]{2,1,0:T(8,128)(2,1)S(1)} %pad_maximum_fusion.a0), channel_id=1, source_target_pairs={{0,24},{1,25},{2,26},{3,27},{4,28},{5,29},{6,30},{7,31},{8,0},{9,1... | collective-permute-start | bytes 2457608 | tf_op jit(solution)/shard_map/weights/ppermute | solution.py:38
  33.0 15.1 %collective-permute-start.15 = (bf16[256,1408]{1,0:T(8,128)(2,1)}, bf16[256,1408]{1,0:T(8,128)(2,1)S(1)}, u32[]{:S(2)}, u32[]{:S(2)}) collective-permute-start(bf16[256,1408]{1,0:T(8,128)(2,1)} %get-tuple-element.50.own), channel_id=1, source_target_pairs={{0,1},{1,0},{2,3},{3,2},{4,5},{5,4},{6,7},{7,6},{8,9},{9,8},{10,11... | collective-permute-start | bytes 2162696 | tf_op jit(solution)/shard_map/prepare/ppermute | solution.py:42
  41.9 13.1 %collective-permute-start.16 = (bf16[256,1664]{1,0:T(8,128)(2,1)}, bf16[256,1664]{1,0:T(8,128)(2,1)}, u32[]{:S(2)}, u32[]{:S(2)}) collective-permute-start(bf16[256,1664]{1,0:T(8,128)(2,1)} %get-tuple-element.51.extra), channel_id=1, source_target_pairs={{0,1},{1,0},{2,3},{3,2},{4,5},{5,4},{6,7},{7,6},{8,9},{9,8},{10,11... | collective-permute-start | bytes 2555912 | tf_op jit(solution)/shard_map/prepare/ppermute | solution.py:42
  42.1 13.0 %collective-permute-start.13 = (bf16[2,80,1280]{2,1,0:T(8,128)(2,1)S(1)}, bf16[2,80,1280]{2,1,0:T(8,128)(2,1)S(1)}, u32[]{:S(2)}, u32[]{:S(2)}) collective-permute-start(bf16[2,80,1280]{2,1,0:T(8,128)(2,1)S(1)} %slice.199), channel_id=1, source_target_pairs={{0,2},{1,3},{2,4},{3,5},{4,6},{5,7},{6,0},{7,1},{8,10},{9,11},{10,... | collective-permute-start | bytes 1228808 | tf_op jit(solution)/shard_map/weights/ppermute | solution.py:38
  46.3 9.3 %collective-permute-start.14 = (bf16[2,80,1280]{2,1,0:T(8,128)(2,1)S(1)}, bf16[2,80,1280]{2,1,0:T(8,128)(2,1)}, u32[]{:S(2)}, u32[]{:S(2)}) collective-permute-start(bf16[2,80,1280]{2,1,0:T(8,128)(2,1)S(1)} %slice.200), channel_id=1, source_target_pairs={{0,6},{1,7},{2,0},{3,1},{4,2},{5,3},{6,4},{7,5},{8,14},{9,15},{10,... | collective-permute-start | bytes 1228808 | tf_op jit(solution)/shard_map/weights/ppermute | solution.py:38
  48.0 10.3 %collective-permute-start.6 = (bf16[2,80,1280]{2,1,0:T(8,128)(2,1)S(1)}, bf16[2,80,1280]{2,1,0:T(8,128)(2,1)S(1)}, u32[]{:S(2)}, u32[]{:S(2)}) collective-permute-start(bf16[2,80,1280]{2,1,0:T(8,128)(2,1)S(1)} %slice.196), channel_id=1, source_target_pairs={{0,8},{1,9},{2,10},{3,11},{4,12},{5,13},{6,14},{7,15},{8,16},{9,17... | collective-permute-start | bytes 1228808 | tf_op jit(solution)/shard_map/weights/ppermute | solution.py:38
  49.1 10.1 %collective-permute-start.7 = (bf16[2,80,1280]{2,1,0:T(8,128)(2,1)S(1)}, bf16[2,80,1280]{2,1,0:T(8,128)(2,1)S(1)}, u32[]{:S(2)}, u32[]{:S(2)}) collective-permute-start(bf16[2,80,1280]{2,1,0:T(8,128)(2,1)S(1)} %slice.197), channel_id=1, source_target_pairs={{0,24},{1,25},{2,26},{3,27},{4,28},{5,29},{6,30},{7,31},{8,0},{9,1... | collective-permute-start | bytes 1228808 | tf_op jit(solution)/shard_map/weights/ppermute | solution.py:38
  60.0 31.6 %all-to-all-start = ((bf16[128,8,640]{2,1,0:T(8,128)(2,1)}), bf16[128,8,640]{2,1,0:T(8,128)(2,1)S(1)}, u32[]{:S(2)}, u32[]{:S(2)}) async-start(bf16[128,8,640]{2,1,0:T(8,128)(2,1)} %bitcast.15), calls=%async_computation | async-start | bytes 2621440 | tf_op jit(solution)/shard_map/grads_in/all_to_all | solution.py:434
  81.2 2.6 %collective-permute-start.17 = (bf16[512,640]{1,0:T(8,128)(2,1)}, bf16[512,640]{1,0:T(8,128)(2,1)S(1)}, u32[]{:S(2)}, u32[]{:S(2)}) collective-permute-start(bf16[512,640]{1,0:T(8,128)(2,1)} %get-tuple-element.63.attended.attended_hbm), channel_id=1, source_target_pairs={{0,1},{1,0},{2,3},{3,2},{4,5},{5,4},{6,7},{7,6},{8,9},{9,8},{10,11... | collective-permute-start | bytes 1966088 | tf_op jit(solution)/shard_map/forward/ppermute | solution.py:42
  98.4 10.0 %collective-permute-start.18 = (bf16[512,640]{1,0:T(8,128)(2,1)}, bf16[512,640]{1,0:T(8,128)(2,1)S(1)}, u32[]{:S(2)}, u32[]{:S(2)}) collective-permute-start(bf16[512,640]{1,0:T(8,128)(2,1)} %get-tuple-element.72), channel_id=1, source_target_pairs={{0,1},{1,0},{2,3},{3,2},{4,5},{5,4},{6,7},{7,6},{8,9},{9,8},{10,11... | collective-permute-start | bytes 1966088 | tf_op jit(solution)/shard_map/grads_in/ppermute | solution.py:42
  98.6 39.9 %all-to-all-start.1 = ((bf16[128,8,640]{2,1,0:T(8,128)(2,1)}), bf16[128,8,640]{2,1,0:T(8,128)(2,1)S(1)}, u32[]{:S(2)}, u32[]{:S(2)}) async-start(bf16[128,8,640]{2,1,0:T(8,128)(2,1)} %bitcast.17), calls=%async_computation.1 | async-start | bytes 2621440 | tf_op jit(solution)/shard_map/rows_out/all_to_all | solution.py:500
  123.5 21.2 %collective-permute-start.19 = (bf16[4,80,1280]{2,1,0:T(8,128)(2,1)}, bf16[4,80,1280]{2,1,0:T(8,128)(2,1)}, u32[]{:S(2)}, u32[]{:S(2)}) collective-permute-start(bf16[4,80,1280]{2,1,0:T(8,128)(2,1)} %get-tuple-element.78), channel_id=1, source_target_pairs={{0,8},{1,9},{2,10},{3,11},{4,12},{5,13},{6,14},{7,15},{8,16},{9,17... | collective-permute-start | bytes 2457608 | tf_op jit(solution)/shard_map/weight_grads/ppermute | solution.py:38
  124.5 20.3 %collective-permute-start.20 = (bf16[4,80,1280]{2,1,0:T(8,128)(2,1)}, bf16[4,80,1280]{2,1,0:T(8,128)(2,1)}, u32[]{:S(2)}, u32[]{:S(2)}) collective-permute-start(bf16[4,80,1280]{2,1,0:T(8,128)(2,1)} %get-tuple-element.79), channel_id=1, source_target_pairs={{0,24},{1,25},{2,26},{3,27},{4,28},{5,29},{6,30},{7,31},{8,0},{9,1... | collective-permute-start | bytes 2457608 | tf_op jit(solution)/shard_map/weight_grads/ppermute | solution.py:38
  126.8 23.8 %collective-permute-start.26 = (bf16[4,80,1280]{2,1,0:T(8,128)(2,1)}, bf16[4,80,1280]{2,1,0:T(8,128)(2,1)S(1)}, u32[]{:S(2)}, u32[]{:S(2)}) collective-permute-start(bf16[4,80,1280]{2,1,0:T(8,128)(2,1)} %get-tuple-element.88), channel_id=1, source_target_pairs={{0,2},{1,3},{2,4},{3,5},{4,6},{5,7},{6,0},{7,1},{8,10},{9,11},{10,... | collective-permute-start | bytes 2457608 | tf_op jit(solution)/shard_map/weight_grads/ppermute | solution.py:38
  127.9 24.5 %collective-permute-start.28 = (bf16[4,80,1280]{2,1,0:T(8,128)(2,1)}, bf16[4,80,1280]{2,1,0:T(8,128)(2,1)S(1)}, u32[]{:S(2)}, u32[]{:S(2)}) collective-permute-start(bf16[4,80,1280]{2,1,0:T(8,128)(2,1)} %get-tuple-element.89), channel_id=1, source_target_pairs={{0,6},{1,7},{2,0},{3,1},{4,2},{5,3},{6,4},{7,5},{8,14},{9,15},{10,... | collective-permute-start | bytes 2457608 | tf_op jit(solution)/shard_map/weight_grads/ppermute | solution.py:38
  146.1 11.7 %collective-permute-start.21 = (bf16[2,80,1280]{2,1,0:T(8,128)(2,1)S(1)}, bf16[2,80,1280]{2,1,0:T(8,128)(2,1)S(1)}, u32[]{:S(2)}, u32[]{:S(2)}) collective-permute-start(bf16[2,80,1280]{2,1,0:T(8,128)(2,1)S(1)} %add_convert_fusion.5), channel_id=1, source_target_pairs={{0,8},{1,9},{2,10},{3,11},{4,12},{5,13},{6,14},{7,15},{8,16},{9,17... | collective-permute-start | bytes 1228808 | tf_op jit(solution)/shard_map/weight_grads/ppermute | solution.py:38
  148.8 10.2 %collective-permute-start.23 = (bf16[2,80,1280]{2,1,0:T(8,128)(2,1)S(1)}, bf16[2,80,1280]{2,1,0:T(8,128)(2,1)S(1)}, u32[]{:S(2)}, u32[]{:S(2)}) collective-permute-start(bf16[2,80,1280]{2,1,0:T(8,128)(2,1)S(1)} %add_convert_fusion.4), channel_id=1, source_target_pairs={{0,24},{1,25},{2,26},{3,27},{4,28},{5,29},{6,30},{7,31},{8,0},{9,1... | collective-permute-start | bytes 1228808 | tf_op jit(solution)/shard_map/weight_grads/ppermute | solution.py:38
  150.7 14.7 %collective-permute-start.27 = (bf16[2,80,1280]{2,1,0:T(8,128)(2,1)S(1)}, bf16[2,80,1280]{2,1,0:T(8,128)(2,1)S(1)}, u32[]{:S(2)}, u32[]{:S(2)}) collective-permute-start(bf16[2,80,1280]{2,1,0:T(8,128)(2,1)S(1)} %add_convert_fusion.2), channel_id=1, source_target_pairs={{0,2},{1,3},{2,4},{3,5},{4,6},{5,7},{6,0},{7,1},{8,10},{9,11},{10,... | collective-permute-start | bytes 1228808 | tf_op jit(solution)/shard_map/weight_grads/ppermute | solution.py:38
  152.5 12.9 %collective-permute-start.30 = (bf16[2,80,1280]{2,1,0:T(8,128)(2,1)S(1)}, bf16[2,80,1280]{2,1,0:T(8,128)(2,1)S(1)}, u32[]{:S(2)}, u32[]{:S(2)}) collective-permute-start(bf16[2,80,1280]{2,1,0:T(8,128)(2,1)S(1)} %add_convert_fusion.1), channel_id=1, source_target_pairs={{0,6},{1,7},{2,0},{3,1},{4,2},{5,3},{6,4},{7,5},{8,14},{9,15},{10,... | collective-permute-start | bytes 1228808 | tf_op jit(solution)/shard_map/weight_grads/ppermute | solution.py:38
  160.4 10.7 %collective-permute-start.24 = (bf16[80,1280]{1,0:T(8,128)(2,1)S(1)}, bf16[80,1280]{1,0:T(8,128)(2,1)S(1)}, u32[]{:S(2)}, u32[]{:S(2)}) collective-permute-start(bf16[80,1280]{1,0:T(8,128)(2,1)S(1)} %get-tuple-element.109), channel_id=1, source_target_pairs={{0,6},{1,7},{2,0},{3,1},{4,2},{5,3},{6,4},{7,5},{8,14},{9,15},{10,... | collective-permute-start | bytes 614408 | tf_op jit(solution)/shard_map/weight_grads/ppermute | solution.py:38
  163.9 8.4 %collective-permute-start.25 = (bf16[80,1280]{1,0:T(8,128)(2,1)S(1)}, bf16[80,1280]{1,0:T(8,128)(2,1)S(1)}, u32[]{:S(2)}, u32[]{:S(2)}) collective-permute-start(bf16[80,1280]{1,0:T(8,128)(2,1)S(1)} %get-tuple-element.110), channel_id=1, source_target_pairs={{0,4},{1,5},{2,6},{3,7},{4,0},{5,1},{6,2},{7,3},{8,12},{9,13},{10,... | collective-permute-start | bytes 614408 | tf_op jit(solution)/shard_map/weight_grads/ppermute | solution.py:38
  164.2 10.0 %collective-permute-start.22 = (bf16[80,1280]{1,0:T(8,128)(2,1)S(1)}, bf16[80,1280]{1,0:T(8,128)(2,1)S(1)}, u32[]{:S(2)}, u32[]{:S(2)}) collective-permute-start(bf16[80,1280]{1,0:T(8,128)(2,1)S(1)} %fusion.9), channel_id=1, source_target_pairs={{0,2},{1,3},{2,4},{3,5},{4,6},{5,7},{6,0},{7,1},{8,10},{9,11},{10,... | collective-permute-start | bytes 614408 | tf_op jit(solution)/shard_map/weight_grads/ppermute | solution.py:38
  165.7 9.5 %collective-permute-start.31 = (bf16[80,1280]{1,0:T(8,128)(2,1)S(1)}, bf16[80,1280]{1,0:T(8,128)(2,1)S(1)}, u32[]{:S(2)}, u32[]{:S(2)}) collective-permute-start(bf16[80,1280]{1,0:T(8,128)(2,1)S(1)} %get-tuple-element.111), channel_id=1, source_target_pairs={{0,24},{1,25},{2,26},{3,27},{4,28},{5,29},{6,30},{7,31},{8,0},{9,1... | collective-permute-start | bytes 614408 | tf_op jit(solution)/shard_map/weight_grads/ppermute | solution.py:38
  169.1 7.8 %collective-permute-start.32 = (bf16[80,1280]{1,0:T(8,128)(2,1)S(1)}, bf16[80,1280]{1,0:T(8,128)(2,1)S(1)}, u32[]{:S(2)}, u32[]{:S(2)}) collective-permute-start(bf16[80,1280]{1,0:T(8,128)(2,1)S(1)} %get-tuple-element.112), channel_id=1, source_target_pairs={{0,16},{1,17},{2,18},{3,19},{4,20},{5,21},{6,22},{7,23},{8,24},{9,... | collective-permute-start | bytes 614408 | tf_op jit(solution)/shard_map/weight_grads/ppermute | solution.py:38
  171.1 7.9 %collective-permute-start.29 = (bf16[80,1280]{1,0:T(8,128)(2,1)S(1)}, bf16[80,1280]{1,0:T(8,128)(2,1)S(1)}, u32[]{:S(2)}, u32[]{:S(2)}) collective-permute-start(bf16[80,1280]{1,0:T(8,128)(2,1)S(1)} %fusion.10), channel_id=1, source_target_pairs={{0,8},{1,9},{2,10},{3,11},{4,12},{5,13},{6,14},{7,15},{8,16},{9,17... | collective-permute-start | bytes 614408 | tf_op jit(solution)/shard_map/weight_grads/ppermute | solution.py:38
  179.2 1.5 collective-permute-start.33
  179.3 15.2 %collective-permute-start.34 = (bf16[256,1280]{1,0:T(8,128)(2,1)}, bf16[256,1280]{1,0:T(8,128)(2,1)}, u32[]{:S(2)}, u32[]{:S(2)}) collective-permute-start(bf16[256,1280]{1,0:T(8,128)(2,1)} %get-tuple-element.94), channel_id=1, source_target_pairs={{0,1},{1,0},{2,3},{3,2},{4,5},{5,4},{6,7},{7,6},{8,9},{9,8},{10,11... | collective-permute-start | bytes 1966088 | tf_op jit(solution)/shard_map/norm_grad/ppermute | solution.py:42
  181.1 6.2 %collective-permute-start.36 = (bf16[40,1280]{1,0:T(8,128)(2,1)S(1)}, bf16[40,1280]{1,0:T(8,128)(2,1)S(1)}, u32[]{:S(2)}, u32[]{:S(2)}) collective-permute-start(bf16[40,1280]{1,0:T(8,128)(2,1)S(1)} %get-tuple-element.106), channel_id=1, source_target_pairs={{0,32},{32,64},{64,96},{96,0},{1,33},{33,65},{65,97},{97,1},{2,34}... | collective-permute-start | bytes 307208 | tf_op jit(solution)/shard_map/over_groups/ppermute | solution.py:37
  182.6 6.2 %collective-permute-start.37 = (bf16[40,1280]{1,0:T(8,128)(2,1)S(1)}, bf16[40,1280]{1,0:T(8,128)(2,1)S(1)}, u32[]{:S(2)}, u32[]{:S(2)}) collective-permute-start(bf16[40,1280]{1,0:T(8,128)(2,1)S(1)} %get-tuple-element.108), channel_id=1, source_target_pairs={{0,96},{32,0},{64,32},{96,64},{1,97},{33,1},{65,33},{97,65},{2,98}... | collective-permute-start | bytes 307208 | tf_op jit(solution)/shard_map/over_groups/ppermute | solution.py:37
  184.4 6.2 %collective-permute-start.38 = (bf16[40,1280]{1,0:T(8,128)(2,1)S(1)}, bf16[40,1280]{1,0:T(8,128)(2,1)S(1)}, u32[]{:S(2)}, u32[]{:S(2)}) collective-permute-start(bf16[40,1280]{1,0:T(8,128)(2,1)S(1)} %get-tuple-element.107), channel_id=1, source_target_pairs={{0,64},{32,96},{64,0},{96,32},{1,65},{33,97},{65,1},{97,33},{2,66}... | collective-permute-start | bytes 307208 | tf_op jit(solution)/shard_map/over_groups/ppermute | solution.py:37
  186.3 8.3 %collective-permute-start.35 = (bf16[256,640]{1,0:T(8,128)(2,1)S(1)}, bf16[256,640]{1,0:T(8,128)(2,1)S(1)}, u32[]{:S(2)}, u32[]{:S(2)}) collective-permute-start(bf16[256,640]{1,0:T(8,128)(2,1)S(1)} %slice.194), channel_id=1, source_target_pairs={{0,1},{1,0},{2,3},{3,2},{4,5},{5,4},{6,7},{7,6},{8,9},{9,8},{10,11... | collective-permute-start | bytes 983048 | tf_op jit(solution)/shard_map/norm_grad/ppermute | solution.py:42
  190.6 8.6 %collective-permute-start.39 = (bf16[40,1280]{1,0:T(8,128)(2,1)S(1)}, bf16[40,1280]{1,0:T(8,128)(2,1)S(1)}, u32[]{:S(2)}, u32[]{:S(2)}) collective-permute-start(bf16[40,1280]{1,0:T(8,128)(2,1)S(1)} %fusion.13), channel_id=1, source_target_pairs={{0,96},{32,0},{64,32},{96,64},{1,97},{33,1},{65,33},{97,65},{2,98}... | collective-permute-start | bytes 307208 | tf_op jit(solution)/shard_map/over_groups/ppermute | solution.py:37
  192.6 7.0 %collective-permute-start.40 = (bf16[40,1280]{1,0:T(8,128)(2,1)S(1)}, bf16[40,1280]{1,0:T(8,128)(2,1)S(1)}, u32[]{:S(2)}, u32[]{:S(2)}) collective-permute-start(bf16[40,1280]{1,0:T(8,128)(2,1)S(1)} %fusion.13), channel_id=1, source_target_pairs={{0,32},{32,64},{64,96},{96,0},{1,33},{33,65},{65,97},{97,1},{2,34}... | collective-permute-start | bytes 307208 | tf_op jit(solution)/shard_map/over_groups/ppermute | solution.py:37
  192.7 6.8 %collective-permute-start.41 = (bf16[40,1280]{1,0:T(8,128)(2,1)S(1)}, bf16[40,1280]{1,0:T(8,128)(2,1)S(1)}, u32[]{:S(2)}, u32[]{:S(2)}) collective-permute-start(bf16[40,1280]{1,0:T(8,128)(2,1)S(1)} %fusion.13), channel_id=1, source_target_pairs={{0,64},{32,96},{64,0},{96,32},{1,65},{33,97},{65,1},{97,33},{2,66}... | collective-permute-start | bytes 307208 | tf_op jit(solution)/shard_map/over_groups/ppermute | solution.py:37
  (19 other events, 101.8 us)

commit v5 on v4

--- a/solution.py
+++ b/solution.py
@@ -264,7 +264,7 @@
     grads[:ROWS, :] = dot(extra[:, :SLOTS], returned[...]).astype(BF)
     grads[ROWS:, :] = dot(sib_extra[:, :SLOTS], returned[...]).astype(BF)
     wait_all(copies)
-    mine[...] = dot_nt(grads[...], wout[at_rows(place[2], HALF), :])
+    mine[...] = dot_nt(grads[...], wout[at_rows(place[2], HALF), :]).astype(BF)
     theirs[...] = dot_nt(grads[...], wout[at_rows(1 - place[2], HALF), :]).astype(BF)
 
 
@@ -302,7 +302,7 @@
     first_in = [copies.start(qkv_hbm, qkv), copies.start(probs_hbm, probs)]
     last_in = copies.start(normed_hbm, normed_t)
     wait_all(grads_in)
-    gatt[...] = (ga[...] + gb[...].astype(F32)).astype(BF)
+    gatt[...] = add(ga[...], gb[...]).astype(BF)
     wait_all(second_in)
     attended_t[at_rows(place[2], HALF), :] = attended[...].T
     attended_t[at_rows(1 - place[2], HALF), :] = other[...].T
@@ -461,7 +461,7 @@
         returned, outgoing = lax.optimization_barrier((returned, outgoing))
         grads, ga_mine, ga_theirs = call(
             pick_kernel,
-            [((512, HALF), BF), ((512, HALF), F32), ((512, HALF), BF)],
+            [((512, HALF), BF)] * 3,
             (place, returned, extra, sib_extra, *part_b),
             "svvv" + "a" * 5,
             scratch=[pltpu.VMEM((D, HALF), BF), pltpu.SemaphoreType.DMA((16,))],
@@ -479,7 +479,7 @@
             scratch=[
                 pltpu.VMEM((512, HALF), BF),
                 pltpu.VMEM((512, HALF), BF),
-                pltpu.VMEM((512, HALF), F32),
+                pltpu.VMEM((512, HALF), BF),
                 pltpu.VMEM((512, HALF), BF),
                 pltpu.VMEM((D, 3 * HALF), BF),
                 pltpu.VMEM((D, HALF), BF),

time: 203 us -> 203 us (level)
  no operation moved by 1% of the time
where the time goes in v5:
time: 203 us; the launch traced here: 202 us
  starting transfers between devices  77.9 us (38%)
  Pallas kernels  57.6 us (28%)
  waiting for transfers between devices  47.9 us (24%)
  local copies, waits for them, and re-layouts  10 us (5%)
  other arithmetic  7.41 us (4%)
    pallas_call x8, Pallas kernels, call(): pl.pallas_call(kernel, out_shape=[jax.ShapeDtypeStruct(s, t) for s, t in...  57.6 us
    ppermute x28, starting transfers between devices, hop(): return lax.ppermute(value, 'enc', ring(axis, step))  48.8 us
    ppermute x28, waiting for transfers between devices, hop(): return lax.ppermute(value, 'enc', ring(axis, step))  38.7 us
    all_to_all x1, starting transfers between devices, body(): lax.all_to_all(outgoing, ('grp', 'enc'), split_axis=0, concat_axis=0, til...  9.79 us
    ppermute x6, starting transfers between devices, hop(): return lax.ppermute(value, 'grp', [(i, (i + step) % 4) for i in range(4)])  9.09 us
    all_to_all x1, starting transfers between devices, body(): lax.all_to_all(sent, ('grp', 'enc'), split_axis=0, concat_axis=0, tiled=T...  8.88 us
    unnamed x48, local copies, waits for them, and re-layouts  7.21 us
    ppermute x8, waiting for transfers between devices, to_sibling(): return lax.ppermute(value, 'enc', [(i, i ^ 1) for i in range(32)])  4.69 us
  transfers between devices with their start and end apart: 44, of which 25 were waited for; matrix products, arithmetic and copies ran while one was open for 4% of the time, Pallas kernels for 26%

profile of v5, /device:TPU:0, one launch (start us, length us, event | category | flops | bytes accessed | tf_op | source)
XLA Modules:
  0.0 202.0 jit_solution(12281419425409889585)
XLA Ops:
  1.8 1.4 collective-permute-done
  3.5 2.9 %collective-permute-start.8 = (bf16[80,1280]{1,0:T(8,128)(2,1)S(1)}, bf16[80,1280]{1,0:T(8,128)(2,1)S(1)}, u32[]{:S(2)}, u32[]{:S(2)}) collective-permute-start(bf16[80,1280]{1,0:T(8,128)(2,1)S(1)} %get-tuple-element.115), channel_id=1, source_target_pairs={{0,24},{1,25},{2,26},{3,27},{4,28},{5,29},{6,30},{7,31},{8,0},{9,1... | collective-permute-start | bytes 614408 | tf_op jit(solution)/shard_map/weights/ppermute | solution.py:38
  6.4 2.3 %collective-permute-start.10 = (bf16[80,1280]{1,0:T(8,128)(2,1)S(1)}, bf16[80,1280]{1,0:T(8,128)(2,1)S(1)}, u32[]{:S(2)}, u32[]{:S(2)}) collective-permute-start(bf16[80,1280]{1,0:T(8,128)(2,1)S(1)} %get-tuple-element.115), channel_id=1, source_target_pairs={{0,16},{1,17},{2,18},{3,19},{4,20},{5,21},{6,22},{7,23},{8,24},{9,... | collective-permute-start | bytes 614408 | tf_op jit(solution)/shard_map/weights/ppermute | solution.py:38
  8.7 4.0 %collective-permute-start.1 = (bf16[80,1280]{1,0:T(8,128)(2,1)S(1)}, bf16[80,1280]{1,0:T(8,128)(2,1)S(1)}, u32[]{:S(2)}, u32[]{:S(2)}) collective-permute-start(bf16[80,1280]{1,0:T(8,128)(2,1)S(1)} %get-tuple-element.116), channel_id=1, source_target_pairs={{0,6},{1,7},{2,0},{3,1},{4,2},{5,3},{6,4},{7,5},{8,14},{9,15},{10,... | collective-permute-start | bytes 614408 | tf_op jit(solution)/shard_map/weights/ppermute | solution.py:38
  12.7 2.7 %collective-permute-done.8 = bf16[80,1280]{1,0:T(8,128)(2,1)S(1)} collective-permute-done((bf16[80,1280]{1,0:T(8,128)(2,1)S(1)}, bf16[80,1280]{1,0:T(8,128)(2,1)S(1)}, u32[]{:S(2)}, u32[]{:S(2)}) %collective-permute-start.8) | collective-permute-done | bytes 204832 | tf_op jit(solution)/shard_map/weights/ppermute | solution.py:38
  15.4 3.9 %collective-permute-start.3 = (bf16[80,1280]{1,0:T(8,128)(2,1)S(1)}, bf16[80,1280]{1,0:T(8,128)(2,1)S(1)}, u32[]{:S(2)}, u32[]{:S(2)}) collective-permute-start(bf16[80,1280]{1,0:T(8,128)(2,1)S(1)} %get-tuple-element.116), channel_id=1, source_target_pairs={{0,4},{1,5},{2,6},{3,7},{4,0},{5,1},{6,2},{7,3},{8,12},{9,13},{10,... | collective-permute-start | bytes 614408 | tf_op jit(solution)/shard_map/weights/ppermute | solution.py:38
  19.4 1.5 collective-permute-start.12
  23.8 2.3 %collective-permute-start.11 = (bf16[4,80,1280]{2,1,0:T(8,128)(2,1)S(1)}, bf16[4,80,1280]{2,1,0:T(8,128)(2,1)S(1)}, u32[]{:S(2)}, u32[]{:S(2)}) collective-permute-start(bf16[4,80,1280]{2,1,0:T(8,128)(2,1)S(1)} %pad_maximum_fusion.1.b0), channel_id=1, source_target_pairs={{0,6},{1,7},{2,0},{3,1},{4,2},{5,3},{6,4},{7,5},{8,14},{9,15},{10,... | collective-permute-start | bytes 2457608 | tf_op jit(solution)/shard_map/weights/ppermute | solution.py:38
  26.2 1.7 collective-permute-start.5
  27.8 1.7 collective-permute-start.4
  29.5 3.5 %prepare.2 = (bf16[256,1408]{1,0:T(8,128)(2,1)}, bf16[256,1664]{1,0:T(8,128)(2,1)}, bf16[256,1280]{1,0:T(8,128)(2,1)}) custom-call(s32[3]{0:T(128)} %pad_add_fusion.place, s32[1,4]{1,0:T(1,128)} %counts.1, bf16[256,1280]{1,0:T(8,128)(2,1)} %patches.1, f32[1,1280]{1,0:T(1,128)} %reshape.37.gain, s32[256,1]{1,0:T(8,128)} %copy.13.order, s32[256,1]{1,0:T(8,128)} %copy.14.owners), custom_call_target="tpu_custom_call" | custom-call | flops 3000000000 | bytes 9000000 | tf_op jit(solution)/shard_map/prepare/pallas_call | solution.py:97
  33.1 8.7 %collective-permute-done.12.b2 = bf16[4,80,1280]{2,1,0:T(8,128)(2,1)S(1)} collective-permute-done((bf16[4,80,1280]{2,1,0:T(8,128)(2,1)S(1)}, bf16[4,80,1280]{2,1,0:T(8,128)(2,1)S(1)}, u32[]{:S(2)}, u32[]{:S(2)}) %collective-permute-start.12) | collective-permute-done | bytes 819232 | tf_op jit(solution)/shard_map/weights/ppermute | solution.py:38
  42.1 1.5 collective-permute-start.13
  43.7 2.7 %collective-permute-done.5.a2 = bf16[4,80,1280]{2,1,0:T(8,128)(2,1)S(1)} collective-permute-done((bf16[4,80,1280]{2,1,0:T(8,128)(2,1)S(1)}, bf16[4,80,1280]{2,1,0:T(8,128)(2,1)S(1)}, u32[]{:S(2)}, u32[]{:S(2)}) %collective-permute-start.5) | collective-permute-done | bytes 819232 | tf_op jit(solution)/shard_map/weights/ppermute | solution.py:38
  46.3 1.6 collective-permute-start.14
  49.1 3.0 %collective-permute-start.7 = (bf16[2,80,1280]{2,1,0:T(8,128)(2,1)S(1)}, bf16[2,80,1280]{2,1,0:T(8,128)(2,1)S(1)}, u32[]{:S(2)}, u32[]{:S(2)}) collective-permute-start(bf16[2,80,1280]{2,1,0:T(8,128)(2,1)S(1)} %slice.197), channel_id=1, source_target_pairs={{0,24},{1,25},{2,26},{3,27},{4,28},{5,29},{6,30},{7,31},{8,0},{9,1... | collective-permute-start | bytes 1228808 | tf_op jit(solution)/shard_map/weights/ppermute | solution.py:38
  52.2 2.8 %prepare.3.normed_hbm = bf16[1280,512]{1,0:T(8,128)(2,1)} custom-call(bf16[256,1408]{1,0:T(8,128)(2,1)} %get-tuple-element.50.own, bf16[256,1408]{1,0:T(8,128)(2,1)} %copy-done.21), custom_call_target="tpu_custom_call" | custom-call | flops 3000000000 | bytes 9000000 | tf_op jit(solution)/shard_map/prepare/pallas_call | solution.py:97
  55.6 2.6 %collective-permute-done.6.a3 = bf16[2,80,1280]{2,1,0:T(8,128)(2,1)S(1)} collective-permute-done((bf16[2,80,1280]{2,1,0:T(8,128)(2,1)S(1)}, bf16[2,80,1280]{2,1,0:T(8,128)(2,1)S(1)}, u32[]{:S(2)}, u32[]{:S(2)}) %collective-permute-start.6) | collective-permute-done | bytes 409632 | tf_op jit(solution)/shard_map/weights/ppermute | solution.py:38
  60.0 8.9 %all-to-all-start = ((bf16[128,8,640]{2,1,0:T(8,128)(2,1)}), bf16[128,8,640]{2,1,0:T(8,128)(2,1)S(1)}, u32[]{:S(2)}, u32[]{:S(2)}) async-start(bf16[128,8,640]{2,1,0:T(8,128)(2,1)} %bitcast.15), calls=%async_computation | async-start | bytes 2621440 | tf_op jit(solution)/shard_map/grads_in/all_to_all | solution.py:434
  68.9 12.3 %forward.2 = (f32[4,8,128,128]{3,2,1,0:T(8,128)}, bf16[512,1920]{1,0:T(8,128)(2,1)}, bf16[512,640]{1,0:T(8,128)(2,1)}) custom-call(s32[3]{0:T(128)} %pad_add_fusion.place, bf16[256,1408]{1,0:T(8,128)(2,1)} %get-tuple-element.50.own, bf16[256,1408]{1,0:T(8,128)(2,1)} %copy-done.21, bf16[4,80,1280]{2,1,0:T(8,128)(2,1)} %copy-done.1, ...), custom_call_target="tpu_custom_call" | custom-call | flops 12000000000 | bytes 36000000 | tf_op jit(solution)/shard_map/forward/pallas_call | solution.py:97
  81.5 2.3 %collective-permute-done.17.other.other_hbm = bf16[512,640]{1,0:T(8,128)(2,1)S(1)} collective-permute-done((bf16[512,640]{1,0:T(8,128)(2,1)}, bf16[512,640]{1,0:T(8,128)(2,1)S(1)}, u32[]{:S(2)}, u32[]{:S(2)}) %collective-permute-start.17) | collective-permute-done | bytes 655392 | tf_op jit(solution)/shard_map/forward/ppermute | solution.py:42
  84.7 7.0 %forward.3 = bf16[1024,640]{1,0:T(8,128)(2,1)} custom-call(s32[3]{0:T(128)} %pad_add_fusion.place, bf16[512,640]{1,0:T(8,128)(2,1)} %get-tuple-element.63.attended.attended_hbm, bf16[512,640]{1,0:T(8,128)(2,1)} %copy-done.10, bf16[256,1280]{1,0:T(8,128)(2,1)} %get-tuple-element.64.ordered, bf16[256,1664]{1,0:T(8,128)(2,1)} %get-tuple-element.51.extra, ...), custom_call_target="tpu_custom_call" | custom-call | flops 3000000000 | bytes 9000000 | tf_op jit(solution)/shard_map/forward/pallas_call | solution.py:97
  92.7 5.7 %grads_in.1 = (bf16[512,640]{1,0:T(8,128)(2,1)}, bf16[512,640]{1,0:T(8,128)(2,1)}, bf16[512,640]{1,0:T(8,128)(2,1)}) custom-call(s32[3]{0:T(128)} %pad_add_fusion.place, bf16[1024,640]{1,0:T(8,128)(2,1)} %bitcast.79, bf16[256,1664]{1,0:T(8,128)(2,1)} %get-tuple-element.51.extra, bf16[256,1664]{1,0:T(8,128)(2,1)} %collective-permute-done.16.sib_extra, ...), custom_call_target="tpu_custom_call" | custom-call | flops 3000000000 | bytes 9000000 | tf_op jit(solution)/shard_map/grads_in/pallas_call | solution.py:97
  98.6 9.8 %all-to-all-start.1 = ((bf16[128,8,640]{2,1,0:T(8,128)(2,1)}), bf16[128,8,640]{2,1,0:T(8,128)(2,1)S(1)}, u32[]{:S(2)}, u32[]{:S(2)}) async-start(bf16[128,8,640]{2,1,0:T(8,128)(2,1)} %bitcast.17), calls=%async_computation.1 | async-start | bytes 2621440 | tf_op jit(solution)/shard_map/rows_out/all_to_all | solution.py:500
  109.3 14.0 %backward.1 = (bf16[512,1920]{1,0:T(8,128)(2,1)}, bf16[4,80,1280]{2,1,0:T(8,128)(2,1)}, bf16[4,80,1280]{2,1,0:T(8,128)(2,1)}, bf16[4,80,1280]{2,1,0:T(8,128)(2,1...) custom-call(s32[3]{0:T(128)} %pad_add_fusion.place, ...), custom_call_target="tpu_custom_call" | custom-call | flops 1000000000 | bytes 3000000 | tf_op jit(solution)/shard_map/backward/pallas_call | solution.py:97
  124.3 2.3 %collective-permute-start.20 = (bf16[4,80,1280]{2,1,0:T(8,128)(2,1)}, bf16[4,80,1280]{2,1,0:T(8,128)(2,1)}, u32[]{:S(2)}, u32[]{:S(2)}) collective-permute-start(bf16[4,80,1280]{2,1,0:T(8,128)(2,1)} %get-tuple-element.79), channel_id=1, source_target_pairs={{0,24},{1,25},{2,26},{3,27},{4,28},{5,29},{6,30},{7,31},{8,0},{9,1... | collective-permute-start | bytes 2457608 | tf_op jit(solution)/shard_map/weight_grads/ppermute | solution.py:38
  127.7 2.2 %collective-permute-start.28 = (bf16[4,80,1280]{2,1,0:T(8,128)(2,1)}, bf16[4,80,1280]{2,1,0:T(8,128)(2,1)S(1)}, u32[]{:S(2)}, u32[]{:S(2)}) collective-permute-start(bf16[4,80,1280]{2,1,0:T(8,128)(2,1)} %get-tuple-element.89), channel_id=1, source_target_pairs={{0,6},{1,7},{2,0},{3,1},{4,2},{5,3},{6,4},{7,5},{8,14},{9,15},{10,... | collective-permute-start | bytes 2457608 | tf_op jit(solution)/shard_map/weight_grads/ppermute | solution.py:38
  129.8 8.4 %norm_grad.2 = (f32[256,1280]{1,0:T(8,128)}, bf16[256,1280]{1,0:T(8,128)(2,1)}) custom-call(s32[3]{0:T(128)} %pad_add_fusion.place, bf16[512,1920]{1,0:T(8,128)(2,1)} %get-tuple-element.80.gqkv, bf16[4,80,1280]{2,1,0:T(8,128)(2,1)} %copy-done.1, bf16[4,80,1280]{2,1,0:T(8,128)(2,1)} %copy-done.5, bf16[4,80,1280]{2,1,0:T(8,128)(2,1)} %copy-done.4, ...), custom_call_target="tpu_custom_call" | custom-call | flops 1000000000 | bytes 3000000 | tf_op jit(solution)/shard_map/norm_grad/pallas_call | solution.py:97
  138.3 6.2 %collective-permute-done.19 = bf16[4,80,1280]{2,1,0:T(8,128)(2,1)} collective-permute-done((bf16[4,80,1280]{2,1,0:T(8,128)(2,1)}, bf16[4,80,1280]{2,1,0:T(8,128)(2,1)}, u32[]{:S(2)}, u32[]{:S(2)}) %collective-permute-start.19) | collective-permute-done | bytes 819232 | tf_op jit(solution)/shard_map/weight_grads/ppermute | solution.py:38
  145.9 1.5 collective-permute-start.21
  148.5 1.8 collective-permute-start.23
  150.5 1.7 collective-permute-start.27
  152.3 1.8 collective-permute-start.30
  154.1 3.4 %collective-permute-done.21 = bf16[2,80,1280]{2,1,0:T(8,128)(2,1)S(1)} collective-permute-done((bf16[2,80,1280]{2,1,0:T(8,128)(2,1)S(1)}, bf16[2,80,1280]{2,1,0:T(8,128)(2,1)S(1)}, u32[]{:S(2)}, u32[]{:S(2)}) %collective-permute-start.21) | collective-permute-done | bytes 409632 | tf_op jit(solution)/shard_map/weight_grads/ppermute | solution.py:38
  160.2 3.4 %collective-permute-start.24 = (bf16[80,1280]{1,0:T(8,128)(2,1)S(1)}, bf16[80,1280]{1,0:T(8,128)(2,1)S(1)}, u32[]{:S(2)}, u32[]{:S(2)}) collective-permute-start(bf16[80,1280]{1,0:T(8,128)(2,1)S(1)} %get-tuple-element.109), channel_id=1, source_target_pairs={{0,6},{1,7},{2,0},{3,1},{4,2},{5,3},{6,4},{7,5},{8,14},{9,15},{10,... | collective-permute-start | bytes 614408 | tf_op jit(solution)/shard_map/weight_grads/ppermute | solution.py:38
  165.5 3.4 %collective-permute-start.31 = (bf16[80,1280]{1,0:T(8,128)(2,1)S(1)}, bf16[80,1280]{1,0:T(8,128)(2,1)S(1)}, u32[]{:S(2)}, u32[]{:S(2)}) collective-permute-start(bf16[80,1280]{1,0:T(8,128)(2,1)S(1)} %get-tuple-element.111), channel_id=1, source_target_pairs={{0,24},{1,25},{2,26},{3,27},{4,28},{5,29},{6,30},{7,31},{8,0},{9,1... | collective-permute-start | bytes 614408 | tf_op jit(solution)/shard_map/weight_grads/ppermute | solution.py:38
  168.9 2.0 collective-permute-done.24
  171.9 2.0 collective-permute-done.22
  175.0 1.7 collective-permute-done.32
  176.7 2.1 %collective-permute-done.29 = bf16[80,1280]{1,0:T(8,128)(2,1)S(1)} collective-permute-done((bf16[80,1280]{1,0:T(8,128)(2,1)S(1)}, bf16[80,1280]{1,0:T(8,128)(2,1)S(1)}, u32[]{:S(2)}, u32[]{:S(2)}) %collective-permute-start.29) | collective-permute-done | bytes 204832 | tf_op jit(solution)/shard_map/weight_grads/ppermute | solution.py:38
  180.8 1.6 collective-permute-start.36
  182.4 1.8 collective-permute-start.37
  184.1 1.8 collective-permute-start.38
  187.0 1.5 collective-permute-done.37
  188.5 1.8 collective-permute-done.38
  190.3 2.0 collective-permute-start.39
  192.4 1.8 collective-permute-start.41
  195.0 4.0 %norm_grad.3 = bf16[256,1280]{1,0:T(8,128)(2,1)} custom-call(s32[3]{0:T(128)} %pad_add_fusion.place, f32[256,1280]{1,0:T(8,128)} %get-tuple-element.93.mine, bf16[256,1280]{1,0:T(8,128)(2,1)} %collective-permute-done.34.theirs, bf16[256,1280]{1,0:T(8,128)(2,1)} %get-tuple-element.64.ordered, f32[1,1280]{1,0:T(1,128)} %reshape.37.gain, ...), custom_call_target="tpu_custom_call" | custom-call | flops 3000000000 | bytes 9000000 | tf_op jit(solution)/shard_map/norm_grad/pallas_call | solution.py:97
  (135 shorter events, 30.0 us)
Async XLA Ops:
  1.8 1.5 collective-permute-start
  3.4 18.2 %copy-start.18 = (f32[1280]{0:T(1024)S(1)}, f32[1280]{0:T(1024)}, u32[]{:S(2)}) copy-start(f32[1280]{0:T(1024)} %param.9) | copy-start | bytes 15364
  3.4 18.8 %copy-start.20 = (s32[2,128]{1,0:T(2,128)S(1)}, s32[2,128]{1,0:T(2,128)}, u32[]{:S(2)}) copy-start(s32[2,128]{1,0:T(2,128)} %param.13) | copy-start | bytes 3076
  3.4 19.6 %copy-start.19 = (s32[256,1]{0,1:T(1,128)S(1)}, s32[256,1]{0,1:T(1,128)}, u32[]{:S(2)}) copy-start(s32[256,1]{0,1:T(1,128)} %param.14) | copy-start | bytes 3076
  3.5 11.9 %collective-permute-start.8 = (bf16[80,1280]{1,0:T(8,128)(2,1)S(1)}, bf16[80,1280]{1,0:T(8,128)(2,1)S(1)}, u32[]{:S(2)}, u32[]{:S(2)}) collective-permute-start(bf16[80,1280]{1,0:T(8,128)(2,1)S(1)} %get-tuple-element.115), channel_id=1, source_target_pairs={{0,24},{1,25},{2,26},{3,27},{4,28},{5,29},{6,30},{7,31},{8,0},{9,1... | collective-permute-start | bytes 614408 | tf_op jit(solution)/shard_map/weights/ppermute | solution.py:38
  6.4 12.9 %collective-permute-start.9 = (bf16[80,1280]{1,0:T(8,128)(2,1)S(1)}, bf16[80,1280]{1,0:T(8,128)(2,1)S(1)}, u32[]{:S(2)}, u32[]{:S(2)}) collective-permute-start(bf16[80,1280]{1,0:T(8,128)(2,1)S(1)} %get-tuple-element.115), channel_id=1, source_target_pairs={{0,8},{1,9},{2,10},{3,11},{4,12},{5,13},{6,14},{7,15},{8,16},{9,17... | collective-permute-start | bytes 614408 | tf_op jit(solution)/shard_map/weights/ppermute | solution.py:38
  6.4 12.9 %collective-permute-start.10 = (bf16[80,1280]{1,0:T(8,128)(2,1)S(1)}, bf16[80,1280]{1,0:T(8,128)(2,1)S(1)}, u32[]{:S(2)}, u32[]{:S(2)}) collective-permute-start(bf16[80,1280]{1,0:T(8,128)(2,1)S(1)} %get-tuple-element.115), channel_id=1, source_target_pairs={{0,16},{1,17},{2,18},{3,19},{4,20},{5,21},{6,22},{7,23},{8,24},{9,... | collective-permute-start | bytes 614408 | tf_op jit(solution)/shard_map/weights/ppermute | solution.py:38
  8.7 17.4 %collective-permute-start.1 = (bf16[80,1280]{1,0:T(8,128)(2,1)S(1)}, bf16[80,1280]{1,0:T(8,128)(2,1)S(1)}, u32[]{:S(2)}, u32[]{:S(2)}) collective-permute-start(bf16[80,1280]{1,0:T(8,128)(2,1)S(1)} %get-tuple-element.116), channel_id=1, source_target_pairs={{0,6},{1,7},{2,0},{3,1},{4,2},{5,3},{6,4},{7,5},{8,14},{9,15},{10,... | collective-permute-start | bytes 614408 | tf_op jit(solution)/shard_map/weights/ppermute | solution.py:38
  12.7 13.4 %collective-permute-start.2 = (bf16[80,1280]{1,0:T(8,128)(2,1)S(1)}, bf16[80,1280]{1,0:T(8,128)(2,1)S(1)}, u32[]{:S(2)}, u32[]{:S(2)}) collective-permute-start(bf16[80,1280]{1,0:T(8,128)(2,1)S(1)} %get-tuple-element.116), channel_id=1, source_target_pairs={{0,2},{1,3},{2,4},{3,5},{4,6},{5,7},{6,0},{7,1},{8,10},{9,11},{10,... | collective-permute-start | bytes 614408 | tf_op jit(solution)/shard_map/weights/ppermute | solution.py:38
  15.4 10.7 %collective-permute-start.3 = (bf16[80,1280]{1,0:T(8,128)(2,1)S(1)}, bf16[80,1280]{1,0:T(8,128)(2,1)S(1)}, u32[]{:S(2)}, u32[]{:S(2)}) collective-permute-start(bf16[80,1280]{1,0:T(8,128)(2,1)S(1)} %get-tuple-element.116), channel_id=1, source_target_pairs={{0,4},{1,5},{2,6},{3,7},{4,0},{5,1},{6,2},{7,3},{8,12},{9,13},{10,... | collective-permute-start | bytes 614408 | tf_op jit(solution)/shard_map/weights/ppermute | solution.py:38
  19.4 13.6 %copy-start = (bf16[4,80,1280]{2,1,0:T(8,128)(2,1)}, bf16[4,80,1280]{2,1,0:T(8,128)(2,1)S(1)}, u32[]{:S(2)}) copy-start(bf16[4,80,1280]{2,1,0:T(8,128)(2,1)S(1)} %pad_maximum_fusion.1.b0) | copy-start | bytes 2457604
  19.4 22.4 %collective-permute-start.12 = (bf16[4,80,1280]{2,1,0:T(8,128)(2,1)S(1)}, bf16[4,80,1280]{2,1,0:T(8,128)(2,1)S(1)}, u32[]{:S(2)}, u32[]{:S(2)}) collective-permute-start(bf16[4,80,1280]{2,1,0:T(8,128)(2,1)S(1)} %pad_maximum_fusion.1.b0), channel_id=1, source_target_pairs={{0,2},{1,3},{2,4},{3,5},{4,6},{5,7},{6,0},{7,1},{8,10},{9,11},{10,... | collective-permute-start | bytes 2457608 | tf_op jit(solution)/shard_map/weights/ppermute | solution.py:38
  23.8 18.3 %collective-permute-start.11 = (bf16[4,80,1280]{2,1,0:T(8,128)(2,1)S(1)}, bf16[4,80,1280]{2,1,0:T(8,128)(2,1)S(1)}, u32[]{:S(2)}, u32[]{:S(2)}) collective-permute-start(bf16[4,80,1280]{2,1,0:T(8,128)(2,1)S(1)} %pad_maximum_fusion.1.b0), channel_id=1, source_target_pairs={{0,6},{1,7},{2,0},{3,1},{4,2},{5,3},{6,4},{7,5},{8,14},{9,15},{10,... | collective-permute-start | bytes 2457608 | tf_op jit(solution)/shard_map/weights/ppermute | solution.py:38
  26.2 20.2 %collective-permute-start.5 = (bf16[4,80,1280]{2,1,0:T(8,128)(2,1)S(1)}, bf16[4,80,1280]{2,1,0:T(8,128)(2,1)S(1)}, u32[]{:S(2)}, u32[]{:S(2)}) collective-permute-start(bf16[4,80,1280]{2,1,0:T(8,128)(2,1)S(1)} %pad_maximum_fusion.a0), channel_id=1, source_target_pairs={{0,8},{1,9},{2,10},{3,11},{4,12},{5,13},{6,14},{7,15},{8,16},{9,17... | collective-permute-start | bytes 2457608 | tf_op jit(solution)/shard_map/weights/ppermute | solution.py:38
  27.8 20.1 %collective-permute-start.4 = (bf16[4,80,1280]{2,1,0:T(8,128)(2,1)S(1)}, bf16[4,80,1280]{2,1,0:T(8,128)(2,1)S(1)}, u32[]{:S(2)}, u32[]{:S(2)}) collective-permute-start(bf16[4,80,1280]{2,1,0:T(8,128)(2,1)S(1)} %pad_maximum_fusion.a0), channel_id=1, source_target_pairs={{0,24},{1,25},{2,26},{3,27},{4,28},{5,29},{6,30},{7,31},{8,0},{9,1... | collective-permute-start | bytes 2457608 | tf_op jit(solution)/shard_map/weights/ppermute | solution.py:38
  33.0 15.1 %collective-permute-start.15 = (bf16[256,1408]{1,0:T(8,128)(2,1)}, bf16[256,1408]{1,0:T(8,128)(2,1)S(1)}, u32[]{:S(2)}, u32[]{:S(2)}) collective-permute-start(bf16[256,1408]{1,0:T(8,128)(2,1)} %get-tuple-element.50.own), channel_id=1, source_target_pairs={{0,1},{1,0},{2,3},{3,2},{4,5},{5,4},{6,7},{7,6},{8,9},{9,8},{10,11... | collective-permute-start | bytes 2162696 | tf_op jit(solution)/shard_map/prepare/ppermute | solution.py:42
  41.9 13.1 %collective-permute-start.16 = (bf16[256,1664]{1,0:T(8,128)(2,1)}, bf16[256,1664]{1,0:T(8,128)(2,1)}, u32[]{:S(2)}, u32[]{:S(2)}) collective-permute-start(bf16[256,1664]{1,0:T(8,128)(2,1)} %get-tuple-element.51.extra), channel_id=1, source_target_pairs={{0,1},{1,0},{2,3},{3,2},{4,5},{5,4},{6,7},{7,6},{8,9},{9,8},{10,11... | collective-permute-start | bytes 2555912 | tf_op jit(solution)/shard_map/prepare/ppermute | solution.py:42
  42.1 13.0 %collective-permute-start.13 = (bf16[2,80,1280]{2,1,0:T(8,128)(2,1)S(1)}, bf16[2,80,1280]{2,1,0:T(8,128)(2,1)S(1)}, u32[]{:S(2)}, u32[]{:S(2)}) collective-permute-start(bf16[2,80,1280]{2,1,0:T(8,128)(2,1)S(1)} %slice.199), channel_id=1, source_target_pairs={{0,2},{1,3},{2,4},{3,5},{4,6},{5,7},{6,0},{7,1},{8,10},{9,11},{10,... | collective-permute-start | bytes 1228808 | tf_op jit(solution)/shard_map/weights/ppermute | solution.py:38
  46.3 9.3 %collective-permute-start.14 = (bf16[2,80,1280]{2,1,0:T(8,128)(2,1)S(1)}, bf16[2,80,1280]{2,1,0:T(8,128)(2,1)}, u32[]{:S(2)}, u32[]{:S(2)}) collective-permute-start(bf16[2,80,1280]{2,1,0:T(8,128)(2,1)S(1)} %slice.200), channel_id=1, source_target_pairs={{0,6},{1,7},{2,0},{3,1},{4,2},{5,3},{6,4},{7,5},{8,14},{9,15},{10,... | collective-permute-start | bytes 1228808 | tf_op jit(solution)/shard_map/weights/ppermute | solution.py:38
  48.0 10.3 %collective-permute-start.6 = (bf16[2,80,1280]{2,1,0:T(8,128)(2,1)S(1)}, bf16[2,80,1280]{2,1,0:T(8,128)(2,1)S(1)}, u32[]{:S(2)}, u32[]{:S(2)}) collective-permute-start(bf16[2,80,1280]{2,1,0:T(8,128)(2,1)S(1)} %slice.196), channel_id=1, source_target_pairs={{0,8},{1,9},{2,10},{3,11},{4,12},{5,13},{6,14},{7,15},{8,16},{9,17... | collective-permute-start | bytes 1228808 | tf_op jit(solution)/shard_map/weights/ppermute | solution.py:38
  49.1 10.1 %collective-permute-start.7 = (bf16[2,80,1280]{2,1,0:T(8,128)(2,1)S(1)}, bf16[2,80,1280]{2,1,0:T(8,128)(2,1)S(1)}, u32[]{:S(2)}, u32[]{:S(2)}) collective-permute-start(bf16[2,80,1280]{2,1,0:T(8,128)(2,1)S(1)} %slice.197), channel_id=1, source_target_pairs={{0,24},{1,25},{2,26},{3,27},{4,28},{5,29},{6,30},{7,31},{8,0},{9,1... | collective-permute-start | bytes 1228808 | tf_op jit(solution)/shard_map/weights/ppermute | solution.py:38
  60.0 31.6 %all-to-all-start = ((bf16[128,8,640]{2,1,0:T(8,128)(2,1)}), bf16[128,8,640]{2,1,0:T(8,128)(2,1)S(1)}, u32[]{:S(2)}, u32[]{:S(2)}) async-start(bf16[128,8,640]{2,1,0:T(8,128)(2,1)} %bitcast.15), calls=%async_computation | async-start | bytes 2621440 | tf_op jit(solution)/shard_map/grads_in/all_to_all | solution.py:434
  81.2 2.6 %collective-permute-start.17 = (bf16[512,640]{1,0:T(8,128)(2,1)}, bf16[512,640]{1,0:T(8,128)(2,1)S(1)}, u32[]{:S(2)}, u32[]{:S(2)}) collective-permute-start(bf16[512,640]{1,0:T(8,128)(2,1)} %get-tuple-element.63.attended.attended_hbm), channel_id=1, source_target_pairs={{0,1},{1,0},{2,3},{3,2},{4,5},{5,4},{6,7},{7,6},{8,9},{9,8},{10,11... | collective-permute-start | bytes 1966088 | tf_op jit(solution)/shard_map/forward/ppermute | solution.py:42
  98.4 10.0 %collective-permute-start.18 = (bf16[512,640]{1,0:T(8,128)(2,1)}, bf16[512,640]{1,0:T(8,128)(2,1)S(1)}, u32[]{:S(2)}, u32[]{:S(2)}) collective-permute-start(bf16[512,640]{1,0:T(8,128)(2,1)} %get-tuple-element.72), channel_id=1, source_target_pairs={{0,1},{1,0},{2,3},{3,2},{4,5},{5,4},{6,7},{7,6},{8,9},{9,8},{10,11... | collective-permute-start | bytes 1966088 | tf_op jit(solution)/shard_map/grads_in/ppermute | solution.py:42
  98.6 39.6 %all-to-all-start.1 = ((bf16[128,8,640]{2,1,0:T(8,128)(2,1)}), bf16[128,8,640]{2,1,0:T(8,128)(2,1)S(1)}, u32[]{:S(2)}, u32[]{:S(2)}) async-start(bf16[128,8,640]{2,1,0:T(8,128)(2,1)} %bitcast.17), calls=%async_computation.1 | async-start | bytes 2621440 | tf_op jit(solution)/shard_map/rows_out/all_to_all | solution.py:500
  123.3 21.2 %collective-permute-start.19 = (bf16[4,80,1280]{2,1,0:T(8,128)(2,1)}, bf16[4,80,1280]{2,1,0:T(8,128)(2,1)}, u32[]{:S(2)}, u32[]{:S(2)}) collective-permute-start(bf16[4,80,1280]{2,1,0:T(8,128)(2,1)} %get-tuple-element.78), channel_id=1, source_target_pairs={{0,8},{1,9},{2,10},{3,11},{4,12},{5,13},{6,14},{7,15},{8,16},{9,17... | collective-permute-start | bytes 2457608 | tf_op jit(solution)/shard_map/weight_grads/ppermute | solution.py:38
  124.3 20.3 %collective-permute-start.20 = (bf16[4,80,1280]{2,1,0:T(8,128)(2,1)}, bf16[4,80,1280]{2,1,0:T(8,128)(2,1)}, u32[]{:S(2)}, u32[]{:S(2)}) collective-permute-start(bf16[4,80,1280]{2,1,0:T(8,128)(2,1)} %get-tuple-element.79), channel_id=1, source_target_pairs={{0,24},{1,25},{2,26},{3,27},{4,28},{5,29},{6,30},{7,31},{8,0},{9,1... | collective-permute-start | bytes 2457608 | tf_op jit(solution)/shard_map/weight_grads/ppermute | solution.py:38
  126.6 23.8 %collective-permute-start.26 = (bf16[4,80,1280]{2,1,0:T(8,128)(2,1)}, bf16[4,80,1280]{2,1,0:T(8,128)(2,1)S(1)}, u32[]{:S(2)}, u32[]{:S(2)}) collective-permute-start(bf16[4,80,1280]{2,1,0:T(8,128)(2,1)} %get-tuple-element.88), channel_id=1, source_target_pairs={{0,2},{1,3},{2,4},{3,5},{4,6},{5,7},{6,0},{7,1},{8,10},{9,11},{10,... | collective-permute-start | bytes 2457608 | tf_op jit(solution)/shard_map/weight_grads/ppermute | solution.py:38
  127.7 24.5 %collective-permute-start.28 = (bf16[4,80,1280]{2,1,0:T(8,128)(2,1)}, bf16[4,80,1280]{2,1,0:T(8,128)(2,1)S(1)}, u32[]{:S(2)}, u32[]{:S(2)}) collective-permute-start(bf16[4,80,1280]{2,1,0:T(8,128)(2,1)} %get-tuple-element.89), channel_id=1, source_target_pairs={{0,6},{1,7},{2,0},{3,1},{4,2},{5,3},{6,4},{7,5},{8,14},{9,15},{10,... | collective-permute-start | bytes 2457608 | tf_op jit(solution)/shard_map/weight_grads/ppermute | solution.py:38
  145.9 11.7 %collective-permute-start.21 = (bf16[2,80,1280]{2,1,0:T(8,128)(2,1)S(1)}, bf16[2,80,1280]{2,1,0:T(8,128)(2,1)S(1)}, u32[]{:S(2)}, u32[]{:S(2)}) collective-permute-start(bf16[2,80,1280]{2,1,0:T(8,128)(2,1)S(1)} %add_convert_fusion.5), channel_id=1, source_target_pairs={{0,8},{1,9},{2,10},{3,11},{4,12},{5,13},{6,14},{7,15},{8,16},{9,17... | collective-permute-start | bytes 1228808 | tf_op jit(solution)/shard_map/weight_grads/ppermute | solution.py:38
  148.5 10.2 %collective-permute-start.23 = (bf16[2,80,1280]{2,1,0:T(8,128)(2,1)S(1)}, bf16[2,80,1280]{2,1,0:T(8,128)(2,1)S(1)}, u32[]{:S(2)}, u32[]{:S(2)}) collective-permute-start(bf16[2,80,1280]{2,1,0:T(8,128)(2,1)S(1)} %add_convert_fusion.4), channel_id=1, source_target_pairs={{0,24},{1,25},{2,26},{3,27},{4,28},{5,29},{6,30},{7,31},{8,0},{9,1... | collective-permute-start | bytes 1228808 | tf_op jit(solution)/shard_map/weight_grads/ppermute | solution.py:38
  150.5 14.7 %collective-permute-start.27 = (bf16[2,80,1280]{2,1,0:T(8,128)(2,1)S(1)}, bf16[2,80,1280]{2,1,0:T(8,128)(2,1)S(1)}, u32[]{:S(2)}, u32[]{:S(2)}) collective-permute-start(bf16[2,80,1280]{2,1,0:T(8,128)(2,1)S(1)} %add_convert_fusion.2), channel_id=1, source_target_pairs={{0,2},{1,3},{2,4},{3,5},{4,6},{5,7},{6,0},{7,1},{8,10},{9,11},{10,... | collective-permute-start | bytes 1228808 | tf_op jit(solution)/shard_map/weight_grads/ppermute | solution.py:38
  152.3 12.9 %collective-permute-start.30 = (bf16[2,80,1280]{2,1,0:T(8,128)(2,1)S(1)}, bf16[2,80,1280]{2,1,0:T(8,128)(2,1)S(1)}, u32[]{:S(2)}, u32[]{:S(2)}) collective-permute-start(bf16[2,80,1280]{2,1,0:T(8,128)(2,1)S(1)} %add_convert_fusion.1), channel_id=1, source_target_pairs={{0,6},{1,7},{2,0},{3,1},{4,2},{5,3},{6,4},{7,5},{8,14},{9,15},{10,... | collective-permute-start | bytes 1228808 | tf_op jit(solution)/shard_map/weight_grads/ppermute | solution.py:38
  160.2 10.7 %collective-permute-start.24 = (bf16[80,1280]{1,0:T(8,128)(2,1)S(1)}, bf16[80,1280]{1,0:T(8,128)(2,1)S(1)}, u32[]{:S(2)}, u32[]{:S(2)}) collective-permute-start(bf16[80,1280]{1,0:T(8,128)(2,1)S(1)} %get-tuple-element.109), channel_id=1, source_target_pairs={{0,6},{1,7},{2,0},{3,1},{4,2},{5,3},{6,4},{7,5},{8,14},{9,15},{10,... | collective-permute-start | bytes 614408 | tf_op jit(solution)/shard_map/weight_grads/ppermute | solution.py:38
  163.6 8.4 %collective-permute-start.25 = (bf16[80,1280]{1,0:T(8,128)(2,1)S(1)}, bf16[80,1280]{1,0:T(8,128)(2,1)S(1)}, u32[]{:S(2)}, u32[]{:S(2)}) collective-permute-start(bf16[80,1280]{1,0:T(8,128)(2,1)S(1)} %get-tuple-element.110), channel_id=1, source_target_pairs={{0,4},{1,5},{2,6},{3,7},{4,0},{5,1},{6,2},{7,3},{8,12},{9,13},{10,... | collective-permute-start | bytes 614408 | tf_op jit(solution)/shard_map/weight_grads/ppermute | solution.py:38
  163.9 10.0 %collective-permute-start.22 = (bf16[80,1280]{1,0:T(8,128)(2,1)S(1)}, bf16[80,1280]{1,0:T(8,128)(2,1)S(1)}, u32[]{:S(2)}, u32[]{:S(2)}) collective-permute-start(bf16[80,1280]{1,0:T(8,128)(2,1)S(1)} %fusion.9), channel_id=1, source_target_pairs={{0,2},{1,3},{2,4},{3,5},{4,6},{5,7},{6,0},{7,1},{8,10},{9,11},{10,... | collective-permute-start | bytes 614408 | tf_op jit(solution)/shard_map/weight_grads/ppermute | solution.py:38
  165.5 9.5 %collective-permute-start.31 = (bf16[80,1280]{1,0:T(8,128)(2,1)S(1)}, bf16[80,1280]{1,0:T(8,128)(2,1)S(1)}, u32[]{:S(2)}, u32[]{:S(2)}) collective-permute-start(bf16[80,1280]{1,0:T(8,128)(2,1)S(1)} %get-tuple-element.111), channel_id=1, source_target_pairs={{0,24},{1,25},{2,26},{3,27},{4,28},{5,29},{6,30},{7,31},{8,0},{9,1... | collective-permute-start | bytes 614408 | tf_op jit(solution)/shard_map/weight_grads/ppermute | solution.py:38
  168.9 7.8 %collective-permute-start.32 = (bf16[80,1280]{1,0:T(8,128)(2,1)S(1)}, bf16[80,1280]{1,0:T(8,128)(2,1)S(1)}, u32[]{:S(2)}, u32[]{:S(2)}) collective-permute-start(bf16[80,1280]{1,0:T(8,128)(2,1)S(1)} %get-tuple-element.112), channel_id=1, source_target_pairs={{0,16},{1,17},{2,18},{3,19},{4,20},{5,21},{6,22},{7,23},{8,24},{9,... | collective-permute-start | bytes 614408 | tf_op jit(solution)/shard_map/weight_grads/ppermute | solution.py:38
  170.9 7.9 %collective-permute-start.29 = (bf16[80,1280]{1,0:T(8,128)(2,1)S(1)}, bf16[80,1280]{1,0:T(8,128)(2,1)S(1)}, u32[]{:S(2)}, u32[]{:S(2)}) collective-permute-start(bf16[80,1280]{1,0:T(8,128)(2,1)S(1)} %fusion.10), channel_id=1, source_target_pairs={{0,8},{1,9},{2,10},{3,11},{4,12},{5,13},{6,14},{7,15},{8,16},{9,17... | collective-permute-start | bytes 614408 | tf_op jit(solution)/shard_map/weight_grads/ppermute | solution.py:38
  178.9 1.5 collective-permute-start.33
  179.1 15.2 %collective-permute-start.34 = (bf16[256,1280]{1,0:T(8,128)(2,1)}, bf16[256,1280]{1,0:T(8,128)(2,1)}, u32[]{:S(2)}, u32[]{:S(2)}) collective-permute-start(bf16[256,1280]{1,0:T(8,128)(2,1)} %get-tuple-element.94), channel_id=1, source_target_pairs={{0,1},{1,0},{2,3},{3,2},{4,5},{5,4},{6,7},{7,6},{8,9},{9,8},{10,11... | collective-permute-start | bytes 1966088 | tf_op jit(solution)/shard_map/norm_grad/ppermute | solution.py:42
  180.8 6.2 %collective-permute-start.36 = (bf16[40,1280]{1,0:T(8,128)(2,1)S(1)}, bf16[40,1280]{1,0:T(8,128)(2,1)S(1)}, u32[]{:S(2)}, u32[]{:S(2)}) collective-permute-start(bf16[40,1280]{1,0:T(8,128)(2,1)S(1)} %get-tuple-element.106), channel_id=1, source_target_pairs={{0,32},{32,64},{64,96},{96,0},{1,33},{33,65},{65,97},{97,1},{2,34}... | collective-permute-start | bytes 307208 | tf_op jit(solution)/shard_map/over_groups/ppermute | solution.py:37
  182.4 6.2 %collective-permute-start.37 = (bf16[40,1280]{1,0:T(8,128)(2,1)S(1)}, bf16[40,1280]{1,0:T(8,128)(2,1)S(1)}, u32[]{:S(2)}, u32[]{:S(2)}) collective-permute-start(bf16[40,1280]{1,0:T(8,128)(2,1)S(1)} %get-tuple-element.108), channel_id=1, source_target_pairs={{0,96},{32,0},{64,32},{96,64},{1,97},{33,1},{65,33},{97,65},{2,98}... | collective-permute-start | bytes 307208 | tf_op jit(solution)/shard_map/over_groups/ppermute | solution.py:37
  184.1 6.2 %collective-permute-start.38 = (bf16[40,1280]{1,0:T(8,128)(2,1)S(1)}, bf16[40,1280]{1,0:T(8,128)(2,1)S(1)}, u32[]{:S(2)}, u32[]{:S(2)}) collective-permute-start(bf16[40,1280]{1,0:T(8,128)(2,1)S(1)} %get-tuple-element.107), channel_id=1, source_target_pairs={{0,64},{32,96},{64,0},{96,32},{1,65},{33,97},{65,1},{97,33},{2,66}... | collective-permute-start | bytes 307208 | tf_op jit(solution)/shard_map/over_groups/ppermute | solution.py:37
  186.0 8.3 %collective-permute-start.35 = (bf16[256,640]{1,0:T(8,128)(2,1)S(1)}, bf16[256,640]{1,0:T(8,128)(2,1)S(1)}, u32[]{:S(2)}, u32[]{:S(2)}) collective-permute-start(bf16[256,640]{1,0:T(8,128)(2,1)S(1)} %slice.194), channel_id=1, source_target_pairs={{0,1},{1,0},{2,3},{3,2},{4,5},{5,4},{6,7},{7,6},{8,9},{9,8},{10,11... | collective-permute-start | bytes 983048 | tf_op jit(solution)/shard_map/norm_grad/ppermute | solution.py:42
  190.3 8.6 %collective-permute-start.39 = (bf16[40,1280]{1,0:T(8,128)(2,1)S(1)}, bf16[40,1280]{1,0:T(8,128)(2,1)S(1)}, u32[]{:S(2)}, u32[]{:S(2)}) collective-permute-start(bf16[40,1280]{1,0:T(8,128)(2,1)S(1)} %fusion.13), channel_id=1, source_target_pairs={{0,96},{32,0},{64,32},{96,64},{1,97},{33,1},{65,33},{97,65},{2,98}... | collective-permute-start | bytes 307208 | tf_op jit(solution)/shard_map/over_groups/ppermute | solution.py:37
  192.3 7.0 %collective-permute-start.40 = (bf16[40,1280]{1,0:T(8,128)(2,1)S(1)}, bf16[40,1280]{1,0:T(8,128)(2,1)S(1)}, u32[]{:S(2)}, u32[]{:S(2)}) collective-permute-start(bf16[40,1280]{1,0:T(8,128)(2,1)S(1)} %fusion.13), channel_id=1, source_target_pairs={{0,32},{32,64},{64,96},{96,0},{1,33},{33,65},{65,97},{97,1},{2,34}... | collective-permute-start | bytes 307208 | tf_op jit(solution)/shard_map/over_groups/ppermute | solution.py:37
  192.4 6.8 %collective-permute-start.41 = (bf16[40,1280]{1,0:T(8,128)(2,1)S(1)}, bf16[40,1280]{1,0:T(8,128)(2,1)S(1)}, u32[]{:S(2)}, u32[]{:S(2)}) collective-permute-start(bf16[40,1280]{1,0:T(8,128)(2,1)S(1)} %fusion.13), channel_id=1, source_target_pairs={{0,64},{32,96},{64,0},{96,32},{1,65},{33,97},{65,1},{97,33},{2,66}... | collective-permute-start | bytes 307208 | tf_op jit(solution)/shard_map/over_groups/ppermute | solution.py:37
  (19 other events, 101.8 us)
